TPU v7x, 512 devices: a whole 4x4x16 slice. The times are simulated.
512 devices in a mesh: role: 2 (over core), grp: 64 (over x, z), tp: 4 (over y).
Axes of the slice: x: 4, y: 4, z: 16, core: 2. Of those that a mesh axis runs over, the one named last changes fastest.
Arguments:
- queries: bfloat16 [512, 64, 576], P(('role', 'grp', 'tp')), may hold values from -50 to 50
- latent_cache: bfloat16 [512, 384, 576], P(('role', 'grp', 'tp')), may hold values from -6 to 6
- lengths: int32 [512], P(('role', 'grp', 'tp')), may hold values from 2 to 384, as said below
- value_up: bfloat16 [64, 512, 128], P(('role', 'tp')), may hold values from -0.25 to 0.25
- output_weight: bfloat16 [3584, 8192], P('grp', ('role', 'tp')), may hold values from -0.0625 to 0.0625
- residual: bfloat16 [3584, 512], P('grp'), may hold values from -15 to 15
- norm_gain: float32 [3584], replicated, may hold values from 0.5 to 1.5
- routed_experts: int32 [512, 8], replicated, may hold values from 0 to 63, as said below
- route_weights: float32 [512, 8], replicated, may hold values from 0.1 to 0.6
- gate_weight: bfloat16 [64, 3584, 1024], P('grp', None, ('role', 'tp')), may hold values from -0.09375 to 0.09375
- up_weight: bfloat16 [64, 3584, 1024], P('grp', None, ('role', 'tp')), may hold values from -0.09375 to 0.09375
- down_weight: bfloat16 [64, 1024, 3584], P('grp', ('role', 'tp')), may hold values from -0.1875 to 0.1875
Outputs:
- layer_output: bfloat16 [3584, 512], P('grp', ('role', 'tp'))
Inputs may be any that keep to these rules, and one draw needn't show every extreme that they name: `routed_experts`: each row names 8 different experts. In each aligned block of 64 rows no expert is named by more than 16 rows, and one expert, the same in every block, is named by exactly 16 rows of each block. `lengths`: at least one request has length 384.
All inputs are finite; a program needn't handle non-finite values.
Results may differ from a plain program's by a relative error of at most 0.028.
Values may be sent and summed in bfloat16 or wider, within the bound.
No kernel may reach another device: no remote copies, remote signals or barrier semaphores. Data moves between devices by JAX's collectives and lax.ppermute only.
A program may use at most 64 MiB of HBM per device.

v0:
```python
import jax
import jax.numpy as jnp
from jax import lax
from jax.sharding import PartitionSpec as P

LAT = 512


SOFTMAX_SCALE = 192.0 ** (-0.5)
NORM_EPS = 1e-06


def slot_tables(routed, experts, block_total, capacity):
    tokens, top_count = routed.shape
    row_count = tokens // block_total
    matches = routed[:, :, None] == jnp.arange(experts, dtype=jnp.int32)[None, None, :]
    named_count = jnp.sum(matches.astype(jnp.int32), axis=1).reshape(
        block_total, row_count, experts
    )
    slot_rank = jnp.cumsum(named_count, axis=1) - named_count
    token_rank = jnp.take_along_axis(slot_rank.reshape(tokens, experts), routed, axis=1)
    token_ids = jnp.arange(tokens, dtype=jnp.int32)
    block_ids = jnp.broadcast_to((token_ids // row_count)[:, None], (tokens, top_count))
    row_ids = jnp.broadcast_to((token_ids % row_count)[:, None], (tokens, top_count))
    source_table = jnp.full((block_total, experts, capacity), -1, jnp.int32)
    source_table = source_table.at[block_ids, routed, token_rank].set(row_ids, mode="drop")
    return (source_table, slot_rank)


def shards(
    queries,
    latent_cache,
    lengths,
    value_up,
    output_weight,
    residual,
    norm_gain,
    routed_experts,
    route_weights,
    gate_weight,
    up_weight,
    down_weight,
):
    members = lax.axis_size(("role", "tp"))
    member_index = lax.axis_index(("role", "tp"))
    owners = lax.axis_size("grp")
    roles = lax.axis_size("role")
    lanes = lax.axis_size("tp")
    per_device = queries.shape[0]
    window = latent_cache.shape[1]
    scores = (
        jnp.einsum("bhc,bjc->bhj", queries, latent_cache, preferred_element_type=jnp.float32)
        * SOFTMAX_SCALE
    )
    visible = (jnp.arange(window, dtype=jnp.int32)[None, :] < lengths[:, None])[:, None, :]
    row_max = jnp.max(jnp.where(visible, scores, -1e30), axis=2, keepdims=True)
    weights = jnp.where(visible, jnp.exp(scores - row_max), 0.0)
    row_total = jnp.sum(weights, axis=2, keepdims=True)
    summed = jnp.einsum(
        "bhj,bjc->bhc",
        weights.astype(jnp.bfloat16),
        latent_cache[:, :, :LAT],
        preferred_element_type=jnp.float32,
    )
    attended = (summed / row_total).astype(jnp.bfloat16)
    regrouped = lax.all_to_all(attended, ("role", "tp"), split_axis=1, concat_axis=0, tiled=True)
    head_values = jnp.einsum(
        "bhc,hcv->bhv", regrouped, value_up, preferred_element_type=jnp.float32
    )
    head_values = head_values.astype(jnp.bfloat16).reshape(regrouped.shape[0], -1)
    gathered_order = jnp.einsum(
        "dv,tv->dt",
        output_weight,
        lax.all_gather(head_values, "grp", axis=0, tiled=True),
        preferred_element_type=jnp.float32,
    )
    columns, tokens = residual.shape
    attention_part = gathered_order.reshape(columns, owners, roles, lanes, per_device)
    attention_part = attention_part.transpose(0, 2, 1, 3, 4).reshape(columns, tokens)
    row_count = tokens // members
    experts = gate_weight.shape[0] * owners
    top_count = routed_experts.shape[1]
    capacity = row_count * top_count // experts * min(2, experts // top_count)
    full_width = columns * owners
    source_table, slot_rank = slot_tables(routed_experts, experts, members, capacity)
    attention_cols = lax.psum(attention_part.astype(jnp.bfloat16), ("role", "tp")).astype(
        jnp.float32
    )
    hidden_all = (residual.astype(jnp.float32) + attention_cols).astype(jnp.bfloat16)
    present = source_table >= 0
    block_base = (jnp.arange(members, dtype=jnp.int32) * row_count)[:, None, None]
    whole_index = jnp.where(present, source_table + block_base, 0).transpose(1, 0, 2)
    picked_cols = hidden_all[:, whole_index]
    picked_cols = jnp.where(
        present.transpose(1, 0, 2)[None], picked_cols, jnp.zeros((), jnp.bfloat16)
    )
    outbound = picked_cols.transpose(1, 0, 2, 3).reshape(experts, columns, members * capacity)
    arrived = lax.all_to_all(outbound, "grp", split_axis=0, concat_axis=1, tiled=True)
    hidden_rows = lax.dynamic_slice_in_dim(hidden_all, member_index * row_count, row_count, 1)
    values = arrived.astype(jnp.float32)
    inv_rms = lax.rsqrt(jnp.sum(values * values, axis=1) / full_width + NORM_EPS)
    normed = (values * inv_rms[:, None, :] * norm_gain[None, :, None]).astype(jnp.bfloat16)
    gate_part = jnp.einsum("edc,edh->ech", normed, gate_weight, preferred_element_type=jnp.float32)
    up_part = jnp.einsum("edc,edh->ech", normed, up_weight, preferred_element_type=jnp.float32)
    activated = (jax.nn.silu(gate_part) * up_part).astype(jnp.bfloat16)
    partial_sum = jnp.einsum(
        "ech,ehd->ced", activated, down_weight, preferred_element_type=jnp.float32
    )
    expert_rows = lax.psum_scatter(
        partial_sum.astype(jnp.bfloat16).astype(jnp.float32).astype(jnp.bfloat16),
        ("role", "tp"),
        scatter_dimension=0,
        tiled=True,
    )
    returned = lax.all_to_all(expert_rows, "grp", split_axis=2, concat_axis=1, tiled=True)
    rank_rows = lax.dynamic_index_in_dim(slot_rank, member_index, 0, keepdims=False)
    routed_rows = lax.dynamic_slice_in_dim(routed_experts, member_index * row_count, row_count, 0)
    weight_rows = lax.dynamic_slice_in_dim(route_weights, member_index * row_count, row_count, 0)
    token_rank = jnp.take_along_axis(rank_rows, routed_rows, axis=1)
    picked = returned[token_rank, routed_rows].astype(jnp.float32)
    mixture = jnp.sum(weight_rows[:, :, None] * picked, axis=1)
    return (hidden_rows.astype(jnp.float32) + mixture.T).astype(jnp.bfloat16)


def solution(mesh):
    return jax.shard_map(
        shards,
        mesh=mesh,
        in_specs=(
            P(("role", "grp", "tp"), None, None),
            P(("role", "grp", "tp"), None, None),
            P(("role", "grp", "tp")),
            P(("role", "tp"), None, None),
            P("grp", ("role", "tp")),
            P("grp", None),
            P(),
            P(),
            P(),
            P("grp", None, ("role", "tp")),
            P("grp", None, ("role", "tp")),
            P("grp", ("role", "tp"), None),
        ),
        out_specs=P("grp", ("role", "tp")),
        check_vma=False,
    )
```

profile of v0, /device:TPU:1, one launch (start us, length us, event | category | flops | bytes accessed | tf_op | source)
XLA Modules:
  0.0 395.9 jit_solution(8876420379105710953)
XLA Ops:
  7.3 1.4 select_reduce_fusion
  8.7 0.2 fusion.17
  8.9 1.3 fusion.2
  10.1 0.1 copy.211
  10.2 0.5 broadcast.363
  10.8 1.0 reduce.11
  11.8 0.7 reshape.408
  12.4 10.1 %all-to-all-start = ((bf16[8,2,2048]{2,1,0:T(2,128)(2,1)}), bf16[8,2,2048]{2,1,0:T(2,128)(2,1)S(1)}, u32[]{:S(2)}, u32[]{:S(2)}) async-start(bf16[8,2,2048]{2,1,0:T(2,128)(2,1)} %reshape.408), calls=%async_computation | async-start | bytes 131072 | tf_op jit(solution)/shard_map/all_to_all | solution.py:66
  22.6 0.1 convert_reduce_fusion
  22.7 0.1 copy.185
  22.8 0.1 copy.193
  23.0 0.2 reshape.371
  23.1 0.1 broadcast_in_dim.90
  23.3 0.2 reshape.385
  23.4 0.1 reshape.346
  23.5 0.2 copy.191
  23.7 3.8 all-to-all-done
  27.6 0.9 fusion.5
  28.6 6.3 %fusion.54 = s32[8,64,64]{2,0,1:T(8,128)S(1)} fusion(s32[8,64,64]{2,0,1:T(8,128)S(1)} %copy.191), kind=kOutput, calls=%fused_computation.97 | output fusion | flops 2064384 | bytes 262144 | tf_op jit(solution)/shard_map/jit(cumsum)/reduce_window_sum | solution.py:20
  34.9 0.2 copy.192
  35.1 0.1 reduce_window_sum.14
  35.3 33.0 %gather_fusion.2 = s32[4096]{0:T(1024)S(1)} fusion(s32[512,64]{0,1:T(8,128)S(1)} %sub.24, s32[4096]{0:T(1024)S(1)} %reshape.371), kind=kCustom, calls=%fused_computation.2 | custom fusion | bytes 65536 | tf_op jit(solution)/shard_map/jit(take_along_axis)/gather | solution.py:21
  68.3 0.2 reshape.374
  68.5 0.1 copy.194
  68.6 0.1 multiply_reduce_fusion.1
  68.7 0.1 and_reduce_fusion
  68.8 0.1 copy.195
  68.9 0.2 reshape.383
  69.1 15.5 %scatter_custom_fusion = s32[8192]{0:T(1024)S(1)} fusion(s32[4096]{0:T(1024)S(1)} %reshape.383, s32[4096]{0:T(1024)S(1)} %reshape.385, s32[]{:T(128)} %constant.99.clone.1), kind=kCustom, calls=%fused_computation.69 | custom fusion | bytes 32772
  84.7 0.1 compare_select_fusion
  84.8 0.1 copy.196
  85.0 0.1 reshape.359
  85.1 71.2 %all-gather.2.cloned.1.call-done = bf16[512,1024]{1,0:T(8,128)(2,1)} async-done(((bf16[8,1024]{1,0:T(8,128)(2,1)}), bf16[512,1024]{1,0:T(8,128)(2,1)}) %all-gather.2.cloned.1.call-update) | async-done | bytes 1048592 | tf_op jit(solution)/shard_map/all_gather | solution.py:74
  156.4 1.7 fusion.3
  158.0 0.1 copy.188
  158.2 37.3 %psum.7 = bf16[56,512]{0,1:T(8,128)(2,1)S(1)} all-reduce(bf16[56,512]{0,1:T(8,128)(2,1)S(1)} %bitcast.108), channel_id=1, replica_groups=mesh['role'=2,'grp'=64,'tp'=4] {'role','tp'}, use_global_device_ids=true, to_apply=%region_2.3 | all-reduce | flops 28672 | bytes 114688 | tf_op jit(solution)/shard_map/psum | solution.py:86
  195.5 24.0 %gather_fusion = bf16[8192,56]{1,0:T(8,128)(2,1)S(1)} fusion(bf16[56,512]{0,1:T(8,128)(2,1)S(1)} %add_convert_fusion, s32[8192]{0:T(1024)S(1)} %broadcast_clamp_fusion), kind=kCustom, calls=%fused_computation | custom fusion | bytes 1867776 | tf_op jit(solution)/shard_map/gather | solution.py:93
  219.6 4.3 %copy.197 = bf16[64,8,16,56]{0,2,1,3:T(8,128)(2,1)} copy(bf16[64,8,16,56]{3,2,1,0:T(8,128)(2,1)S(1)} %bitcast.99) | data formatting | bytes 1835008 | tf_op jit(solution)/shard_map/gather | solution.py:93
  223.9 1.6 broadcast_select_fusion
  225.5 2.7 copy.198
  228.2 55.8 %all_to_all.33 = bf16[64,56,128]{2,1,0:T(8,128)(2,1)S(1)} all-to-all(bf16[64,56,128]{2,1,0:T(8,128)(2,1)} %copy.198), channel_id=1, replica_groups=mesh['role'=2,'grp'=64,'tp'=4] {'grp'}, dimensions={0} | all-to-all | bytes 1835008 | tf_op jit(solution)/shard_map/all_to_all | solution.py:98
  284.0 0.5 multiply_reduce_fusion
  284.5 1.0 fusion.10
  285.5 3.5 fusion
  289.1 0.1 copy.205
  289.2 34.4 %reduce-scatter.2.cloned.1.call-done = bf16[16,1,3584]{2,0,1:T(8,128)(2,1)} async-done(((bf16[128,1,3584]{2,0,1:T(8,128)(2,1)}), bf16[16,1,3584]{2,0,1:T(8,128)(2,1)}) %reduce-scatter.2.cloned.1.call-update) | async-done | bytes 114704 | tf_op jit(solution)/shard_map/reduce_scatter | solution.py:109
  323.6 3.7 copy.199
  327.3 20.6 %reduce.12 = bf16[3584,16]{1,0:T(8,128)(2,1)} reduce(bf16[3584,1,16]{2,1,0:T(2,128)(2,1)S(1)} %bitcast.103, bf16[]{:T(256)} %broadcast.363), dimensions={1}, to_apply=%bitcast.83.reduce_sub_computation | reduce | bytes 229378
  348.0 2.8 reshape.410
  350.8 15.6 %all-to-all-start.2 = ((bf16[64,2,448]{2,1,0:T(2,128)(2,1)}), bf16[64,2,448]{2,1,0:T(2,128)(2,1)S(1)}, u32[]{:S(2)}, u32[]{:S(2)}) async-start(bf16[64,2,448]{2,1,0:T(2,128)(2,1)} %reshape.410), calls=%async_computation.3 | async-start | bytes 262144 | tf_op jit(solution)/shard_map/all_to_all | solution.py:115
  366.3 0.8 constant_dynamic-slice_fusion.1
  367.1 0.1 copy.190
  367.2 0.1 reshape.377
  367.3 1.1 dynamic-slice_subtract_fusion
  368.4 3.8 gather_fusion.3
  372.1 0.1 reshape.380
  372.3 0.1 reshape.365
  372.3 9.4 %all-to-all-done.2 = bf16[64,2,448]{2,1,0:T(2,128)(2,1)S(1)} async-done(((bf16[64,2,448]{2,1,0:T(2,128)(2,1)}), bf16[64,2,448]{2,1,0:T(2,128)(2,1)S(1)}, u32[]{:S(2)}, u32[]{:S(2)}) %all-to-all-start.2) | async-done | bytes 114720 | tf_op jit(solution)/shard_map/all_to_all | solution.py:115
  381.7 1.0 reshape.411
  382.7 1.8 copy.200
  384.5 0.5 all_to_all.14
  385.0 3.2 gather_fusion.1
  388.2 0.2 fusion.15
  388.3 0.7 copy.203
  (48 shorter events, 0.6 us)
Async XLA Ops:
  6.5 21.1 %copy-start = (bf16[8,512,128]{2,1,0:T(8,128)(2,1)S(1)}, bf16[8,512,128]{2,1,0:T(8,128)(2,1)}, u32[]{:S(2)}) copy-start(bf16[8,512,128]{2,1,0:T(8,128)(2,1)} %param.15) | copy-start | bytes 3145732
  6.5 16.0 %copy-start.4 = (s32[512,8]{0,1:T(8,128)S(1)}, s32[512,8]{0,1:T(8,128)}, u32[]{:S(2)}) copy-start(s32[512,8]{0,1:T(8,128)} %param.19) | copy-start | bytes 49156
  6.5 16.2 %copy-start.6 = (bf16[56,512]{1,0:T(8,128)(2,1)S(1)}, bf16[56,512]{1,0:T(8,128)(2,1)}, u32[]{:S(2)}) copy-start(bf16[56,512]{1,0:T(8,128)(2,1)} %param.17) | copy-start | bytes 172036
  12.4 15.1 %all-to-all-start = ((bf16[8,2,2048]{2,1,0:T(2,128)(2,1)}), bf16[8,2,2048]{2,1,0:T(2,128)(2,1)S(1)}, u32[]{:S(2)}, u32[]{:S(2)}) async-start(bf16[8,2,2048]{2,1,0:T(2,128)(2,1)} %reshape.408), calls=%async_computation | async-start | bytes 131072 | tf_op jit(solution)/shard_map/all_to_all | solution.py:66
  22.6 133.8 %all-gather.2.cloned.1.call-start = ((), (), s32[]{:S(2)}) async-start(), calls=%async_computation.4 | async-start | bytes 1064960 | tf_op jit(solution)/shard_map/all_gather | solution.py:74
  23.7 11.4 %copy-start.1 = (s32[8,64,64]{2,0,1:T(8,128)}, s32[8,64,64]{2,0,1:T(8,128)S(1)}, u32[]{:S(2)}) copy-start(s32[8,64,64]{2,0,1:T(8,128)S(1)} %copy.191) | copy-start | bytes 393220
  28.5 295.1 %reduce-scatter.2.cloned.1.call-start = ((), (), s32[]{:S(2)}) async-start(), calls=%async_computation.5 | async-start | bytes 1032192 | tf_op jit(solution)/shard_map/reduce_scatter | solution.py:109
  34.9 33.4 %copy-start.2 = (s32[8,64,64]{2,0,1:T(8,128)}, s32[8,64,64]{2,0,1:T(8,128)S(1)}, u32[]{:S(2)}) copy-start(s32[8,64,64]{2,0,1:T(8,128)S(1)} %fusion.54) | copy-start | bytes 393220
  35.2 33.4 %copy-start.9 = (s32[3]{0:T(128)S(1)}, s32[3]{0:T(128)}, u32[]{:S(2)}) copy-start(s32[3]{0:T(128)} %constant.118) | copy-start | bytes 40
  35.2 33.5 %copy-start.8 = (s32[3]{0:T(128)S(1)}, s32[3]{0:T(128)}, u32[]{:S(2)}) copy-start(s32[3]{0:T(128)} %constant.121) | copy-start | bytes 40
  68.3 88.1 %copy-start.5 = (bf16[56,1024]{1,0:T(8,128)(2,1)S(1)}, bf16[56,1024]{1,0:T(8,128)(2,1)}, u32[]{:S(2)}) copy-start(bf16[56,1024]{1,0:T(8,128)(2,1)} %param.16) | copy-start | bytes 344068
  228.2 56.3 %copy-start.7 = (f32[3584]{0:T(1024)S(1)}, f32[3584]{0:T(1024)}, u32[]{:S(2)}) copy-start(f32[3584]{0:T(1024)} %param.18) | copy-start | bytes 43012
  228.2 56.3 %copy-start.10 = (bf16[1,3584,128]{2,1,0:T(8,128)(2,1)S(1)}, bf16[1,3584,128]{2,1,0:T(8,128)(2,1)}, u32[]{:S(2)}) copy-start(bf16[1,3584,128]{2,1,0:T(8,128)(2,1)} %param.21) | copy-start | bytes 2752516
  284.0 1.5 copy-start.3
  350.8 30.9 %all-to-all-start.2 = ((bf16[64,2,448]{2,1,0:T(2,128)(2,1)}), bf16[64,2,448]{2,1,0:T(2,128)(2,1)S(1)}, u32[]{:S(2)}, u32[]{:S(2)}) async-start(bf16[64,2,448]{2,1,0:T(2,128)(2,1)} %reshape.410), calls=%async_computation.3 | async-start | bytes 262144 | tf_op jit(solution)/shard_map/all_to_all | solution.py:115
Sparse Core Ops, SparseCore 0:
  28.6 127.6 all-gather.1
  289.2 34.4 reduce-scatter.1
where the time goes:
time: 397 us; the launch traced here: 396 us
  waiting for transfers between devices  119 us (30%)
  local copies, waits for them, and re-layouts  102 us (26%)
  blocking collectives  93.1 us (23%)
  other arithmetic  32 us (8%)
  starting transfers between devices  25.7 us (6%)
  between operations  14.6 us (4%)
  matrix products  9.62 us (2%)
    all_gather x1, waiting for transfers between devices, shards(): lax.all_gather(head_values, 'grp', axis=0, tiled=True)  71.2 us
    all_to_all x1, blocking collectives, shards(): lax.all_to_all(outbound, 'grp', split_axis=0, concat_axis=1, tiled=True)  55.8 us
    psum x1, blocking collectives, shards(): lax.psum(attention_part.astype(jnp.bfloat16), ('role', 'tp'))  37.3 us
    reduce_scatter x1, waiting for transfers between devices, shards(): lax.psum_scatter(partial_sum.astype(jnp.bfloat16).astype(jnp.float32).ast...  34.4 us
    gather x5, local copies, waits for them, and re-layouts, slot_tables(): jnp.take_along_axis(slot_rank.reshape(tokens, experts), routed, axis=1)  33.6 us
    gather x2, local copies, waits for them, and re-layouts, shards(): picked_cols = hidden_all[:, whole_index]  28.3 us
    unnamed x5, other arithmetic  21.8 us
    unnamed x33, local copies, waits for them, and re-layouts  21.1 us
  transfers between devices with their start and end apart: 4, of which 4 were waited for; matrix products, arithmetic and copies ran while one was open for 16% of the time, Pallas kernels for 0%

commit v1 on v0

v1 whole, which is shorter than its diff:
```python
import jax
import jax.numpy as jnp
from jax import lax
from jax.experimental import pallas as pl
from jax.experimental.pallas import tpu as pltpu
from jax.sharding import Mesh
from jax.sharding import PartitionSpec as P

LAT = 512
SOFTMAX_SCALE = 192.0 ** (-0.5)
NORM_EPS = 1e-06

ROLE, X, ZH, ZL, TP = 2, 4, 4, 4, 4
Z = ZH * ZL
MEMBERS = ROLE * TP
ROWBLK = 64
MOST = 16
EXPERTS = 64
COLS = 56
WIDTH = 3584
PART = ZH * COLS
PLANE = Z * COLS
HALF = 64

F32 = jnp.float32
BF16 = jnp.bfloat16
VMEM_LIMIT = 48 * 1024 * 1024


def nt_dot(a, b):
    return lax.dot_general(a, b, (((1,), (1,)), ((), ())), preferred_element_type=F32)


def nn_dot(a, b):
    return lax.dot_general(a, b, (((1,), (0,)), ((), ())), preferred_element_type=F32)


def local_call(body, out_shape, *args, scratch=(), smem=()):
    specs = [
        pl.BlockSpec(memory_space=pltpu.SMEM if i in smem else pltpu.VMEM)
        for i in range(len(args))
    ]
    return pl.pallas_call(
        body,
        out_shape=out_shape,
        in_specs=specs,
        out_specs=jax.tree.map(lambda _: pl.BlockSpec(memory_space=pltpu.VMEM), out_shape),
        scratch_shapes=list(scratch),
        compiler_params=pltpu.CompilerParams(vmem_limit_bytes=VMEM_LIMIT),
    )(*args)


def shape(dims, dtype=BF16):
    return jax.ShapeDtypeStruct(dims, dtype)


def attend_kernel(length_ref, query_ref, cache_ref, out_ref):
    cache = cache_ref[0]
    scores = nt_dot(query_ref[0], cache) * SOFTMAX_SCALE
    visible = lax.broadcasted_iota(jnp.int32, scores.shape, 1) < length_ref[0]
    scores = jnp.where(visible, scores, -1e30)
    row_max = jnp.max(scores, axis=1, keepdims=True)
    weights = jnp.where(visible, jnp.exp(scores - row_max), 0.0)
    row_total = jnp.sum(weights, axis=1, keepdims=True)
    summed = nn_dot(weights.astype(BF16), cache[:, :LAT])
    out_ref[...] = (summed / row_total).astype(BF16)


def value_kernel(att_ref, value_ref, out_ref):
    heads = value_ref.shape[0]
    att = att_ref[...]
    rows = att.shape[0]
    row_head = lax.broadcasted_iota(jnp.int32, (rows, 128), 0) % heads
    for head in range(heads):
        product = nn_dot(att, value_ref[head])
        kept = jnp.where(row_head == head, product, 0.0)
        value = jnp.sum(kept.reshape(rows // heads, heads, 128), axis=1).astype(BF16)
        out_ref[:, :, head * 128 : (head + 1) * 128] = jnp.broadcast_to(
            value[None], (out_ref.shape[0],) + value.shape
        )


def project_kernel(values_ref, weight_ref, out_ref):
    rows = values_ref.shape[0]
    place = lax.broadcasted_iota(jnp.int32, (rows, rows), 0)
    source = lax.broadcasted_iota(jnp.int32, (rows, rows), 1)
    lane = place % TP
    chunk = (place // TP) % (X * ZL)
    role = place // (TP * X * ZL)
    order = (source == chunk * MEMBERS + role * TP + lane).astype(F32).astype(BF16)
    values = nn_dot(order, values_ref[...]).astype(BF16)
    out_ref[...] = nt_dot(values, weight_ref[...]).astype(BF16)


def reduce_kernel(parts_ref, out_ref):
    total = jnp.sum(parts_ref[...].astype(F32), axis=0).astype(BF16)
    out_ref[...] = jnp.broadcast_to(total[None], out_ref.shape)


def route_kernel(
    place_ref, routed_ref, weight_ref, pick_ref, high_ref, low_ref, named_ref, rank_ref
):
    dims = (EXPERTS, ROWBLK)
    expert_ids = lax.broadcasted_iota(jnp.int32, dims, 0)
    named = jnp.zeros(dims, F32)
    weights = jnp.zeros(dims, F32)
    for k in range(routed_ref.shape[0]):
        chosen = expert_ids == routed_ref[k : k + 1, :]
        named = named + jnp.where(chosen, 1.0, 0.0)
        weights = weights + jnp.where(chosen, weight_ref[k : k + 1, :], 0.0)
    earlier = lax.broadcasted_iota(jnp.int32, (ROWBLK, ROWBLK), 0) < lax.broadcasted_iota(
        jnp.int32, (ROWBLK, ROWBLK), 1
    )
    before = jnp.where(earlier, 1.0, 0.0).astype(BF16)
    rank = nn_dot(named.astype(BF16), before)
    rank = jnp.where(named > 0.5, rank, -1.0)
    rank_ref[...] = rank
    named_ref[...] = weights
    slots = lax.broadcasted_iota(jnp.int32, (MOST, ROWBLK), 0).astype(F32)
    for half in range(2):
        for z in range(Z):
            for pair in range(2):
                expert = (half * 2 + pair) * Z + z
                hit = rank_ref[expert : expert + 1, :] == slots
                table = jnp.where(hit, named_ref[expert : expert + 1, :], 0.0)
                high = table.astype(BF16)
                low = (table - high.astype(F32)).astype(BF16)
                rows = pl.ds(z * 32 + pair * MOST, MOST)
                lanes = pl.ds(half * HALF, ROWBLK)
                high_ref[rows, lanes] = high
                low_ref[rows, lanes] = low
    for x in range(X):
        row = rank_ref[pl.ds(x * Z + place_ref[0] * ZL + place_ref[1], 1), :]
        pick_ref[x * MOST : (x + 1) * MOST, :] = jnp.where(row == slots, 1.0, 0.0).astype(BF16)


def dispatch_kernel(place_ref, parts_ref, residual_ref, pick_ref, out_ref, own_ref):
    pick = pick_ref[...]
    own = jnp.zeros((COLS, ROWBLK), F32)
    column = lax.broadcasted_iota(jnp.int32, (COLS, PART), 0)
    feature = lax.broadcasted_iota(jnp.int32, (COLS, PART), 1)
    for zl in range(ZL):
        attention = jnp.concatenate(
            [parts_ref[zh * ZL + zl].astype(F32) for zh in range(ZH)], axis=0
        )
        hidden = (residual_ref[zl].astype(F32) + attention).astype(BF16)
        wanted = (feature == column + place_ref[0] * COLS) & (place_ref[1] == zl)
        own = own + nt_dot(jnp.where(wanted, 1.0, 0.0).astype(BF16), hidden)
        rows = nn_dot(pick, hidden).astype(BF16)
        for x in range(X):
            piece = rows[x * MOST : (x + 1) * MOST]
            for lane in range(TP):
                out_ref[x * TP + lane, zl] = piece
    own_ref[...] = own


def expert_kernel(
    arrived_ref, gain_ref, own_in_ref, peer_in_ref, own_down_ref, peer_down_ref, out_ref
):
    rows = TP * MOST
    values = []
    total = jnp.zeros((rows, 1), F32)
    for x in range(X):
        for zl in range(ZL):
            value = jnp.concatenate(
                [arrived_ref[x * TP + lane, zl] for lane in range(TP)], axis=0
            ).astype(F32)
            total = total + jnp.sum(value * value, axis=1, keepdims=True)
            values.append(value)
    inverse = lax.rsqrt(total / WIDTH + NORM_EPS)
    own = jnp.zeros((rows, 256), F32)
    peer = jnp.zeros((rows, 256), F32)
    for i, value in enumerate(values):
        normed = (value * inverse * gain_ref[i]).astype(BF16)
        own = own + nn_dot(normed, own_in_ref[i])
        peer = peer + nn_dot(normed, peer_in_ref[i])

    def activate(both):
        gate, up = both[:, :128], both[:, 128:]
        return (gate / (1.0 + jnp.exp(-gate)) * up).astype(BF16)

    own_act, peer_act = activate(own), activate(peer)
    for x in range(X):
        lanes = pl.ds(x * PLANE, PLANE)
        product = nn_dot(own_act, own_down_ref[:, lanes]) + nn_dot(
            peer_act, peer_down_ref[:, lanes]
        )
        product = product.astype(BF16)
        for lane in range(TP):
            out_ref[x * TP + lane] = product[lane * MOST : (lane + 1) * MOST]


def columns_kernel(parts_ref, out_ref):
    summed = []
    for x in range(X):
        total = parts_ref[x * TP].astype(F32)
        for lane in range(1, TP):
            total = total + parts_ref[x * TP + lane].astype(F32)
        summed.append(total)
    low = jnp.concatenate(summed[:2], axis=0)
    high = jnp.concatenate(summed[2:], axis=0)
    gap = jnp.zeros((32, HALF - COLS), F32)
    for z in range(Z):
        cut = slice(z * COLS, (z + 1) * COLS)
        out_ref[z] = jnp.concatenate([low[:, cut], gap, high[:, cut], gap], axis=1).astype(BF16)


def combine_kernel(returned_ref, high_ref, low_ref, own_ref, out_ref):
    returned = returned_ref[...]
    dims = (((0,), (0,)), ((), ()))
    mixed = lax.dot_general(returned, high_ref[...], dims, preferred_element_type=F32)
    mixed = mixed + lax.dot_general(returned, low_ref[...], dims, preferred_element_type=F32)
    mixture = mixed[:COLS, :ROWBLK] + mixed[HALF : HALF + COLS, HALF : HALF + ROWBLK]
    out_ref[...] = (own_ref[...] + mixture).astype(BF16)


def shards(
    queries,
    latent_cache,
    lengths,
    value_up,
    output_weight,
    residual,
    norm_gain,
    routed_experts,
    route_weights,
    gate_weight,
    up_weight,
    down_weight,
):
    swap = [(0, 1), (1, 0)]
    block = lax.axis_index("role") * TP + lax.axis_index("tp")
    place = jnp.stack([lax.axis_index("zh"), lax.axis_index("zl")]).astype(jnp.int32)

    weight_rows = lax.all_gather(output_weight, "zh", axis=0, tiled=True)
    residual_block = lax.dynamic_slice_in_dim(residual, block * ROWBLK, ROWBLK, 1).T
    residual_rows = lax.all_gather(residual_block, ("zh", "zl"), axis=0, tiled=False)
    residual_rows = (
        residual_rows.reshape(ZH, ZL, ROWBLK, COLS)
        .transpose(1, 2, 0, 3)
        .reshape(ZL, ROWBLK, PART)
    )
    gain_rows = norm_gain.reshape(X, ZH, ZL, COLS).transpose(0, 2, 1, 3).reshape(X * ZL, 1, PART)
    own_in = jnp.concatenate([gate_weight[0], up_weight[0]], axis=1)
    own_in = (
        own_in.reshape(X, ZH, ZL, COLS, 256).transpose(0, 2, 1, 3, 4).reshape(X * ZL, PART, 256)
    )
    own_down = down_weight[0]
    peer_in = lax.ppermute(own_in, "role", swap)
    peer_down = lax.ppermute(own_down, "role", swap)
    routed_rows = lax.dynamic_slice_in_dim(routed_experts, block * ROWBLK, ROWBLK, 0).T
    route_rows = lax.dynamic_slice_in_dim(route_weights, block * ROWBLK, ROWBLK, 0).T
    pick, high, low = local_call(
        route_kernel,
        (shape((X * MOST, ROWBLK)), shape((Z * 32, 128)), shape((Z * 32, 128))),
        place,
        routed_rows,
        route_rows,
        scratch=(pltpu.VMEM((EXPERTS, ROWBLK), F32), pltpu.VMEM((EXPERTS, ROWBLK), F32)),
        smem=(0,),
    )

    heads = queries.shape[1]
    own_heads = heads // MEMBERS
    attended = local_call(
        attend_kernel, shape((heads, LAT)), lengths, queries, latent_cache, smem=(0,)
    )
    attended = attended.reshape(MEMBERS, own_heads, LAT)
    regrouped = lax.all_to_all(attended, ("role", "tp"), 0, 0, tiled=True)
    values = local_call(
        value_kernel,
        shape((X * ZL, MEMBERS, own_heads * 128)),
        regrouped.reshape(MEMBERS * own_heads, LAT),
        value_up,
    )
    gathered = lax.all_to_all(values, ("x", "zl"), 0, 0, tiled=True)
    projected = local_call(
        project_kernel,
        shape((X * ZL * MEMBERS, PART)),
        gathered.reshape(X * ZL * MEMBERS, own_heads * 128),
        weight_rows,
    )
    head_parts = lax.all_to_all(
        projected.reshape(MEMBERS, ZL * TP, PART), ("role", "tp"), 0, 0, tiled=True
    )
    attention = local_call(reduce_kernel, shape((Z, ZL * TP, PART)), head_parts)
    attention = lax.all_to_all(attention, ("zh", "zl"), 0, 0, tiled=True)
    outbound, own_hidden = local_call(
        dispatch_kernel,
        (shape((X * TP, ZL, MOST, PART)), shape((COLS, ROWBLK), F32)),
        place,
        attention,
        residual_rows,
        pick,
        smem=(0,),
    )
    arrived = lax.all_to_all(outbound, ("x", "tp"), 0, 0, tiled=True)
    partial = local_call(
        expert_kernel,
        shape((X * TP, MOST, PLANE)),
        arrived,
        gain_rows,
        own_in,
        peer_in,
        own_down,
        peer_down,
    )
    hidden_parts = lax.all_to_all(partial, ("x", "tp"), 0, 0, tiled=True)
    columns = local_call(columns_kernel, shape((Z, 32, 128)), hidden_parts)
    returned = lax.all_to_all(columns, ("zh", "zl"), 0, 0, tiled=True)
    return local_call(
        combine_kernel,
        shape((COLS, ROWBLK)),
        returned.reshape(Z * 32, 128),
        high,
        low,
        own_hidden,
    )


def solution(mesh):
    grp = ("x", "zh", "zl")
    fine = Mesh(
        mesh.devices.reshape(ROLE, X, ZH, ZL, TP), ("role", "x", "zh", "zl", "tp")
    )
    return jax.shard_map(
        shards,
        mesh=fine,
        in_specs=(
            P(("role",) + grp + ("tp",), None, None),
            P(("role",) + grp + ("tp",), None, None),
            P(("role",) + grp + ("tp",)),
            P(("role", "tp"), None, None),
            P(grp, ("role", "tp")),
            P(grp, None),
            P(),
            P(),
            P(),
            P(grp, None, ("role", "tp")),
            P(grp, None, ("role", "tp")),
            P(grp, ("role", "tp"), None),
        ),
        out_specs=P(grp, ("role", "tp")),
        check_vma=False,
    )
```

time: 397 us -> 174 us (0.44)
  the two profiles are of different devices: /device:TPU:1 before, /device:TPU:32 now
where the time goes in v1:
time: 174 us; the launch traced here: 173 us
  blocking collectives  111 us (64%)
  starting transfers between devices  31.1 us (18%)
  waiting for transfers between devices  11.4 us (7%)
  local copies, waits for them, and re-layouts  8.88 us (5%)
  Pallas kernels  8.56 us (5%)
    all_gather x1, blocking collectives, shards(): lax.all_gather(residual_block, ('zh', 'zl'), axis=0, tiled=False)  33.2 us
    all_gather x1, blocking collectives, shards(): weight_rows = lax.all_gather(output_weight, 'zh', axis=0, tiled=True)  30.3 us
    all_to_all x1, blocking collectives, shards(): returned = lax.all_to_all(columns, ('zh', 'zl'), 0, 0, tiled=True)  24.6 us
    all_to_all x1, blocking collectives, shards(): hidden_parts = lax.all_to_all(partial, ('x', 'tp'), 0, 0, tiled=True)  13.1 us
    all_to_all x1, blocking collectives, shards(): regrouped = lax.all_to_all(attended, ('role', 'tp'), 0, 0, tiled=True)  9.63 us
    all_to_all x1, starting transfers between devices, shards(): attention = lax.all_to_all(attention, ('zh', 'zl'), 0, 0, tiled=True)  9.44 us
    pallas_call x9, Pallas kernels, local_call(): pl.pallas_call(body, out_shape=out_shape, in_specs=specs, out_specs=jax.t...  8.56 us
    all_to_all x1, starting transfers between devices, shards(): gathered = lax.all_to_all(values, ('x', 'zl'), 0, 0, tiled=True)  8.49 us
  transfers between devices with their start and end apart: 6, of which 2 were waited for; matrix products, arithmetic and copies ran while one was open for 4% of the time, Pallas kernels for 2%

profile of v1, /device:TPU:32, one launch (start us, length us, event | category | flops | bytes accessed | tf_op | source)
XLA Modules:
  0.0 173.3 jit_solution(17330321072742230422)
XLA Ops:
  0.0 0.0 copy-start
  0.0 0.0 copy-start.1
  0.7 1.3 copy.22.cache_ref
  2.0 0.0 copy-start.7
  2.0 0.9 copy-done.7
  2.9 0.0 copy-start.8
  2.9 0.6 shard_map.118
  3.5 9.6 %all_to_all.35 = bf16[8,8,512]{2,1,0:T(8,128)(2,1)S(1)} all-to-all(bf16[8,8,512]{2,1,0:T(8,128)(2,1)S(1)} %bitcast.31), channel_id=1, replica_groups=mesh['role'=2,'x'=4,'zh'=4,'zl'=4,'tp'=4] {'role','tp'}, dimensions={0} | all-to-all | bytes 131072 | tf_op jit(solution)/shard_map/all_to_all | solution.py:269
  13.1 0.0 copy-done.1
  13.1 1.0 shard_map.119
  14.1 8.5 %all-to-all-start.1 = ((bf16[16,8,1024]{2,1,0:T(8,128)(2,1)}), bf16[16,8,1024]{2,1,0:T(8,128)(2,1)S(1)}, u32[]{:S(2)}, u32[]{:S(2)}) async-start(bf16[16,8,1024]{2,1,0:T(8,128)(2,1)} %shard_map.119), calls=%async_computation.1 | async-start | bytes 524288 | tf_op jit(solution)/shard_map/all_to_all | solution.py:276
  22.6 0.0 copy-done.8
  22.6 1.6 pad_maximum_fusion
  24.2 0.0 copy-start.9
  24.2 0.0 copy-start.2
  24.2 0.2 copy.27
  24.4 2.1 %collective-permute-start = (bf16[16,224,256]{2,1,0:T(8,128)(2,1)S(1)}, bf16[16,224,256]{2,1,0:T(8,128)(2,1)}, u32[]{:S(2)}, u32[]{:S(2)}) collective-permute-start(bf16[16,224,256]{2,1,0:T(8,128)(2,1)S(1)} %bitcast.24), channel_id=1, source_target_pairs={{0,256},{256,0},{1,257},{257,1},{2,258},{258,2},{3,259},{259,3},{4... | collective-permute-start | bytes 5505032 | tf_op jit(solution)/shard_map/ppermute | solution.py:249
  26.5 0.0 copy-done.9
  26.5 30.3 %all_gather.9.weight_ref = bf16[224,1024]{1,0:T(8,128)(2,1)S(1)} all-gather(bf16[56,1024]{1,0:T(8,128)(2,1)S(1)} %copy-done.9), channel_id=1, replica_groups=mesh['role'=2,'x'=4,'zh'=4,'zl'=4,'tp'=4] {'zh'}, dimensions={0}, use_global_device_ids=true | all-gather | bytes 573440 | tf_op jit(solution)/shard_map/all_gather | solution.py:235
  56.8 0.0 all-to-all-done.1
  56.8 0.0 copy-start.10
  56.8 0.4 shard_map.120
  57.2 0.0 copy-start.4
  57.2 0.6 copy-done.4
  57.8 3.3 %all-to-all-start.2 = ((bf16[8,16,224]{2,1,0:T(8,128)(2,1)}), bf16[8,16,224]{2,1,0:T(8,128)(2,1)S(1)}, u32[]{:S(2)}, u32[]{:S(2)}) async-start(bf16[8,16,224]{2,1,0:T(8,128)(2,1)} %bitcast.30), calls=%async_computation.2 | async-start | bytes 131072 | tf_op jit(solution)/shard_map/all_to_all | solution.py:283
  61.1 0.0 copy-done.2
  61.2 2.3 %collective-permute-start.1 = (bf16[128,3584]{1,0:T(8,128)(2,1)S(1)}, bf16[128,3584]{1,0:T(8,128)(2,1)}, u32[]{:S(2)}, u32[]{:S(2)}) collective-permute-start(bf16[128,3584]{1,0:T(8,128)(2,1)S(1)} %bitcast.27), channel_id=1, source_target_pairs={{0,256},{256,0},{1,257},{257,1},{2,258},{258,2},{3,259},{259,3},{4... | collective-permute-start | bytes 2752520 | tf_op jit(solution)/shard_map/ppermute | solution.py:250
  63.5 2.9 %all-to-all-done.2.parts_ref = bf16[8,16,224]{2,1,0:T(8,128)(2,1)S(1)} async-done(((bf16[8,16,224]{2,1,0:T(8,128)(2,1)}), bf16[8,16,224]{2,1,0:T(8,128)(2,1)S(1)}, u32[]{:S(2)}, u32[]{:S(2)}) %all-to-all-start.2) | async-done | bytes 57376 | tf_op jit(solution)/shard_map/all_to_all | solution.py:283
  66.4 0.7 shard_map.121
  67.1 9.4 %all-to-all-start.3 = ((bf16[16,16,224]{2,1,0:T(8,128)(2,1)}), bf16[16,16,224]{2,1,0:T(8,128)(2,1)S(1)}, u32[]{:S(2)}, u32[]{:S(2)}) async-start(bf16[16,16,224]{2,1,0:T(8,128)(2,1)} %shard_map.121), calls=%async_computation.3 | async-start | bytes 262144 | tf_op jit(solution)/shard_map/all_to_all | solution.py:287
  76.5 0.0 copy-done
  76.5 0.1 dynamic-slice_bitcast_fusion
  76.6 33.2 %all-gather.1 = bf16[16,64,56]{1,2,0:T(8,128)(2,1)} all-gather(bf16[1,64,56]{1,2,0:T(8,128)(2,1)S(1)} %dynamic-slice_bitcast_fusion), channel_id=2, replica_groups=mesh['role'=2,'x'=4,'zh'=4,'zl'=4,'tp'=4] {'zh','zl'}, dimensions={0}, use_global_device_ids=true | all-gather | bytes 121856 | tf_op jit(solution)/shard_map/all_gather | solution.py:237
  109.8 1.1 copy.23
  110.9 0.2 reshape.40.residual_ref
  111.1 0.1 pad_add_fusion.place_ref
  111.2 0.8 dynamic-slice_bitcast_fusion.2.routed_ref
  111.9 0.8 dynamic-slice_bitcast_fusion.1.weight_ref
  112.7 0.9 shard_map.122
  113.6 0.0 copy-start.5
  113.6 0.6 copy-done.5
  114.2 0.0 all-to-all-done.3.parts_ref
  114.3 0.8 shard_map.123
  115.0 0.0 copy-start.3
  115.0 0.8 copy-done.3
  115.8 5.4 %all-to-all-start.4 = ((bf16[16,4,16,224]{3,2,1,0:T(8,128)(2,1)}), bf16[16,4,16,224]{3,2,1,0:T(8,128)(2,1)S(1)}, u32[]{:S(2)}, u32[]{:S(2)}) async-start(bf16[16,4,16,224]{3,2,1,0:T(8,128)(2,1)} %copy-done.3), calls=%async_computation.4 | async-start | bytes 1048576 | tf_op jit(solution)/shard_map/all_to_all | solution.py:297
  121.2 0.0 copy-done.10
  121.2 0.7 reshape.41
  122.0 0.8 copy.24
  122.7 0.1 reshape.42.gain_ref
  122.8 0.0 collective-permute-done.1.peer_down_ref
  122.8 0.0 collective-permute-done.peer_in_ref
  122.9 8.5 %all-to-all-done.4.arrived_ref = bf16[16,4,16,224]{3,2,1,0:T(8,128)(2,1)S(1)} async-done(((bf16[16,4,16,224]{3,2,1,0:T(8,128)(2,1)}), bf16[16,4,16,224]{3,2,1,0:T(8,128)(2,1)S(1)}, u32[]{:S(2)}, u32[]{:S(2)}) %all-to-all-start.4) | async-done | bytes 458784 | tf_op jit(solution)/shard_map/all_to_all | solution.py:297
  131.3 3.1 %shard_map.124 = bf16[16,16,896]{2,1,0:T(8,128)(2,1)S(1)} custom-call(bf16[16,4,16,224]{3,2,1,0:T(8,128)(2,1)S(1)} %all-to-all-done.4.arrived_ref, f32[16,1,224]{2,1,0:T(1,128)S(1)} %reshape.42.gain_ref, bf16[16,224,256]{2,1,0:T(8,128)(2,1)S(1)} %bitcast.25, bf16[16,224,256]{2,1,0:T(8,128)(2,1)} %collective-permute-done.peer_in_ref, ...), custom_call_target="tpu_custom_call" | custom-call | tf_op jit(solution)/shard_map/pallas_call | solution.py:43
  134.5 0.0 copy-start.6
  134.5 13.1 %all_to_all.36.parts_ref = bf16[16,16,896]{2,1,0:T(8,128)(2,1)S(1)} all-to-all(bf16[16,16,896]{2,1,0:T(8,128)(2,1)S(1)} %shard_map.124), channel_id=1, replica_groups=mesh['role'=2,'x'=4,'zh'=4,'zl'=4,'tp'=4] {'x','tp'}, dimensions={0} | all-to-all | bytes 917504 | tf_op jit(solution)/shard_map/all_to_all | solution.py:308
  147.6 0.2 shard_map.125
  147.8 24.6 %all_to_all.37 = bf16[16,32,128]{2,1,0:T(8,128)(2,1)S(1)} all-to-all(bf16[16,32,128]{2,1,0:T(8,128)(2,1)S(1)} %shard_map.125), channel_id=1, replica_groups=mesh['role'=2,'x'=4,'zh'=4,'zl'=4,'tp'=4] {'zh','zl'}, dimensions={0} | all-to-all | bytes 262144 | tf_op jit(solution)/shard_map/all_to_all | solution.py:310
  172.4 0.0 copy-done.6
  172.4 0.9 shard_map.126
Async XLA Ops:
  0.0 76.5 %copy-start = (bf16[56,512]{1,0:T(8,128)(2,1)S(1)}, bf16[56,512]{1,0:T(8,128)(2,1)}, u32[]{:S(2)}) copy-start(bf16[56,512]{1,0:T(8,128)(2,1)} %param.17) | copy-start | bytes 172036
  0.0 13.1 %copy-start.1 = (bf16[8,512,128]{2,1,0:T(8,128)(2,1)S(1)}, bf16[8,512,128]{2,1,0:T(8,128)(2,1)}, u32[]{:S(2)}) copy-start(bf16[8,512,128]{2,1,0:T(8,128)(2,1)} %value_ref.1) | copy-start | bytes 3145732
  2.0 0.9 copy-start.7
  2.9 19.7 %copy-start.8 = (bf16[1,3584,128]{2,1,0:T(8,128)(2,1)S(1)}, bf16[1,3584,128]{2,1,0:T(8,128)(2,1)}, u32[]{:S(2)}) copy-start(bf16[1,3584,128]{2,1,0:T(8,128)(2,1)} %param.22) | copy-start | bytes 2752516
  14.1 42.6 %all-to-all-start.1 = ((bf16[16,8,1024]{2,1,0:T(8,128)(2,1)}), bf16[16,8,1024]{2,1,0:T(8,128)(2,1)S(1)}, u32[]{:S(2)}, u32[]{:S(2)}) async-start(bf16[16,8,1024]{2,1,0:T(8,128)(2,1)} %shard_map.119), calls=%async_computation.1 | async-start | bytes 524288 | tf_op jit(solution)/shard_map/all_to_all | solution.py:276
  24.2 2.3 %copy-start.9 = (bf16[56,1024]{1,0:T(8,128)(2,1)S(1)}, bf16[56,1024]{1,0:T(8,128)(2,1)}, u32[]{:S(2)}) copy-start(bf16[56,1024]{1,0:T(8,128)(2,1)} %param.16) | copy-start | bytes 344068
  24.2 36.9 %copy-start.2 = (bf16[1,128,3584]{2,1,0:T(8,128)(2,1)S(1)}, bf16[1,128,3584]{2,1,0:T(8,128)(2,1)}, u32[]{:S(2)}) copy-start(bf16[1,128,3584]{2,1,0:T(8,128)(2,1)} %param.23) | copy-start | bytes 2752516
  24.4 98.4 %collective-permute-start = (bf16[16,224,256]{2,1,0:T(8,128)(2,1)S(1)}, bf16[16,224,256]{2,1,0:T(8,128)(2,1)}, u32[]{:S(2)}, u32[]{:S(2)}) collective-permute-start(bf16[16,224,256]{2,1,0:T(8,128)(2,1)S(1)} %bitcast.24), channel_id=1, source_target_pairs={{0,256},{256,0},{1,257},{257,1},{2,258},{258,2},{3,259},{259,3},{4... | collective-permute-start | bytes 5505032 | tf_op jit(solution)/shard_map/ppermute | solution.py:249
  56.8 64.5 %copy-start.10 = (f32[3584]{0:T(1024)S(1)}, f32[3584]{0:T(1024)}, u32[]{:S(2)}) copy-start(f32[3584]{0:T(1024)} %param.18) | copy-start | bytes 43012
  57.2 0.6 copy-start.4
  57.8 8.6 %all-to-all-start.2 = ((bf16[8,16,224]{2,1,0:T(8,128)(2,1)}), bf16[8,16,224]{2,1,0:T(8,128)(2,1)S(1)}, u32[]{:S(2)}, u32[]{:S(2)}) async-start(bf16[8,16,224]{2,1,0:T(8,128)(2,1)} %bitcast.30), calls=%async_computation.2 | async-start | bytes 131072 | tf_op jit(solution)/shard_map/all_to_all | solution.py:283
  61.2 61.7 %collective-permute-start.1 = (bf16[128,3584]{1,0:T(8,128)(2,1)S(1)}, bf16[128,3584]{1,0:T(8,128)(2,1)}, u32[]{:S(2)}, u32[]{:S(2)}) collective-permute-start(bf16[128,3584]{1,0:T(8,128)(2,1)S(1)} %bitcast.27), channel_id=1, source_target_pairs={{0,256},{256,0},{1,257},{257,1},{2,258},{258,2},{3,259},{259,3},{4... | collective-permute-start | bytes 2752520 | tf_op jit(solution)/shard_map/ppermute | solution.py:250
  67.1 47.2 %all-to-all-start.3 = ((bf16[16,16,224]{2,1,0:T(8,128)(2,1)}), bf16[16,16,224]{2,1,0:T(8,128)(2,1)S(1)}, u32[]{:S(2)}, u32[]{:S(2)}) async-start(bf16[16,16,224]{2,1,0:T(8,128)(2,1)} %shard_map.121), calls=%async_computation.3 | async-start | bytes 262144 | tf_op jit(solution)/shard_map/all_to_all | solution.py:287
  113.6 0.6 copy-start.5
  115.0 0.8 copy-start.3
  115.8 15.5 %all-to-all-start.4 = ((bf16[16,4,16,224]{3,2,1,0:T(8,128)(2,1)}), bf16[16,4,16,224]{3,2,1,0:T(8,128)(2,1)S(1)}, u32[]{:S(2)}, u32[]{:S(2)}) async-start(bf16[16,4,16,224]{3,2,1,0:T(8,128)(2,1)} %copy-done.3), calls=%async_computation.4 | async-start | bytes 1048576 | tf_op jit(solution)/shard_map/all_to_all | solution.py:297
  134.5 37.9 %copy-start.6 = (bf16[512,128]{1,0:T(8,128)(2,1)S(1)}, bf16[512,128]{1,0:T(8,128)(2,1)}, u32[]{:S(2)}) copy-start(bf16[512,128]{1,0:T(8,128)(2,1)} %copy-done.5) | copy-start | bytes 393220

commit v2 on v1

--- a/solution.py
+++ b/solution.py
@@ -56,13 +56,13 @@
 
 def attend_kernel(length_ref, query_ref, cache_ref, out_ref):
     cache = cache_ref[0]
-    scores = nt_dot(query_ref[0], cache) * SOFTMAX_SCALE
+    scores = nn_dot(query_ref[0], cache) * SOFTMAX_SCALE
     visible = lax.broadcasted_iota(jnp.int32, scores.shape, 1) < length_ref[0]
     scores = jnp.where(visible, scores, -1e30)
     row_max = jnp.max(scores, axis=1, keepdims=True)
     weights = jnp.where(visible, jnp.exp(scores - row_max), 0.0)
     row_total = jnp.sum(weights, axis=1, keepdims=True)
-    summed = nn_dot(weights.astype(BF16), cache[:, :LAT])
+    summed = nt_dot(weights.astype(BF16), cache[:LAT])
     out_ref[...] = (summed / row_total).astype(BF16)
 
 
@@ -80,7 +80,11 @@
         )
 
 
-def project_kernel(values_ref, weight_ref, out_ref):
+def project_kernel(place_ref, values_ref, *refs):
+    payloads, (out_ref, residual_ref, held_ref) = refs[:ZH], refs[ZH:]
+    zh = place_ref[0]
+    for step, payload in enumerate(payloads):
+        held_ref[lax.rem(zh + ZH - step, ZH)] = payload[...]
     rows = values_ref.shape[0]
     place = lax.broadcasted_iota(jnp.int32, (rows, rows), 0)
     source = lax.broadcasted_iota(jnp.int32, (rows, rows), 1)
@@ -89,11 +93,22 @@
     role = place // (TP * X * ZL)
     order = (source == chunk * MEMBERS + role * TP + lane).astype(F32).astype(BF16)
     values = nn_dot(order, values_ref[...]).astype(BF16)
-    out_ref[...] = nt_dot(values, weight_ref[...]).astype(BF16)
-
-
-def reduce_kernel(parts_ref, out_ref):
-    total = jnp.sum(parts_ref[...].astype(F32), axis=0).astype(BF16)
+    depth = values.shape[1]
+    token = lax.broadcasted_iota(jnp.int32, (ZL * TP, ROWBLK), 0)
+    request = lax.broadcasted_iota(jnp.int32, (ZL * TP, ROWBLK), 1)
+    mine = (request == token + zh * (ZL * TP)).astype(F32).astype(BF16)
+    out, residual = [], []
+    for i in range(ZH):
+        held = held_ref[i]
+        out.append(nt_dot(values, held[:, :depth]))
+        residual.append(nt_dot(mine, held[:, depth : depth + ROWBLK]))
+    out_ref[...] = jnp.concatenate(out, axis=1).astype(BF16)
+    residual_ref[...] = jnp.concatenate(residual, axis=1)
+
+
+def hidden_kernel(parts_ref, residual_ref, out_ref):
+    total = jnp.sum(parts_ref[...].astype(F32), axis=0)
+    total = (residual_ref[...] + total).astype(BF16)
     out_ref[...] = jnp.broadcast_to(total[None], out_ref.shape)
 
 
@@ -134,24 +149,23 @@
         pick_ref[x * MOST : (x + 1) * MOST, :] = jnp.where(row == slots, 1.0, 0.0).astype(BF16)
 
 
-def dispatch_kernel(place_ref, parts_ref, residual_ref, pick_ref, out_ref, own_ref):
-    pick = pick_ref[...]
-    own = jnp.zeros((COLS, ROWBLK), F32)
-    column = lax.broadcasted_iota(jnp.int32, (COLS, PART), 0)
-    feature = lax.broadcasted_iota(jnp.int32, (COLS, PART), 1)
-    for zl in range(ZL):
-        attention = jnp.concatenate(
-            [parts_ref[zh * ZL + zl].astype(F32) for zh in range(ZH)], axis=0
-        )
-        hidden = (residual_ref[zl].astype(F32) + attention).astype(BF16)
-        wanted = (feature == column + place_ref[0] * COLS) & (place_ref[1] == zl)
-        own = own + nt_dot(jnp.where(wanted, 1.0, 0.0).astype(BF16), hidden)
-        rows = nn_dot(pick, hidden).astype(BF16)
-        for x in range(X):
-            piece = rows[x * MOST : (x + 1) * MOST]
-            for lane in range(TP):
-                out_ref[x * TP + lane, zl] = piece
-    own_ref[...] = own
+def dispatch_kernel(place_ref, parts_ref, pick_ref, out_ref, own_ref):
+    hidden = jnp.concatenate(
+        [
+            jnp.concatenate([parts_ref[zh * ZL + zl].astype(F32) for zh in range(ZH)], axis=0)
+            for zl in range(ZL)
+        ],
+        axis=1,
+    ).astype(BF16)
+    rows = nn_dot(pick_ref[...], hidden).astype(BF16)
+    for x in range(X):
+        piece = rows[x * MOST : (x + 1) * MOST]
+        for lane in range(TP):
+            out_ref[x * TP + lane] = piece
+    column = lax.broadcasted_iota(jnp.int32, (COLS, PLANE), 0)
+    feature = lax.broadcasted_iota(jnp.int32, (COLS, PLANE), 1)
+    wanted = feature == column + (place_ref[1] * PART + place_ref[0] * COLS)
+    own_ref[...] = nt_dot(jnp.where(wanted, 1.0, 0.0).astype(BF16), hidden)
 
 
 def expert_kernel(
@@ -161,12 +175,11 @@
     values = []
     total = jnp.zeros((rows, 1), F32)
     for x in range(X):
-        for zl in range(ZL):
-            value = jnp.concatenate(
-                [arrived_ref[x * TP + lane, zl] for lane in range(TP)], axis=0
-            ).astype(F32)
-            total = total + jnp.sum(value * value, axis=1, keepdims=True)
-            values.append(value)
+        value = jnp.concatenate(
+            [arrived_ref[x * TP + lane] for lane in range(TP)], axis=0
+        ).astype(F32)
+        total = total + jnp.sum(value * value, axis=1, keepdims=True)
+        values.append(value)
     inverse = lax.rsqrt(total / WIDTH + NORM_EPS)
     own = jnp.zeros((rows, 256), F32)
     peer = jnp.zeros((rows, 256), F32)
@@ -232,18 +245,18 @@
     block = lax.axis_index("role") * TP + lax.axis_index("tp")
     place = jnp.stack([lax.axis_index("zh"), lax.axis_index("zl")]).astype(jnp.int32)
 
-    weight_rows = lax.all_gather(output_weight, "zh", axis=0, tiled=True)
-    residual_block = lax.dynamic_slice_in_dim(residual, block * ROWBLK, ROWBLK, 1).T
-    residual_rows = lax.all_gather(residual_block, ("zh", "zl"), axis=0, tiled=False)
-    residual_rows = (
-        residual_rows.reshape(ZH, ZL, ROWBLK, COLS)
-        .transpose(1, 2, 0, 3)
-        .reshape(ZL, ROWBLK, PART)
-    )
-    gain_rows = norm_gain.reshape(X, ZH, ZL, COLS).transpose(0, 2, 1, 3).reshape(X * ZL, 1, PART)
+    residual_block = lax.dynamic_slice_in_dim(residual, block * ROWBLK, ROWBLK, 1)
+    payload = jnp.concatenate(
+        [output_weight, residual_block, jnp.zeros((COLS, 128 - ROWBLK), BF16)], axis=1
+    )
+    payloads = [payload] + [
+        lax.ppermute(payload, "zh", [(i, (i + step) % ZH) for i in range(ZH)])
+        for step in range(1, ZH)
+    ]
+    gain_rows = norm_gain.reshape(X, ZH, ZL, COLS).transpose(0, 2, 1, 3).reshape(X, 1, PLANE)
     own_in = jnp.concatenate([gate_weight[0], up_weight[0]], axis=1)
     own_in = (
-        own_in.reshape(X, ZH, ZL, COLS, 256).transpose(0, 2, 1, 3, 4).reshape(X * ZL, PART, 256)
+        own_in.reshape(X, ZH, ZL, COLS, 256).transpose(0, 2, 1, 3, 4).reshape(X, PLANE, 256)
     )
     own_down = down_weight[0]
     peer_in = lax.ppermute(own_in, "role", swap)
@@ -263,7 +276,7 @@
     heads = queries.shape[1]
     own_heads = heads // MEMBERS
     attended = local_call(
-        attend_kernel, shape((heads, LAT)), lengths, queries, latent_cache, smem=(0,)
+        attend_kernel, shape((heads, LAT)), lengths, queries, latent_cache.swapaxes(1, 2), smem=(0,)
     )
     attended = attended.reshape(MEMBERS, own_heads, LAT)
     regrouped = lax.all_to_all(attended, ("role", "tp"), 0, 0, tiled=True)
@@ -274,23 +287,25 @@
         value_up,
     )
     gathered = lax.all_to_all(values, ("x", "zl"), 0, 0, tiled=True)
-    projected = local_call(
+    projected, residual_rows = local_call(
         project_kernel,
-        shape((X * ZL * MEMBERS, PART)),
+        (shape((X * ZL * MEMBERS, PART)), shape((ZL * TP, PART), F32)),
+        place,
         gathered.reshape(X * ZL * MEMBERS, own_heads * 128),
-        weight_rows,
+        *payloads,
+        scratch=(pltpu.VMEM((ZH,) + payload.shape, BF16),),
+        smem=(0,),
     )
     head_parts = lax.all_to_all(
         projected.reshape(MEMBERS, ZL * TP, PART), ("role", "tp"), 0, 0, tiled=True
     )
-    attention = local_call(reduce_kernel, shape((Z, ZL * TP, PART)), head_parts)
-    attention = lax.all_to_all(attention, ("zh", "zl"), 0, 0, tiled=True)
+    hidden = local_call(hidden_kernel, shape((Z, ZL * TP, PART)), head_parts, residual_rows)
+    hidden = lax.all_to_all(hidden, ("zh", "zl"), 0, 0, tiled=True)
     outbound, own_hidden = local_call(
         dispatch_kernel,
-        (shape((X * TP, ZL, MOST, PART)), shape((COLS, ROWBLK), F32)),
+        (shape((X * TP, MOST, PLANE)), shape((COLS, ROWBLK), F32)),
         place,
-        attention,
-        residual_rows,
+        hidden,
         pick,
         smem=(0,),
     )

time: 174 us -> 156 us (0.90)
  blocking collectives: 111 us -> 48.8 us
  starting transfers between devices: 31.1 us -> 54.7 us
  waiting for transfers between devices: 11.4 us -> 30.4 us
    all_gather x2 -> x0, blocking collectives: 63.4 us -> none  [the longest x1 33.2 us: shards(): lax.all_gather(residual_block, ('zh', 'zl'), axis=0, tiled=False)]
    ppermute x0 -> x3, starting transfers between devices: none -> 22.8 us  [shards(): lax.ppermute(payload, 'zh', [(i, (i + step) % ZH) for i in range(ZH)])]
    ppermute x0 -> x3, waiting for transfers between devices: none -> 12.2 us  [shards(): lax.ppermute(payload, 'zh', [(i, (i + step) % ZH) for i in range(ZH)])]
    all_to_all x2 -> x1, waiting for transfers between devices: 2.93 us -> 11.5 us  [shards(): hidden = lax.all_to_all(hidden, ('zh', 'zl'), 0, 0, tiled=True)]
    all_to_all x0 -> x1, blocking collectives: none -> 7.86 us  [shards(): lax.all_to_all(projected.reshape(MEMBERS, ZL * TP, PART), ('role', 'tp'),...]
    all_to_all x1, blocking collectives: 24.6 us -> 18.3 us  [shards(): returned = lax.all_to_all(columns, ('zh', 'zl'), 0, 0, tiled=True)]
    all_to_all x2 -> x1, starting transfers between devices: 12.8 us -> 13.8 us  [shards(): hidden = lax.all_to_all(hidden, ('zh', 'zl'), 0, 0, tiled=True)]
    unnamed x24 -> x22, local copies, waits for them, and re-layouts: 4.29 us -> 4.52 us
  transfers between devices with their start and end apart: 6 -> 8, of which waited for: 2 -> 4; matrix products, arithmetic and copies ran while one was open for 4% -> 4% of each run, Pallas kernels for 2% -> 3%
where the time goes in v2:
time: 156 us; the launch traced here: 155 us
  starting transfers between devices  54.7 us (35%)
  blocking collectives  48.8 us (31%)
  waiting for transfers between devices  30.4 us (19%)
  Pallas kernels  9.58 us (6%)
  local copies, waits for them, and re-layouts  9.36 us (6%)
  other arithmetic  1.64 us (1%)
    ppermute x3, starting transfers between devices, shards(): lax.ppermute(payload, 'zh', [(i, (i + step) % ZH) for i in range(ZH)])  22.8 us
    all_to_all x1, blocking collectives, shards(): returned = lax.all_to_all(columns, ('zh', 'zl'), 0, 0, tiled=True)  18.3 us
    all_to_all x1, starting transfers between devices, shards(): hidden = lax.all_to_all(hidden, ('zh', 'zl'), 0, 0, tiled=True)  13.8 us
    all_to_all x1, blocking collectives, shards(): hidden_parts = lax.all_to_all(partial, ('x', 'tp'), 0, 0, tiled=True)  13 us
    ppermute x3, waiting for transfers between devices, shards(): lax.ppermute(payload, 'zh', [(i, (i + step) % ZH) for i in range(ZH)])  12.2 us
    all_to_all x1, waiting for transfers between devices, shards(): hidden = lax.all_to_all(hidden, ('zh', 'zl'), 0, 0, tiled=True)  11.5 us
    all_to_all x1, blocking collectives, shards(): regrouped = lax.all_to_all(attended, ('role', 'tp'), 0, 0, tiled=True)  9.63 us
    pallas_call x9, Pallas kernels, local_call(): pl.pallas_call(body, out_shape=out_shape, in_specs=specs, out_specs=jax.t...  9.58 us
  transfers between devices with their start and end apart: 8, of which 4 were waited for; matrix products, arithmetic and copies ran while one was open for 4% of the time, Pallas kernels for 3%

profile of v2, /device:TPU:32, one launch (start us, length us, event | category | flops | bytes accessed | tf_op | source)
XLA Modules:
  0.0 155.3 jit_solution(12074885638739713122)
XLA Ops:
  0.0 0.0 copy-start
  0.7 0.0 copy-start.4
  0.7 1.0 copy-done.4
  1.7 0.0 copy-start.5
  1.7 0.9 copy-done.5
  2.6 0.5 shard_map.118
  3.0 9.6 %all_to_all.35 = bf16[8,8,512]{2,1,0:T(8,128)(2,1)S(1)} all-to-all(bf16[8,8,512]{2,1,0:T(8,128)(2,1)S(1)} %bitcast.26), channel_id=1, replica_groups=mesh['role'=2,'x'=4,'zh'=4,'zl'=4,'tp'=4] {'role','tp'}, dimensions={0} | all-to-all | bytes 131072 | tf_op jit(solution)/shard_map/all_to_all | solution.py:282
  12.7 0.0 copy-start.1
  12.7 1.2 copy-done.1
  13.9 0.0 copy-start.8
  13.9 1.0 shard_map.119
  14.9 8.5 %all-to-all-start.1 = ((bf16[16,8,1024]{2,1,0:T(8,128)(2,1)}), bf16[16,8,1024]{2,1,0:T(8,128)(2,1)S(1)}, u32[]{:S(2)}, u32[]{:S(2)}) async-start(bf16[16,8,1024]{2,1,0:T(8,128)(2,1)} %shard_map.119), calls=%async_computation.1 | async-start | bytes 524288 | tf_op jit(solution)/shard_map/all_to_all | solution.py:289
  23.4 0.0 copy-done.8
  23.4 1.6 %pad_maximum_fusion = bf16[4,4,4,56,256]{4,3,2,1,0:T(8,128)(2,1)S(1)} fusion(bf16[4,4,4,56,128]{4,3,2,1,0:T(8,128)(2,1)S(1)} %bitcast.29, bf16[4,4,4,56,128]{4,3,2,1,0:T(8,128)(2,1)} %bitcast.30), kind=kLoop, calls=%fused_computation | loop fusion | flops 3670016 | bytes 3670016 | tf_op jit(solution)/shard_map/concatenate | solution.py:257
  25.0 0.0 copy-start.9
  25.0 0.0 copy-start.2
  25.0 0.2 copy.18
  25.2 0.0 copy-start.10
  25.2 2.1 %collective-permute-start.3 = (bf16[4,896,256]{2,1,0:T(8,128)(2,1)S(1)}, bf16[4,896,256]{2,1,0:T(8,128)(2,1)}, u32[]{:S(2)}, u32[]{:S(2)}) collective-permute-start(bf16[4,896,256]{2,1,0:T(8,128)(2,1)S(1)} %bitcast.19), channel_id=1, source_target_pairs={{0,256},{256,0},{1,257},{257,1},{2,258},{258,2},{3,259},{259,3},{4... | collective-permute-start | bytes 5505032 | tf_op jit(solution)/shard_map/ppermute | solution.py:262
  27.3 0.0 copy-done
  27.3 0.1 constant_dynamic-slice_fusion
  27.4 0.0 copy-done.9
  27.4 0.1 concatenate.11.refs_0_
  27.5 10.0 %collective-permute-start.2 = (bf16[56,1152]{1,0:T(8,128)(2,1)S(1)}, bf16[56,1152]{1,0:T(8,128)(2,1)S(1)}, u32[]{:S(2)}, u32[]{:S(2)}) collective-permute-start(bf16[56,1152]{1,0:T(8,128)(2,1)S(1)} %concatenate.11.refs_0_), channel_id=1, source_target_pairs={{0,48},{16,0},{32,16},{48,32},{1,49},{17,1},{33,17},{49,33},{2,50}... | collective-permute-start | bytes 387080 | tf_op jit(solution)/shard_map/ppermute | solution.py:253
  37.6 6.3 %collective-permute-start.1 = (bf16[56,1152]{1,0:T(8,128)(2,1)S(1)}, bf16[56,1152]{1,0:T(8,128)(2,1)S(1)}, u32[]{:S(2)}, u32[]{:S(2)}) collective-permute-start(bf16[56,1152]{1,0:T(8,128)(2,1)S(1)} %concatenate.11.refs_0_), channel_id=1, source_target_pairs={{0,32},{16,48},{32,0},{48,16},{1,33},{17,49},{33,1},{49,17},{2,34}... | collective-permute-start | bytes 387080 | tf_op jit(solution)/shard_map/ppermute | solution.py:253
  43.9 6.4 %collective-permute-start = (bf16[56,1152]{1,0:T(8,128)(2,1)S(1)}, bf16[56,1152]{1,0:T(8,128)(2,1)}, u32[]{:S(2)}, u32[]{:S(2)}) collective-permute-start(bf16[56,1152]{1,0:T(8,128)(2,1)S(1)} %concatenate.11.refs_0_), channel_id=1, source_target_pairs={{0,16},{16,32},{32,48},{48,0},{1,17},{17,33},{33,49},{49,1},{2,18}... | collective-permute-start | bytes 387080 | tf_op jit(solution)/shard_map/ppermute | solution.py:253
  50.3 0.0 copy-done.2
  50.3 1.9 %collective-permute-start.4 = (bf16[128,3584]{1,0:T(8,128)(2,1)S(1)}, bf16[128,3584]{1,0:T(8,128)(2,1)}, u32[]{:S(2)}, u32[]{:S(2)}) collective-permute-start(bf16[128,3584]{1,0:T(8,128)(2,1)S(1)} %bitcast.22), channel_id=1, source_target_pairs={{0,256},{256,0},{1,257},{257,1},{2,258},{258,2},{3,259},{259,3},{4... | collective-permute-start | bytes 2752520 | tf_op jit(solution)/shard_map/ppermute | solution.py:263
  52.2 0.1 pad_add_fusion.place_ref
  52.3 0.7 collective-permute-done.2.refs_3_
  53.1 11.4 %collective-permute-done.1.refs_2_ = bf16[56,1152]{1,0:T(8,128)(2,1)S(1)} collective-permute-done((bf16[56,1152]{1,0:T(8,128)(2,1)S(1)}, bf16[56,1152]{1,0:T(8,128)(2,1)S(1)}, u32[]{:S(2)}, u32[]{:S(2)}) %collective-permute-start.1) | collective-permute-done | bytes 129056 | tf_op jit(solution)/shard_map/ppermute | solution.py:253
  64.5 0.0 collective-permute-done.refs_1_
  64.5 0.0 all-to-all-done.1
  64.5 1.6 %shard_map.120 = (bf16[128,224]{1,0:T(8,128)(2,1)S(1)}, f32[16,224]{1,0:T(8,128)S(1)}) custom-call(s32[2]{0:T(128)S(1)} %pad_add_fusion.place_ref, bf16[128,1024]{1,0:T(8,128)(2,1)S(1)} %bitcast.21, bf16[56,1152]{1,0:T(8,128)(2,1)S(1)} %concatenate.11.refs_0_, bf16[56,1152]{1,0:T(8,128)(2,1)} %collective-permute-done.refs_1_, ...), custom_call_target="tpu_custom_call" | custom-call | tf_op jit(solution)/shard_map/pallas_call | solution.py:43
  66.1 7.9 %all_to_all.36.parts_ref = bf16[8,16,224]{2,1,0:T(8,128)(2,1)S(1)} all-to-all(bf16[8,16,224]{2,1,0:T(8,128)(2,1)S(1)} %bitcast.28), channel_id=1, replica_groups=mesh['role'=2,'x'=4,'zh'=4,'zl'=4,'tp'=4] {'role','tp'}, dimensions={0} | all-to-all | bytes 114688 | tf_op jit(solution)/shard_map/all_to_all | solution.py:299
  73.9 0.7 shard_map.121
  74.6 13.8 %all-to-all-start.3 = ((bf16[16,16,224]{2,1,0:T(8,128)(2,1)}), bf16[16,16,224]{2,1,0:T(8,128)(2,1)S(1)}, u32[]{:S(2)}, u32[]{:S(2)}) async-start(bf16[16,16,224]{2,1,0:T(8,128)(2,1)} %shard_map.121), calls=%async_computation.3 | async-start | bytes 262144 | tf_op jit(solution)/shard_map/all_to_all | solution.py:303
  88.4 0.8 dynamic-slice_bitcast_fusion.1.routed_ref
  89.1 0.8 dynamic-slice_bitcast_fusion.weight_ref
  89.9 0.9 shard_map.122
  90.8 11.5 %all-to-all-done.3.parts_ref = bf16[16,16,224]{2,1,0:T(8,128)(2,1)S(1)} async-done(((bf16[16,16,224]{2,1,0:T(8,128)(2,1)}), bf16[16,16,224]{2,1,0:T(8,128)(2,1)S(1)}, u32[]{:S(2)}, u32[]{:S(2)}) %all-to-all-start.3) | async-done | bytes 114720 | tf_op jit(solution)/shard_map/all_to_all | solution.py:303
  102.3 0.8 shard_map.123
  103.1 0.0 copy-start.3
  103.1 0.8 copy-done.3
  103.9 0.0 copy-start.6
  103.9 0.6 copy-done.6
  104.5 5.7 %all-to-all-start.4 = ((bf16[16,16,896]{2,1,0:T(8,128)(2,1)}), bf16[16,16,896]{2,1,0:T(8,128)(2,1)S(1)}, u32[]{:S(2)}, u32[]{:S(2)}) async-start(bf16[16,16,896]{2,1,0:T(8,128)(2,1)} %copy-done.3), calls=%async_computation.4 | async-start | bytes 917504 | tf_op jit(solution)/shard_map/all_to_all | solution.py:312
  110.2 0.0 copy-done.10
  110.2 0.7 reshape.33
  110.9 1.4 copy.15
  112.3 0.9 reshape.34.gain_ref
  113.1 0.0 collective-permute-done.4.peer_down_ref
  113.1 0.0 collective-permute-done.3.peer_in_ref
  113.1 6.8 %all-to-all-done.4.arrived_ref = bf16[16,16,896]{2,1,0:T(8,128)(2,1)S(1)} async-done(((bf16[16,16,896]{2,1,0:T(8,128)(2,1)}), bf16[16,16,896]{2,1,0:T(8,128)(2,1)S(1)}, u32[]{:S(2)}, u32[]{:S(2)}) %all-to-all-start.4) | async-done | bytes 458784 | tf_op jit(solution)/shard_map/all_to_all | solution.py:312
  119.9 0.0 copy-start.7
  119.9 3.0 %shard_map.124 = bf16[16,16,896]{2,1,0:T(8,128)(2,1)S(1)} custom-call(bf16[16,16,896]{2,1,0:T(8,128)(2,1)S(1)} %all-to-all-done.4.arrived_ref, f32[4,1,896]{2,1,0:T(1,128)S(1)} %reshape.34.gain_ref, bf16[4,896,256]{2,1,0:T(8,128)(2,1)S(1)} %bitcast.20, bf16[4,896,256]{2,1,0:T(8,128)(2,1)} %collective-permute-done.3.peer_in_ref, ...), custom_call_target="tpu_custom_call" | custom-call | tf_op jit(solution)/shard_map/pallas_call | solution.py:43
  122.9 13.0 %all_to_all.37.parts_ref = bf16[16,16,896]{2,1,0:T(8,128)(2,1)S(1)} all-to-all(bf16[16,16,896]{2,1,0:T(8,128)(2,1)S(1)} %shard_map.124), channel_id=1, replica_groups=mesh['role'=2,'x'=4,'zh'=4,'zl'=4,'tp'=4] {'x','tp'}, dimensions={0} | all-to-all | bytes 917504 | tf_op jit(solution)/shard_map/all_to_all | solution.py:323
  135.9 0.2 shard_map.125
  136.1 18.3 %all_to_all.38 = bf16[16,32,128]{2,1,0:T(8,128)(2,1)S(1)} all-to-all(bf16[16,32,128]{2,1,0:T(8,128)(2,1)S(1)} %shard_map.125), channel_id=1, replica_groups=mesh['role'=2,'x'=4,'zh'=4,'zl'=4,'tp'=4] {'zh','zl'}, dimensions={0} | all-to-all | bytes 262144 | tf_op jit(solution)/shard_map/all_to_all | solution.py:325
  154.4 0.0 copy-done.7
  154.4 0.9 shard_map.126
  (1 shorter events, 0.0 us)
Async XLA Ops:
  0.0 27.3 %copy-start = (bf16[56,512]{1,0:T(8,128)(2,1)S(1)}, bf16[56,512]{1,0:T(8,128)(2,1)}, u32[]{:S(2)}) copy-start(bf16[56,512]{1,0:T(8,128)(2,1)} %param.17) | copy-start | bytes 172036
  0.7 1.0 copy-start.4
  1.7 0.9 copy-start.5
  12.7 1.2 copy-start.1
  13.9 9.5 %copy-start.8 = (bf16[1,3584,128]{2,1,0:T(8,128)(2,1)S(1)}, bf16[1,3584,128]{2,1,0:T(8,128)(2,1)}, u32[]{:S(2)}) copy-start(bf16[1,3584,128]{2,1,0:T(8,128)(2,1)} %param.22) | copy-start | bytes 2752516
  14.9 49.6 %all-to-all-start.1 = ((bf16[16,8,1024]{2,1,0:T(8,128)(2,1)}), bf16[16,8,1024]{2,1,0:T(8,128)(2,1)S(1)}, u32[]{:S(2)}, u32[]{:S(2)}) async-start(bf16[16,8,1024]{2,1,0:T(8,128)(2,1)} %shard_map.119), calls=%async_computation.1 | async-start | bytes 524288 | tf_op jit(solution)/shard_map/all_to_all | solution.py:289
  25.0 2.4 %copy-start.9 = (bf16[56,1024]{1,0:T(8,128)(2,1)S(1)}, bf16[56,1024]{1,0:T(8,128)(2,1)}, u32[]{:S(2)}) copy-start(bf16[56,1024]{1,0:T(8,128)(2,1)} %param.16) | copy-start | bytes 344068
  25.0 25.3 %copy-start.2 = (bf16[1,128,3584]{2,1,0:T(8,128)(2,1)S(1)}, bf16[1,128,3584]{2,1,0:T(8,128)(2,1)}, u32[]{:S(2)}) copy-start(bf16[1,128,3584]{2,1,0:T(8,128)(2,1)} %param.23) | copy-start | bytes 2752516
  25.2 84.9 %copy-start.10 = (f32[3584]{0:T(1024)S(1)}, f32[3584]{0:T(1024)}, u32[]{:S(2)}) copy-start(f32[3584]{0:T(1024)} %param.18) | copy-start | bytes 43012
  25.2 87.9 %collective-permute-start.3 = (bf16[4,896,256]{2,1,0:T(8,128)(2,1)S(1)}, bf16[4,896,256]{2,1,0:T(8,128)(2,1)}, u32[]{:S(2)}, u32[]{:S(2)}) collective-permute-start(bf16[4,896,256]{2,1,0:T(8,128)(2,1)S(1)} %bitcast.19), channel_id=1, source_target_pairs={{0,256},{256,0},{1,257},{257,1},{2,258},{258,2},{3,259},{259,3},{4... | collective-permute-start | bytes 5505032 | tf_op jit(solution)/shard_map/ppermute | solution.py:262
  27.5 25.6 %collective-permute-start.2 = (bf16[56,1152]{1,0:T(8,128)(2,1)S(1)}, bf16[56,1152]{1,0:T(8,128)(2,1)S(1)}, u32[]{:S(2)}, u32[]{:S(2)}) collective-permute-start(bf16[56,1152]{1,0:T(8,128)(2,1)S(1)} %concatenate.11.refs_0_), channel_id=1, source_target_pairs={{0,48},{16,0},{32,16},{48,32},{1,49},{17,1},{33,17},{49,33},{2,50}... | collective-permute-start | bytes 387080 | tf_op jit(solution)/shard_map/ppermute | solution.py:253
  37.6 26.9 %collective-permute-start.1 = (bf16[56,1152]{1,0:T(8,128)(2,1)S(1)}, bf16[56,1152]{1,0:T(8,128)(2,1)S(1)}, u32[]{:S(2)}, u32[]{:S(2)}) collective-permute-start(bf16[56,1152]{1,0:T(8,128)(2,1)S(1)} %concatenate.11.refs_0_), channel_id=1, source_target_pairs={{0,32},{16,48},{32,0},{48,16},{1,33},{17,49},{33,1},{49,17},{2,34}... | collective-permute-start | bytes 387080 | tf_op jit(solution)/shard_map/ppermute | solution.py:253
  43.9 20.6 %collective-permute-start = (bf16[56,1152]{1,0:T(8,128)(2,1)S(1)}, bf16[56,1152]{1,0:T(8,128)(2,1)}, u32[]{:S(2)}, u32[]{:S(2)}) collective-permute-start(bf16[56,1152]{1,0:T(8,128)(2,1)S(1)} %concatenate.11.refs_0_), channel_id=1, source_target_pairs={{0,16},{16,32},{32,48},{48,0},{1,17},{17,33},{33,49},{49,1},{2,18}... | collective-permute-start | bytes 387080 | tf_op jit(solution)/shard_map/ppermute | solution.py:253
  50.3 62.8 %collective-permute-start.4 = (bf16[128,3584]{1,0:T(8,128)(2,1)S(1)}, bf16[128,3584]{1,0:T(8,128)(2,1)}, u32[]{:S(2)}, u32[]{:S(2)}) collective-permute-start(bf16[128,3584]{1,0:T(8,128)(2,1)S(1)} %bitcast.22), channel_id=1, source_target_pairs={{0,256},{256,0},{1,257},{257,1},{2,258},{258,2},{3,259},{259,3},{4... | collective-permute-start | bytes 2752520 | tf_op jit(solution)/shard_map/ppermute | solution.py:263
  74.6 27.7 %all-to-all-start.3 = ((bf16[16,16,224]{2,1,0:T(8,128)(2,1)}), bf16[16,16,224]{2,1,0:T(8,128)(2,1)S(1)}, u32[]{:S(2)}, u32[]{:S(2)}) async-start(bf16[16,16,224]{2,1,0:T(8,128)(2,1)} %shard_map.121), calls=%async_computation.3 | async-start | bytes 262144 | tf_op jit(solution)/shard_map/all_to_all | solution.py:303
  103.1 0.8 copy-start.3
  103.9 0.6 copy-start.6
  104.5 15.4 %all-to-all-start.4 = ((bf16[16,16,896]{2,1,0:T(8,128)(2,1)}), bf16[16,16,896]{2,1,0:T(8,128)(2,1)S(1)}, u32[]{:S(2)}, u32[]{:S(2)}) async-start(bf16[16,16,896]{2,1,0:T(8,128)(2,1)} %copy-done.3), calls=%async_computation.4 | async-start | bytes 917504 | tf_op jit(solution)/shard_map/all_to_all | solution.py:312
  119.9 34.5 %copy-start.7 = (f32[56,64]{1,0:T(8,128)S(1)}, f32[56,64]{1,0:T(8,128)}, u32[]{:S(2)}) copy-start(f32[56,64]{1,0:T(8,128)} %copy-done.6) | copy-start | bytes 43012

commit v3 on v2

v3 whole, which is shorter than its diff:
```python
import jax
import jax.numpy as jnp
from jax import lax
from jax.experimental import pallas as pl
from jax.experimental.pallas import tpu as pltpu
from jax.sharding import Mesh
from jax.sharding import PartitionSpec as P

LAT = 512
SOFTMAX_SCALE = 192.0 ** (-0.5)
NORM_EPS = 1e-06

ROLE, X, Z, TP = 2, 4, 16, 4
MEMBERS = ROLE * TP
ROWBLK = 64
MOST = 16
EXPERTS = 64
COLS = 56
WIDTH = 3584
PLANE = Z * COLS
HALF = 64
PAYLOAD = 2432

F32 = jnp.float32
BF16 = jnp.bfloat16
VMEM_LIMIT = 48 * 1024 * 1024


def nt_dot(a, b):
    return lax.dot_general(a, b, (((1,), (1,)), ((), ())), preferred_element_type=F32)


def nn_dot(a, b):
    return lax.dot_general(a, b, (((1,), (0,)), ((), ())), preferred_element_type=F32)


def local_call(body, out_shape, *args, scratch=(), smem=()):
    specs = [
        pl.BlockSpec(memory_space=pltpu.SMEM if i in smem else pltpu.VMEM)
        for i in range(len(args))
    ]
    return pl.pallas_call(
        body,
        out_shape=out_shape,
        in_specs=specs,
        out_specs=jax.tree.map(lambda _: pl.BlockSpec(memory_space=pltpu.VMEM), out_shape),
        scratch_shapes=list(scratch),
        compiler_params=pltpu.CompilerParams(vmem_limit_bytes=VMEM_LIMIT),
    )(*args)


def shape(dims, dtype=BF16):
    return jax.ShapeDtypeStruct(dims, dtype)


def attend_kernel(length_ref, query_ref, cache_ref, out_ref):
    cache = cache_ref[0]
    scores = nn_dot(query_ref[0], cache) * SOFTMAX_SCALE
    visible = lax.broadcasted_iota(jnp.int32, scores.shape, 1) < length_ref[0]
    scores = jnp.where(visible, scores, -1e30)
    row_max = jnp.max(scores, axis=1, keepdims=True)
    weights = jnp.where(visible, jnp.exp(scores - row_max), 0.0)
    row_total = jnp.sum(weights, axis=1, keepdims=True)
    summed = nt_dot(weights.astype(BF16), cache[:LAT])
    out_ref[...] = (summed / row_total).astype(BF16)


def value_kernel(att_ref, value_ref, out_ref):
    heads = value_ref.shape[0]
    att = att_ref[...]
    rows = att.shape[0]
    row_head = lax.broadcasted_iota(jnp.int32, (rows, 128), 0) % heads
    for head in range(heads):
        product = nn_dot(att, value_ref[head])
        kept = jnp.where(row_head == head, product, 0.0)
        value = jnp.sum(kept.reshape(rows // heads, heads, 128), axis=1).astype(BF16)
        out_ref[:, :, head * 128 : (head + 1) * 128] = jnp.broadcast_to(
            value[None], (out_ref.shape[0],) + value.shape
        )


def packed(tile):
    gap = jnp.zeros((ROWBLK // 2, HALF - COLS), F32)
    return jnp.concatenate([tile[: ROWBLK // 2], gap, tile[ROWBLK // 2 :], gap], axis=1)


def project_kernel(place_ref, values_ref, payload_ref, out_ref, residual_ref):
    rows, depth = values_ref.shape
    place = lax.broadcasted_iota(jnp.int32, (rows, rows), 0)
    source = lax.broadcasted_iota(jnp.int32, (rows, rows), 1)
    lane = place % TP
    z = (place // TP) % Z
    role = place // (TP * Z)
    order = (source == z * MEMBERS + role * TP + lane).astype(F32).astype(BF16)
    values = nn_dot(order, values_ref[...]).astype(BF16)
    for x in range(X):
        product = nt_dot(values, payload_ref[x, :, :depth])
        for role in range(ROLE):
            tile = packed(product[role * ROWBLK : (role + 1) * ROWBLK])
            out_ref[role * X + x] = tile.astype(BF16)
    columns = payload_ref[place_ref[3], :, depth : depth + ROWBLK * MEMBERS]
    token = lax.broadcasted_iota(jnp.int32, (ROWBLK, ROWBLK * MEMBERS), 0)
    request = lax.broadcasted_iota(jnp.int32, (ROWBLK, ROWBLK * MEMBERS), 1)
    mine = request == token + (place_ref[2] * X + place_ref[0]) * ROWBLK
    residual_ref[...] = packed(nt_dot(mine.astype(F32).astype(BF16), columns))


def hidden_kernel(parts_ref, residual_ref, out_ref, own_ref):
    total = jnp.sum(parts_ref[...].astype(F32), axis=0)
    total = (residual_ref[...] + total).astype(BF16)
    own_ref[...] = total
    out_ref[...] = jnp.broadcast_to(total[None], out_ref.shape)


def route_kernel(
    place_ref, sent_ref, routed_ref, weight_ref, pick_ref, high_ref, low_ref, weights_ref, rank_ref
):
    dims = (EXPERTS, ROWBLK)
    expert_ids = lax.broadcasted_iota(jnp.int32, dims, 0)
    earlier = lax.broadcasted_iota(jnp.int32, (ROWBLK, ROWBLK), 0) < lax.broadcasted_iota(
        jnp.int32, (ROWBLK, ROWBLK), 1
    )
    before = jnp.where(earlier, 1.0, 0.0).astype(BF16)
    slots = lax.broadcasted_iota(jnp.int32, (MOST, ROWBLK), 0).astype(F32)

    def ranks(ids_ref):
        named = jnp.zeros(dims, F32)
        weights = jnp.zeros(dims, F32)
        for k in range(ids_ref.shape[0]):
            chosen = expert_ids == ids_ref[k : k + 1, :]
            named = named + jnp.where(chosen, 1.0, 0.0)
            weights = weights + jnp.where(chosen, weight_ref[k : k + 1, :], 0.0)
        rank = nn_dot(named.astype(BF16), before)
        return jnp.where(named > 0.5, rank, -1.0), weights

    rank_ref[...], _ = ranks(sent_ref)
    for x in range(X):
        row = rank_ref[pl.ds(x * Z + place_ref[1], 1), :]
        pick_ref[x * MOST : (x + 1) * MOST, :] = jnp.where(row == slots, 1.0, 0.0).astype(BF16)
    rank_ref[...], weights_ref[...] = ranks(routed_ref)
    for half in range(2):
        for z in range(Z):
            for pair in range(2):
                expert = (half * 2 + pair) * Z + z
                hit = rank_ref[expert : expert + 1, :] == slots
                table = jnp.where(hit, weights_ref[expert : expert + 1, :], 0.0)
                high = table.astype(BF16)
                low = (table - high.astype(F32)).astype(BF16)
                rows = pl.ds(z * 32 + pair * MOST, MOST)
                lanes = pl.ds(half * HALF, ROWBLK)
                high_ref[rows, lanes] = high
                low_ref[rows, lanes] = low


def dispatch_kernel(parts_ref, pick_ref, out_ref):
    parts = [parts_ref[z].astype(F32) for z in range(Z)]
    hidden = jnp.concatenate(
        [
            jnp.concatenate([part[:, start : start + COLS] for part in parts], axis=1)
            for start in (0, HALF)
        ],
        axis=0,
    ).astype(BF16)
    rows = nn_dot(pick_ref[...], hidden).astype(BF16)
    for x in range(X):
        piece = rows[x * MOST : (x + 1) * MOST]
        for lane in range(TP):
            out_ref[x * TP + lane] = piece


def expert_kernel(
    arrived_ref, gain_ref, own_in_ref, peer_in_ref, own_down_ref, peer_down_ref, out_ref
):
    rows = X * MOST
    values = []
    total = jnp.zeros((rows, 1), F32)
    for lane in range(TP):
        value = jnp.concatenate([arrived_ref[x * TP + lane] for x in range(X)], axis=0).astype(F32)
        total = total + jnp.sum(value * value, axis=1, keepdims=True)
        values.append(value)
    inverse = lax.rsqrt(total / WIDTH + NORM_EPS)
    own = jnp.zeros((rows, 256), F32)
    peer = jnp.zeros((rows, 256), F32)
    for i, value in enumerate(values):
        normed = (value * inverse * gain_ref[i]).astype(BF16)
        own = own + nn_dot(normed, own_in_ref[i])
        peer = peer + nn_dot(normed, peer_in_ref[i])

    def activate(both):
        gate, up = both[:, :128], both[:, 128:]
        return (gate / (1.0 + jnp.exp(-gate)) * up).astype(BF16)

    own_act, peer_act = activate(own), activate(peer)
    for x in range(X):
        lanes = pl.ds(x * PLANE, PLANE)
        product = nn_dot(own_act, own_down_ref[:, lanes]) + nn_dot(
            peer_act, peer_down_ref[:, lanes]
        )
        product = product.astype(BF16)
        for lane in range(TP):
            out_ref[x * TP + lane] = product[lane * MOST : (lane + 1) * MOST]


def columns_kernel(parts_ref, out_ref):
    summed = []
    for x in range(X):
        total = parts_ref[x * TP].astype(F32)
        for lane in range(1, TP):
            total = total + parts_ref[x * TP + lane].astype(F32)
        summed.append(total)
    low = jnp.concatenate(summed[:2], axis=0)
    high = jnp.concatenate(summed[2:], axis=0)
    gap = jnp.zeros((32, HALF - COLS), F32)
    for z in range(Z):
        cut = slice(z * COLS, (z + 1) * COLS)
        out_ref[z] = jnp.concatenate([low[:, cut], gap, high[:, cut], gap], axis=1).astype(BF16)


def combine_kernel(returned_ref, high_ref, low_ref, own_ref, out_ref):
    returned = returned_ref[...]
    dims = (((0,), (0,)), ((), ()))
    mixed = lax.dot_general(returned, high_ref[...], dims, preferred_element_type=F32)
    mixed = mixed + lax.dot_general(returned, low_ref[...], dims, preferred_element_type=F32)
    mixture = mixed[:COLS, :ROWBLK] + mixed[HALF : HALF + COLS, HALF : HALF + ROWBLK]
    column = lax.broadcasted_iota(jnp.int32, (COLS, 2 * HALF), 0)
    place = lax.broadcasted_iota(jnp.int32, (COLS, 2 * HALF), 1)
    own = own_ref[...]
    hidden = [
        nt_dot((place == column + start).astype(F32).astype(BF16), own) for start in (0, HALF)
    ]
    out_ref[...] = (jnp.concatenate(hidden, axis=1) + mixture).astype(BF16)


def shards(
    queries,
    latent_cache,
    lengths,
    value_up,
    output_weight,
    residual,
    norm_gain,
    routed_experts,
    route_weights,
    gate_weight,
    up_weight,
    down_weight,
):
    swap = [(0, 1), (1, 0)]
    role, x, z, lane = (lax.axis_index(name) for name in ("role", "x", "z", "tp"))
    place = jnp.stack([x, z, role, lane]).astype(jnp.int32)

    depth = output_weight.shape[1]
    payload = jnp.concatenate(
        [output_weight, residual, jnp.zeros((COLS, PAYLOAD - depth - residual.shape[1]), BF16)],
        axis=1,
    )
    payload = lax.all_gather(payload, "x", axis=0, tiled=True).reshape(X, COLS, PAYLOAD)
    gain_rows = norm_gain.reshape(TP, 1, PLANE)
    own_in = jnp.concatenate([gate_weight[0], up_weight[0]], axis=1).reshape(TP, PLANE, 256)
    own_down = down_weight[0]
    peer_in = lax.ppermute(own_in, "role", swap)
    peer_down = lax.ppermute(own_down, "role", swap)
    sent = lax.dynamic_slice_in_dim(routed_experts, (role * X + x) * ROWBLK, ROWBLK, 0).T
    block = (role * TP + lane) * ROWBLK
    routed = lax.dynamic_slice_in_dim(routed_experts, block, ROWBLK, 0).T
    weights = lax.dynamic_slice_in_dim(route_weights, block, ROWBLK, 0).T
    pick, high, low = local_call(
        route_kernel,
        (shape((X * MOST, ROWBLK)), shape((Z * 32, 128)), shape((Z * 32, 128))),
        place,
        sent,
        routed,
        weights,
        scratch=(pltpu.VMEM((EXPERTS, ROWBLK), F32), pltpu.VMEM((EXPERTS, ROWBLK), F32)),
        smem=(0,),
    )

    heads = queries.shape[1]
    own_heads = heads // MEMBERS
    attended = local_call(
        attend_kernel, shape((heads, LAT)), lengths, queries, latent_cache.swapaxes(1, 2), smem=(0,)
    )
    attended = attended.reshape(MEMBERS, own_heads, LAT)
    regrouped = lax.all_to_all(attended, ("role", "tp"), 0, 0, tiled=True)
    values = local_call(
        value_kernel,
        shape((Z, MEMBERS, own_heads * 128)),
        regrouped.reshape(MEMBERS * own_heads, LAT),
        value_up,
    )
    gathered = lax.all_to_all(values, "z", 0, 0, tiled=True)
    projected, residual_tile = local_call(
        project_kernel,
        (shape((MEMBERS, 32, 128)), shape((32, 128), F32)),
        place,
        gathered.reshape(Z * MEMBERS, own_heads * 128),
        payload,
        smem=(0,),
    )
    head_parts = lax.all_to_all(projected, ("role", "tp"), 0, 0, tiled=True)
    hidden, own = local_call(
        hidden_kernel, (shape((Z, 32, 128)), shape((32, 128))), head_parts, residual_tile
    )
    own = lax.ppermute(
        own, ("x", "tp"), [(a * TP + b, b * TP + a) for a in range(X) for b in range(TP)]
    )
    hidden = lax.all_to_all(hidden, "z", 0, 0, tiled=True)
    outbound = local_call(dispatch_kernel, shape((X * TP, MOST, PLANE)), hidden, pick)
    arrived = lax.all_to_all(outbound, ("x", "tp"), 0, 0, tiled=True)
    partial = local_call(
        expert_kernel,
        shape((X * TP, MOST, PLANE)),
        arrived,
        gain_rows,
        own_in,
        peer_in,
        own_down,
        peer_down,
    )
    hidden_parts = lax.all_to_all(partial, ("x", "tp"), 0, 0, tiled=True)
    columns = local_call(columns_kernel, shape((Z, 32, 128)), hidden_parts)
    returned = lax.all_to_all(columns, "z", 0, 0, tiled=True)
    return local_call(
        combine_kernel,
        shape((COLS, ROWBLK)),
        returned.reshape(Z * 32, 128),
        high,
        low,
        own,
    )


def solution(mesh):
    grp = ("x", "z")
    fine = Mesh(mesh.devices.reshape(ROLE, X, Z, TP), ("role", "x", "z", "tp"))
    return jax.shard_map(
        shards,
        mesh=fine,
        in_specs=(
            P(("role",) + grp + ("tp",), None, None),
            P(("role",) + grp + ("tp",), None, None),
            P(("role",) + grp + ("tp",)),
            P(("role", "tp"), None, None),
            P(grp, ("role", "tp")),
            P(grp, None),
            P(),
            P(),
            P(),
            P(grp, None, ("role", "tp")),
            P(grp, None, ("role", "tp")),
            P(grp, ("role", "tp"), None),
        ),
        out_specs=P(grp, ("role", "tp")),
        check_vma=False,
    )
```

time: 156 us -> 146 us (0.936)
  blocking collectives: 48.8 us -> 30.4 us
  starting transfers between devices: 54.7 us -> 36.9 us
  waiting for transfers between devices: 30.4 us -> 47.2 us
  between operations: 0.89 us -> 14.2 us
  local copies, waits for them, and re-layouts: 9.36 us -> 3.34 us
  other arithmetic: 1.64 us -> 3.6 us
    all_to_all x2 -> x3, waiting for transfers between devices: 11.5 us -> 37.4 us  [the longest x1 14.5 us: shards(): gathered = lax.all_to_all(values, 'z', 0, 0, tiled=True)]
    ppermute x3 -> x1, starting transfers between devices: 22.8 us -> 0.65 us  [shards(): lax.ppermute(own, ('x', 'tp'), [(a * TP + b, b * TP + a) for a in range(X...]
    all_to_all x2 -> x1, blocking collectives: 26.1 us -> 7.73 us  [shards(): head_parts = lax.all_to_all(projected, ('role', 'tp'), 0, 0, tiled=True)]
    ppermute x3 -> x1, waiting for transfers between devices: 12.2 us -> 0.01 us  [shards(): lax.ppermute(own, ('x', 'tp'), [(a * TP + b, b * TP + a) for a in range(X...]
    all_to_all x2 -> x3, starting transfers between devices: 22.3 us -> 27.1 us  [the longest x1 15.2 us: shards(): gathered = lax.all_to_all(values, 'z', 0, 0, tiled=True)]
    all_to_all x1, waiting for transfers between devices: 6.76 us -> 9.69 us  [shards(): arrived = lax.all_to_all(outbound, ('x', 'tp'), 0, 0, tiled=True)]
    transpose x3 -> x2, local copies, waits for them, and re-layouts: 2.89 us -> 0.15 us  [the longest x1 0.08 us: shards(): weights = lax.dynamic_slice_in_dim(route_weights, block, ROWBLK, 0).T]
    concatenate x1 -> x2, other arithmetic: 1.57 us -> 3.53 us  [the longest x1 1.76 us: shards(): jnp.concatenate([output_weight, residual, jnp.zeros((COLS, PAYLOAD - dept...]
  transfers between devices with their start and end apart: 8 -> 8, of which waited for: 4 -> 4; matrix products, arithmetic and copies ran while one was open for 4% -> 1% of each run, Pallas kernels for 3% -> 4%
where the time goes in v3:
time: 146 us
  waiting for transfers between devices  47.2 us (32%)
  starting transfers between devices  36.9 us (25%)
  blocking collectives  30.4 us (21%)
  between operations  14.2 us (10%)
  Pallas kernels  10.1 us (7%)
  other arithmetic  3.6 us (2%)
  local copies, waits for them, and re-layouts  3.34 us (2%)
    all_to_all x1, starting transfers between devices, shards(): gathered = lax.all_to_all(values, 'z', 0, 0, tiled=True)  15.2 us
    all_to_all x1, waiting for transfers between devices, shards(): gathered = lax.all_to_all(values, 'z', 0, 0, tiled=True)  14.5 us
    all_to_all x1, blocking collectives, shards(): hidden_parts = lax.all_to_all(partial, ('x', 'tp'), 0, 0, tiled=True)  13 us
    all_to_all x1, waiting for transfers between devices, shards(): returned = lax.all_to_all(columns, 'z', 0, 0, tiled=True)  12.1 us
    all_to_all x1, waiting for transfers between devices, shards(): hidden = lax.all_to_all(hidden, 'z', 0, 0, tiled=True)  10.9 us
    pallas_call x9, Pallas kernels, local_call(): pl.pallas_call(body, out_shape=out_shape, in_specs=specs, out_specs=jax.t...  10.1 us
    all_to_all x1, waiting for transfers between devices, shards(): arrived = lax.all_to_all(outbound, ('x', 'tp'), 0, 0, tiled=True)  9.69 us
    all_to_all x1, blocking collectives, shards(): regrouped = lax.all_to_all(attended, ('role', 'tp'), 0, 0, tiled=True)  9.63 us
  transfers between devices with their start and end apart: 8, of which 4 were waited for; matrix products, arithmetic and copies ran while one was open for 1% of the time, Pallas kernels for 4%

profile of v3, /device:TPU:32, one launch (start us, length us, event | category | flops | bytes accessed | tf_op | source)
XLA Modules:
  0.0 145.6 jit_solution(13529558254155877285)
XLA Ops:
  6.5 0.0 copy-start
  6.5 0.0 copy-start.2
  6.5 0.0 all-gather.2.cloned.1.call-start
  6.6 1.8 %maximum_maximum_fusion = bf16[56,2432]{1,0:T(8,128)(2,1)} fusion(bf16[56,512]{1,0:T(8,128)(2,1)} %param.17, bf16[56,1024]{1,0:T(8,128)(2,1)} %param.16, bf16[2432]{0:T(1024)(128)(2,1)S(1)} %pad.4.clone), kind=kLoop, calls=%fused_computation.1 | loop fusion | flops 817152 | bytes 449280 | tf_op jit(solution)/shard_map/concatenate | solution.py:253
  8.3 0.0 all-gather.2.cloned.1.call-update
  9.0 0.0 copy-start.4
  9.0 1.0 copy-done.4
  10.0 0.0 copy-start.5
  10.0 0.9 copy-done.5
  10.9 0.5 shard_map.118
  11.4 9.6 %all_to_all.35 = bf16[8,8,512]{2,1,0:T(8,128)(2,1)S(1)} all-to-all(bf16[8,8,512]{2,1,0:T(8,128)(2,1)S(1)} %bitcast.25), channel_id=1, replica_groups=mesh['role'=2,'x'=4,'z'=16,'tp'=4] {'role','tp'}, dimensions={0} | all-to-all | bytes 131072 | tf_op jit(solution)/shard_map/all_to_all | solution.py:284
  21.0 0.0 copy-done.2
  21.0 1.0 shard_map.119
  22.0 15.2 %all-to-all-start.1 = ((bf16[16,8,1024]{2,1,0:T(8,128)(2,1)}), bf16[16,8,1024]{2,1,0:T(8,128)(2,1)S(1)}, u32[]{:S(2)}, u32[]{:S(2)}) async-start(bf16[16,8,1024]{2,1,0:T(8,128)(2,1)} %shard_map.119), calls=%async_computation.1 | async-start | bytes 524288 | tf_op jit(solution)/shard_map/all_to_all | solution.py:291
  37.2 0.0 copy-start.3
  37.3 1.8 %pad_maximum_fusion.own_in_ref = bf16[4,896,256]{2,1,0:T(8,128)(2,1)S(1)} fusion(bf16[4,896,128]{2,1,0:T(8,128)(2,1)} %bitcast.27, bf16[4,896,128]{2,1,0:T(8,128)(2,1)} %bitcast.28), kind=kLoop, calls=%fused_computation | loop fusion | flops 3670016 | bytes 3670016 | tf_op jit(solution)/shard_map/concatenate | solution.py:259
  39.0 0.0 copy-start.7
  39.0 0.0 copy-start.6
  39.0 1.9 %collective-permute-start = (bf16[4,896,256]{2,1,0:T(8,128)(2,1)S(1)}, bf16[4,896,256]{2,1,0:T(8,128)(2,1)}, u32[]{:S(2)}, u32[]{:S(2)}) collective-permute-start(bf16[4,896,256]{2,1,0:T(8,128)(2,1)S(1)} %pad_maximum_fusion.own_in_ref), channel_id=1, source_target_pairs={{0,256},{256,0},{1,257},{257,1},{2,258},{258,2},{3,259},{259,3},{4... | collective-permute-start | bytes 5505032 | tf_op jit(solution)/shard_map/ppermute | solution.py:261
  41.0 0.1 pad_add_fusion.place_ref
  41.1 14.5 %all-to-all-done.1 = bf16[16,8,1024]{2,1,0:T(8,128)(2,1)S(1)} async-done(((bf16[16,8,1024]{2,1,0:T(8,128)(2,1)}), bf16[16,8,1024]{2,1,0:T(8,128)(2,1)S(1)}, u32[]{:S(2)}, u32[]{:S(2)}) %all-to-all-start.1) | async-done | bytes 262176 | tf_op jit(solution)/shard_map/all_to_all | solution.py:291
  55.6 0.0 all-gather.2.cloned.1.call-done
  55.6 0.0 copy-start.1
  55.6 1.2 copy-done.1
  56.8 1.2 shard_map.120
  58.0 7.7 %all_to_all.36.parts_ref = bf16[8,32,128]{2,1,0:T(8,128)(2,1)S(1)} all-to-all(bf16[8,32,128]{2,1,0:T(8,128)(2,1)S(1)} %get-tuple-element.12), channel_id=1, replica_groups=mesh['role'=2,'x'=4,'z'=16,'tp'=4] {'role','tp'}, dimensions={0} | all-to-all | bytes 131072 | tf_op jit(solution)/shard_map/all_to_all | solution.py:300
  65.7 0.7 shard_map.121
  66.4 6.1 %all-to-all-start.3 = ((bf16[16,32,128]{2,1,0:T(8,128)(2,1)}), bf16[16,32,128]{2,1,0:T(8,128)(2,1)S(1)}, u32[]{:S(2)}, u32[]{:S(2)}) async-start(bf16[16,32,128]{2,1,0:T(8,128)(2,1)} %get-tuple-element.14), calls=%async_computation.3 | async-start | bytes 262144 | tf_op jit(solution)/shard_map/all_to_all | solution.py:307
  72.5 0.0 copy-done.3
  72.5 1.9 %collective-permute-start.1 = (bf16[128,3584]{1,0:T(8,128)(2,1)S(1)}, bf16[128,3584]{1,0:T(8,128)(2,1)}, u32[]{:S(2)}, u32[]{:S(2)}) collective-permute-start(bf16[128,3584]{1,0:T(8,128)(2,1)S(1)} %bitcast.21), channel_id=1, source_target_pairs={{0,256},{256,0},{1,257},{257,1},{2,258},{258,2},{3,259},{259,3},{4... | collective-permute-start | bytes 2752520 | tf_op jit(solution)/shard_map/ppermute | solution.py:262
  74.4 0.0 copy-done
  74.5 0.1 dynamic-slice_bitcast_fusion.weight_ref
  74.5 0.0 copy-done.7
  74.5 0.1 dynamic-slice_bitcast_fusion.1
  74.6 0.9 shard_map.122
  75.6 10.9 %all-to-all-done.3.parts_ref = bf16[16,32,128]{2,1,0:T(8,128)(2,1)S(1)} async-done(((bf16[16,32,128]{2,1,0:T(8,128)(2,1)}), bf16[16,32,128]{2,1,0:T(8,128)(2,1)S(1)}, u32[]{:S(2)}, u32[]{:S(2)}) %all-to-all-start.3) | async-done | bytes 131104 | tf_op jit(solution)/shard_map/all_to_all | solution.py:307
  86.4 1.0 shard_map.123
  87.5 5.3 %all-to-all-start.4 = ((bf16[16,16,896]{2,1,0:T(8,128)(2,1)}), bf16[16,16,896]{2,1,0:T(8,128)(2,1)S(1)}, u32[]{:S(2)}, u32[]{:S(2)}) async-start(bf16[16,16,896]{2,1,0:T(8,128)(2,1)} %shard_map.123), calls=%async_computation.4 | async-start | bytes 917504 | tf_op jit(solution)/shard_map/all_to_all | solution.py:309
  92.7 0.0 copy-done.6
  92.8 0.0 collective-permute-done.1.peer_down_ref
  92.8 0.0 collective-permute-done.peer_in_ref
  92.8 9.7 %all-to-all-done.4.arrived_ref = bf16[16,16,896]{2,1,0:T(8,128)(2,1)S(1)} async-done(((bf16[16,16,896]{2,1,0:T(8,128)(2,1)}), bf16[16,16,896]{2,1,0:T(8,128)(2,1)S(1)}, u32[]{:S(2)}, u32[]{:S(2)}) %all-to-all-start.4) | async-done | bytes 458784 | tf_op jit(solution)/shard_map/all_to_all | solution.py:309
  102.5 3.0 %shard_map.124 = bf16[16,16,896]{2,1,0:T(8,128)(2,1)S(1)} custom-call(bf16[16,16,896]{2,1,0:T(8,128)(2,1)S(1)} %all-to-all-done.4.arrived_ref, f32[4,1,896]{2,1,0:T(1,128)S(1)} %reshape.27.gain_ref, bf16[4,896,256]{2,1,0:T(8,128)(2,1)S(1)} %pad_maximum_fusion.own_in_ref, bf16[4,896,256]{2,1,0:T(8,128)(2,1)} %collective-permute-done.peer_in_ref, ...), custom_call_target="tpu_custom_call" | custom-call | tf_op jit(solution)/shard_map/pallas_call | solution.py:42
  105.5 13.0 %all_to_all.37.parts_ref = bf16[16,16,896]{2,1,0:T(8,128)(2,1)S(1)} all-to-all(bf16[16,16,896]{2,1,0:T(8,128)(2,1)S(1)} %shard_map.124), channel_id=1, replica_groups=mesh['role'=2,'x'=4,'z'=16,'tp'=4] {'x','tp'}, dimensions={0} | all-to-all | bytes 917504 | tf_op jit(solution)/shard_map/all_to_all | solution.py:320
  118.5 0.8 shard_map.125
  119.3 5.8 %all-to-all-start.6 = ((bf16[16,32,128]{2,1,0:T(8,128)(2,1)}), bf16[16,32,128]{2,1,0:T(8,128)(2,1)S(1)}, u32[]{:S(2)}, u32[]{:S(2)}) async-start(bf16[16,32,128]{2,1,0:T(8,128)(2,1)} %shard_map.125), calls=%async_computation.6 | async-start | bytes 262144 | tf_op jit(solution)/shard_map/all_to_all | solution.py:322
  125.1 0.6 collective-permute-start.2
  125.7 0.0 collective-permute-done.2.own_ref
  125.8 12.1 %all-to-all-done.6 = bf16[16,32,128]{2,1,0:T(8,128)(2,1)S(1)} async-done(((bf16[16,32,128]{2,1,0:T(8,128)(2,1)}), bf16[16,32,128]{2,1,0:T(8,128)(2,1)S(1)}, u32[]{:S(2)}, u32[]{:S(2)}) %all-to-all-start.6) | async-done | bytes 131104 | tf_op jit(solution)/shard_map/all_to_all | solution.py:322
  137.8 0.9 shard_map.126
  (3 shorter events, 0.0 us)
Async XLA Ops:
  6.5 67.9 %copy-start = (f32[512,8]{0,1:T(8,128)S(1)}, f32[512,8]{0,1:T(8,128)}, u32[]{:S(2)}) copy-start(f32[512,8]{0,1:T(8,128)} %param.20) | copy-start | bytes 49156
  6.5 14.5 %copy-start.2 = (bf16[8,512,128]{2,1,0:T(8,128)(2,1)S(1)}, bf16[8,512,128]{2,1,0:T(8,128)(2,1)}, u32[]{:S(2)}) copy-start(bf16[8,512,128]{2,1,0:T(8,128)(2,1)} %value_ref.1) | copy-start | bytes 3145732
  6.5 49.1 %all-gather.2.cloned.1.call-start = ((), (), s32[]{:S(2)}) async-start(), calls=%async_computation.7 | async-start | bytes 1361920 | tf_op jit(solution)/shard_map/all_gather | solution.py:257
  9.0 1.0 copy-start.4
  10.0 0.9 copy-start.5
  22.0 33.6 %all-to-all-start.1 = ((bf16[16,8,1024]{2,1,0:T(8,128)(2,1)}), bf16[16,8,1024]{2,1,0:T(8,128)(2,1)S(1)}, u32[]{:S(2)}, u32[]{:S(2)}) async-start(bf16[16,8,1024]{2,1,0:T(8,128)(2,1)} %shard_map.119), calls=%async_computation.1 | async-start | bytes 524288 | tf_op jit(solution)/shard_map/all_to_all | solution.py:291
  37.2 35.3 %copy-start.3 = (bf16[1,128,3584]{2,1,0:T(8,128)(2,1)S(1)}, bf16[1,128,3584]{2,1,0:T(8,128)(2,1)}, u32[]{:S(2)}) copy-start(bf16[1,128,3584]{2,1,0:T(8,128)(2,1)} %param.23) | copy-start | bytes 2752516
  39.0 35.5 %copy-start.7 = (s32[512,8]{0,1:T(8,128)S(1)}, s32[512,8]{0,1:T(8,128)}, u32[]{:S(2)}) copy-start(s32[512,8]{0,1:T(8,128)} %param.19) | copy-start | bytes 49156
  39.0 53.7 %copy-start.6 = (f32[3584]{0:T(1024)S(1)}, f32[3584]{0:T(1024)}, u32[]{:S(2)}) copy-start(f32[3584]{0:T(1024)} %param.18) | copy-start | bytes 43012
  39.0 53.7 %collective-permute-start = (bf16[4,896,256]{2,1,0:T(8,128)(2,1)S(1)}, bf16[4,896,256]{2,1,0:T(8,128)(2,1)}, u32[]{:S(2)}, u32[]{:S(2)}) collective-permute-start(bf16[4,896,256]{2,1,0:T(8,128)(2,1)S(1)} %pad_maximum_fusion.own_in_ref), channel_id=1, source_target_pairs={{0,256},{256,0},{1,257},{257,1},{2,258},{258,2},{3,259},{259,3},{4... | collective-permute-start | bytes 5505032 | tf_op jit(solution)/shard_map/ppermute | solution.py:261
  55.6 1.2 copy-start.1
  66.4 20.0 %all-to-all-start.3 = ((bf16[16,32,128]{2,1,0:T(8,128)(2,1)}), bf16[16,32,128]{2,1,0:T(8,128)(2,1)S(1)}, u32[]{:S(2)}, u32[]{:S(2)}) async-start(bf16[16,32,128]{2,1,0:T(8,128)(2,1)} %get-tuple-element.14), calls=%async_computation.3 | async-start | bytes 262144 | tf_op jit(solution)/shard_map/all_to_all | solution.py:307
  72.5 20.3 %collective-permute-start.1 = (bf16[128,3584]{1,0:T(8,128)(2,1)S(1)}, bf16[128,3584]{1,0:T(8,128)(2,1)}, u32[]{:S(2)}, u32[]{:S(2)}) collective-permute-start(bf16[128,3584]{1,0:T(8,128)(2,1)S(1)} %bitcast.21), channel_id=1, source_target_pairs={{0,256},{256,0},{1,257},{257,1},{2,258},{258,2},{3,259},{259,3},{4... | collective-permute-start | bytes 2752520 | tf_op jit(solution)/shard_map/ppermute | solution.py:262
  87.5 15.0 %all-to-all-start.4 = ((bf16[16,16,896]{2,1,0:T(8,128)(2,1)}), bf16[16,16,896]{2,1,0:T(8,128)(2,1)S(1)}, u32[]{:S(2)}, u32[]{:S(2)}) async-start(bf16[16,16,896]{2,1,0:T(8,128)(2,1)} %shard_map.123), calls=%async_computation.4 | async-start | bytes 917504 | tf_op jit(solution)/shard_map/all_to_all | solution.py:309
  119.3 18.5 %all-to-all-start.6 = ((bf16[16,32,128]{2,1,0:T(8,128)(2,1)}), bf16[16,32,128]{2,1,0:T(8,128)(2,1)S(1)}, u32[]{:S(2)}, u32[]{:S(2)}) async-start(bf16[16,32,128]{2,1,0:T(8,128)(2,1)} %shard_map.125), calls=%async_computation.6 | async-start | bytes 262144 | tf_op jit(solution)/shard_map/all_to_all | solution.py:322
  125.1 0.7 collective-permute-start.2
Sparse Core Ops, SparseCore 0:
  9.5 35.8 all-gather.1

commit v4 on v3

v4 whole, which is shorter than its diff:
```python
import jax
import jax.numpy as jnp
from jax import lax
from jax.experimental import pallas as pl
from jax.experimental.pallas import tpu as pltpu
from jax.sharding import Mesh
from jax.sharding import PartitionSpec as P

LAT = 512
SOFTMAX_SCALE = 192.0 ** (-0.5)
NORM_EPS = 1e-06

ROLE, X, Z, TP = 2, 4, 16, 4
MEMBERS = ROLE * TP
ROWBLK = 64
MOST = 16
EXPERTS = 64
COLS = 56
WIDTH = 3584
PLANE = Z * COLS
HALF = 64

Z_FIRST, X_FIRST, TP_FIRST = 8, 2, 2
Z_ORDER = [(i + Z_FIRST) % Z for i in range(Z)]
HEAD_ORDER = [
    (1 - role) * TP + (lane + TP_FIRST) % TP for role in range(ROLE) for lane in range(TP)
]
PLANE_ORDER = [
    (x + X_FIRST) % X * TP + (lane + TP_FIRST) % TP for x in range(X) for lane in range(TP)
]
Z_AT = [Z_ORDER.index(z) for z in range(Z)]
HEAD_AT = [HEAD_ORDER.index(i) for i in range(MEMBERS)]
PLANE_AT = [[PLANE_ORDER.index(x * TP + lane) for lane in range(TP)] for x in range(X)]

F32 = jnp.float32
BF16 = jnp.bfloat16
VMEM_LIMIT = 48 * 1024 * 1024
ALL_VMEM = 60 * 1024 * 1024


def nt_dot(a, b):
    return lax.dot_general(a, b, (((1,), (1,)), ((), ())), preferred_element_type=F32)


def nn_dot(a, b):
    return lax.dot_general(a, b, (((1,), (0,)), ((), ())), preferred_element_type=F32)


def local_call(
    body, out_shape, *args, scratch=(), smem=(), hbm=(), out_hbm=(), vmem=VMEM_LIMIT
):
    def space(i, smem, hbm):
        return pltpu.SMEM if i in smem else pltpu.HBM if i in hbm else pltpu.VMEM

    many = isinstance(out_shape, tuple)
    outs = [
        pl.BlockSpec(memory_space=space(i, (), out_hbm))
        for i in range(len(out_shape) if many else 1)
    ]
    return pl.pallas_call(
        body,
        out_shape=out_shape,
        in_specs=[pl.BlockSpec(memory_space=space(i, smem, hbm)) for i in range(len(args))],
        out_specs=tuple(outs) if many else outs[0],
        scratch_shapes=list(scratch),
        compiler_params=pltpu.CompilerParams(vmem_limit_bytes=vmem),
    )(*args)


def exchange(chunks, axes, order):
    return lax.all_to_all(chunks, axes, 0, 0, tiled=True, axis_index_groups=[order])


def shape(dims, dtype=BF16):
    return jax.ShapeDtypeStruct(dims, dtype)


def attend_kernel(
    length_ref,
    query_hbm,
    cache_hbm,
    weight_hbm,
    residual_hbm,
    out_ref,
    payload_hbm,
    query_ref,
    cache_ref,
    sems,
):
    depth = weight_hbm.shape[1]
    span = residual_hbm.shape[1] // ROLE
    start = pl.multiple_of(lax.axis_index("role") * span, span)
    copies = [
        pltpu.make_async_copy(cache_hbm.at[0], cache_ref, sems.at[0]),
        pltpu.make_async_copy(query_hbm.at[0], query_ref, sems.at[1]),
        pltpu.make_async_copy(weight_hbm, payload_hbm.at[:, pl.ds(0, depth)], sems.at[2]),
        pltpu.make_async_copy(
            residual_hbm.at[:, pl.ds(start, span)], payload_hbm.at[:, pl.ds(depth, span)], sems.at[3]
        ),
    ]
    for copy in copies:
        copy.start()
    copies[0].wait()
    copies[1].wait()
    scores = nn_dot(query_ref[...], cache_ref[...]) * SOFTMAX_SCALE
    visible = lax.broadcasted_iota(jnp.int32, scores.shape, 1) < length_ref[0]
    scores = jnp.where(visible, scores, -1e30)
    row_max = jnp.max(scores, axis=1, keepdims=True)
    weights = jnp.where(visible, jnp.exp(scores - row_max), 0.0)
    row_total = jnp.sum(weights, axis=1, keepdims=True)
    summed = nt_dot(weights.astype(BF16), cache_ref[:LAT])
    attended = summed / row_total
    heads = attended.shape[0] // MEMBERS
    attended = [attended[i * heads : (i + 1) * heads] for i in HEAD_ORDER]
    out_ref[...] = jnp.concatenate(attended, axis=0).astype(BF16)
    for copy in copies[2:]:
        copy.wait()


def value_kernel(att_ref, value_ref, out_ref):
    heads = value_ref.shape[0]
    att = att_ref[...]
    rows = att.shape[0]
    row_head = lax.broadcasted_iota(jnp.int32, (rows, 256), 0) % heads
    lane_head = lax.broadcasted_iota(jnp.int32, (rows, 256), 1) // 128
    for head in range(0, heads, 2):
        pair = jnp.concatenate([value_ref[head], value_ref[head + 1]], axis=1)
        kept = jnp.where(row_head == head + lane_head, nn_dot(att, pair), 0.0)
        value = jnp.sum(kept.reshape(rows // heads, heads, 256), axis=1)
        value = jnp.concatenate([value[i : i + 1] for i in HEAD_AT], axis=0).astype(BF16)
        out_ref[:, :, head * 128 : (head + 2) * 128] = jnp.broadcast_to(
            value[None], (out_ref.shape[0],) + value.shape
        )


def packed(tile):
    gap = jnp.zeros((ROWBLK // 2, HALF - COLS), F32)
    return jnp.concatenate([tile[: ROWBLK // 2], gap, tile[ROWBLK // 2 :], gap], axis=1)


def by_source(refs):
    for step, ref in zip((0, 2, 3, 1), refs):
        yield lax.rem(lax.axis_index("x") + step, X), ref


def project_kernel(values_ref, *refs):
    weights, out_ref = refs[:X], refs[X]
    depth = values_ref.shape[1]
    values = values_ref[...]
    for x, weight in by_source(weights):
        product = nt_dot(values, weight[:, :depth]).reshape(Z, MEMBERS, COLS)
        lane = lax.rem(x + TP - TP_FIRST, TP)
        for role in range(ROLE):
            tile = jnp.concatenate(
                [product[Z_AT[z], role * TP : (role + 1) * TP] for z in range(Z)], axis=0
            )
            out_ref[(1 - role) * TP + lane] = packed(tile).astype(BF16)


def residual_kernel(own_ref, *refs):
    payloads, out_ref = refs[: X - 1], refs[X - 1]
    span = ROWBLK * X
    token = lax.broadcasted_iota(jnp.int32, (ROWBLK, span), 0)
    request = lax.broadcasted_iota(jnp.int32, (ROWBLK, span), 1)
    mine = request == token + lax.axis_index("x") * ROWBLK
    start = pl.multiple_of(lax.axis_index("role") * span, span)
    columns = [own_ref[:, pl.ds(start, span)]]
    columns += [payload[:, payload.shape[1] - span :] for payload in payloads]
    total = jnp.zeros((ROWBLK, COLS), F32)
    for x, column in by_source(columns):
        wanted = mine & (x == lax.axis_index("tp"))
        total = total + nt_dot(jnp.where(wanted, 1.0, 0.0).astype(BF16), column)
    out_ref[...] = packed(total)


def hidden_kernel(parts_ref, residual_ref, out_ref, own_ref):
    total = jnp.sum(parts_ref[...].astype(F32), axis=0)
    total = (residual_ref[...] + total).astype(BF16)
    own_ref[...] = total
    out_ref[...] = jnp.broadcast_to(total[None], out_ref.shape)


def route_kernel(
    sent_ref, routed_ref, weight_ref, pick_ref, high_ref, low_ref, weights_ref, rank_ref
):
    dims = (EXPERTS, ROWBLK)
    expert_ids = lax.broadcasted_iota(jnp.int32, dims, 0)
    earlier = lax.broadcasted_iota(jnp.int32, (ROWBLK, ROWBLK), 0) < lax.broadcasted_iota(
        jnp.int32, (ROWBLK, ROWBLK), 1
    )
    before = jnp.where(earlier, 1.0, 0.0).astype(BF16)
    slots = lax.broadcasted_iota(jnp.int32, (MOST, ROWBLK), 0).astype(F32)

    def ranks(ids_ref):
        named = jnp.zeros(dims, F32)
        weights = jnp.zeros(dims, F32)
        for k in range(ids_ref.shape[0]):
            chosen = expert_ids == ids_ref[k : k + 1, :]
            named = named + jnp.where(chosen, 1.0, 0.0)
            weights = weights + jnp.where(chosen, weight_ref[k : k + 1, :], 0.0)
        rank = nn_dot(named.astype(BF16), before)
        return jnp.where(named > 0.5, rank, -1.0), weights

    rank_ref[...], _ = ranks(sent_ref)
    for x in range(X):
        row = rank_ref[pl.ds(x * Z + lax.axis_index("z"), 1), :]
        pick_ref[x * MOST : (x + 1) * MOST, :] = jnp.where(row == slots, 1.0, 0.0).astype(BF16)
    rank_ref[...], weights_ref[...] = ranks(routed_ref)
    for half in range(2):
        for z in range(Z):
            for pair in range(2):
                expert = (half * 2 + pair) * Z + z
                hit = rank_ref[expert : expert + 1, :] == slots
                table = jnp.where(hit, weights_ref[expert : expert + 1, :], 0.0)
                high = table.astype(BF16)
                low = (table - high.astype(F32)).astype(BF16)
                rows = pl.ds(Z_AT[z] * 32 + pair * MOST, MOST)
                lanes = pl.ds(half * HALF, ROWBLK)
                high_ref[rows, lanes] = high
                low_ref[rows, lanes] = low


def dispatch_kernel(parts_ref, pick_ref, own_ref, out_ref):
    parts = [parts_ref[Z_AT[z]].astype(F32) for z in range(Z)]
    hidden = jnp.concatenate(
        [
            jnp.concatenate([part[:, start : start + COLS] for part in parts], axis=1)
            for start in (0, HALF)
        ],
        axis=0,
    ).astype(BF16)
    rows = nn_dot(pick_ref[...], hidden).astype(BF16)
    own = own_ref[...]
    for x in range(X):
        piece = jnp.concatenate([rows[x * MOST : (x + 1) * MOST], own[:MOST], own[MOST:]], axis=1)
        for lane in range(TP):
            out_ref[PLANE_AT[x][lane]] = piece


def expert_kernel(arrived_ref, gain_ref, *refs):
    own_refs, peer_refs, (out_ref, tile_ref) = refs[:3], refs[3:6], refs[6:]
    x = lax.rem(lax.axis_index("tp") + X - X_FIRST, X)
    lane = lax.rem(lax.axis_index("x") + TP - TP_FIRST, TP)
    tile = arrived_ref[x * TP + lane]
    tile_ref[:MOST] = tile[:, PLANE : PLANE + 128]
    tile_ref[MOST:] = tile[:, PLANE + 128 :]
    rows = X * MOST
    total = jnp.zeros((rows, 1), F32)
    own = jnp.zeros((rows, 256), F32)
    peer = jnp.zeros((rows, 256), F32)
    for lane in range(TP):
        value = jnp.concatenate(
            [arrived_ref[PLANE_AT[x][lane], :, :PLANE] for x in range(X)], axis=0
        ).astype(F32)
        depth = pl.ds(lane * PLANE, PLANE)
        total = total + jnp.sum(value * value, axis=1, keepdims=True)
        scaled = (value * gain_ref[lane]).astype(BF16)
        own, peer = [
            so_far + nn_dot(scaled, jnp.concatenate([refs[0][depth], refs[1][depth]], axis=1))
            for so_far, refs in ((own, own_refs), (peer, peer_refs))
        ]
    inverse = lax.rsqrt(total / WIDTH + NORM_EPS)

    def activate(both):
        both = both * inverse
        gate, up = both[:, :128], both[:, 128:]
        return (gate / (1.0 + jnp.exp(-gate)) * up).astype(BF16)

    activated = jnp.concatenate([activate(own), activate(peer)], axis=1)
    for x in range(X):
        lanes = slice(x * PLANE, (x + 1) * PLANE)
        down = jnp.concatenate([own_refs[2][:, lanes], peer_refs[2][:, lanes]], axis=0)
        product = nn_dot(activated, down).astype(BF16)
        for lane in range(TP):
            out_ref[PLANE_AT[x][lane]] = product[lane * MOST : (lane + 1) * MOST]


def columns_kernel(parts_ref, out_ref):
    summed = []
    for x in range(X):
        total = parts_ref[PLANE_AT[x][0]].astype(F32)
        for lane in range(1, TP):
            total = total + parts_ref[PLANE_AT[x][lane]].astype(F32)
        summed.append(total)
    low = jnp.concatenate(summed[:2], axis=0)
    high = jnp.concatenate(summed[2:], axis=0)
    gap = jnp.zeros((32, HALF - COLS), F32)
    for z in range(Z):
        cut = slice(z * COLS, (z + 1) * COLS)
        out_ref[Z_AT[z]] = jnp.concatenate([low[:, cut], gap, high[:, cut], gap], axis=1).astype(BF16)


def combine_kernel(returned_ref, high_ref, low_ref, own_ref, out_ref):
    returned = returned_ref[...]
    dims = (((0,), (0,)), ((), ()))
    mixed = lax.dot_general(returned, high_ref[...], dims, preferred_element_type=F32)
    mixed = mixed + lax.dot_general(returned, low_ref[...], dims, preferred_element_type=F32)
    mixture = mixed[:COLS, :ROWBLK] + mixed[HALF : HALF + COLS, HALF : HALF + ROWBLK]
    column = lax.broadcasted_iota(jnp.int32, (COLS, 2 * HALF), 0)
    place = lax.broadcasted_iota(jnp.int32, (COLS, 2 * HALF), 1)
    own = own_ref[...]
    hidden = [
        nt_dot((place == column + start).astype(F32).astype(BF16), own) for start in (0, HALF)
    ]
    out_ref[...] = (jnp.concatenate(hidden, axis=1) + mixture).astype(BF16)


def shards(
    queries,
    latent_cache,
    lengths,
    value_up,
    output_weight,
    residual,
    norm_gain,
    routed_experts,
    route_weights,
    gate_weight,
    up_weight,
    down_weight,
):
    swap = [(0, 1), (1, 0)]
    role, x, lane = (lax.axis_index(name) for name in ("role", "x", "tp"))

    sent = lax.dynamic_slice_in_dim(routed_experts, (role * X + x) * ROWBLK, ROWBLK, 0).T
    block = (role * TP + lane) * ROWBLK
    routed = lax.dynamic_slice_in_dim(routed_experts, block, ROWBLK, 0).T
    weights = lax.dynamic_slice_in_dim(route_weights, block, ROWBLK, 0).T
    pick, high, low = local_call(
        route_kernel,
        (shape((X * MOST, ROWBLK)), shape((Z * 32, 128)), shape((Z * 32, 128))),
        sent,
        routed,
        weights,
        scratch=(pltpu.VMEM((EXPERTS, ROWBLK), F32), pltpu.VMEM((EXPERTS, ROWBLK), F32)),
    )

    heads = queries.shape[1]
    own_heads = heads // MEMBERS
    width = output_weight.shape[1] + residual.shape[1] // ROLE
    attended, payload = local_call(
        attend_kernel,
        (shape((heads, LAT)), shape((COLS, width))),
        lengths,
        queries,
        latent_cache.swapaxes(1, 2),
        output_weight,
        residual,
        scratch=(
            pltpu.VMEM(queries.shape[1:], BF16),
            pltpu.VMEM(latent_cache.shape[:0:-1], BF16),
            pltpu.SemaphoreType.DMA((4,)),
        ),
        smem=(0,),
        hbm=(1, 2, 3, 4),
        vmem=ALL_VMEM,
    )
    attended = attended.reshape(MEMBERS, own_heads, LAT)
    across = lax.ppermute(payload, "x", [(i, (i + 2) % X) for i in range(X)])
    regrouped = exchange(attended, ("role", "tp"), HEAD_ORDER)
    regrouped, across = lax.optimization_barrier((regrouped, across))
    values = local_call(
        value_kernel,
        shape((Z, MEMBERS, own_heads * 128)),
        regrouped.reshape(MEMBERS * own_heads, LAT),
        value_up,
    )
    payloads = [across] + [
        lax.ppermute(payload, "x", [(i, (i + step) % X) for i in range(X)]) for step in (1, 3)
    ]
    gathered = exchange(values, "z", Z_ORDER)
    projected = local_call(
        project_kernel,
        shape((MEMBERS, 32, 128)),
        gathered.reshape(Z * MEMBERS, own_heads * 128),
        output_weight,
        *payloads,
    )
    residual_tile = local_call(
        residual_kernel, shape((32, 128), F32), residual, *payloads
    )
    head_parts = exchange(projected, ("role", "tp"), HEAD_ORDER)
    hidden, own = local_call(
        hidden_kernel, (shape((Z, 32, 128)), shape((32, 128))), head_parts, residual_tile
    )

    gain_rows = norm_gain.reshape(TP, 1, PLANE)
    own_expert = (gate_weight[0], up_weight[0], down_weight[0])
    peer_expert = [lax.ppermute(weight, "role", swap) for weight in own_expert]
    hidden = exchange(hidden, "z", Z_ORDER)
    outbound = local_call(
        dispatch_kernel, shape((X * TP, MOST, PLANE + 256)), hidden, pick, own
    )
    arrived = exchange(outbound, ("x", "tp"), PLANE_ORDER)
    partial, own = local_call(
        expert_kernel,
        (shape((X * TP, MOST, PLANE)), shape((32, 128))),
        arrived,
        gain_rows,
        *own_expert,
        *peer_expert,
    )
    hidden_parts = exchange(partial, ("x", "tp"), PLANE_ORDER)
    columns = local_call(columns_kernel, shape((Z, 32, 128)), hidden_parts)
    returned = exchange(columns, "z", Z_ORDER)
    return local_call(
        combine_kernel,
        shape((COLS, ROWBLK)),
        returned.reshape(Z * 32, 128),
        high,
        low,
        own,
    )


def solution(mesh):
    grp = ("x", "z")
    fine = Mesh(mesh.devices.reshape(ROLE, X, Z, TP), ("role", "x", "z", "tp"))
    return jax.shard_map(
        shards,
        mesh=fine,
        in_specs=(
            P(("role",) + grp + ("tp",), None, None),
            P(("role",) + grp + ("tp",), None, None),
            P(("role",) + grp + ("tp",)),
            P(("role", "tp"), None, None),
            P(grp, ("role", "tp")),
            P(grp, None),
            P(),
            P(),
            P(),
            P(grp, None, ("role", "tp")),
            P(grp, None, ("role", "tp")),
            P(grp, ("role", "tp"), None),
        ),
        out_specs=P(grp, ("role", "tp")),
        check_vma=False,
    )
```

time: 146 us -> 133 us (0.911)
  the two profiles are of different devices: /device:TPU:32 before, /device:TPU:8 now
where the time goes in v4:
time: 133 us; the launch traced here: 132 us
  starting transfers between devices  57.3 us (43%)
  blocking collectives  39.8 us (30%)
  waiting for transfers between devices  19.4 us (15%)
  Pallas kernels  10.7 us (8%)
  local copies, waits for them, and re-layouts  3.59 us (3%)
    all_to_all x4, starting transfers between devices, exchange(): lax.all_to_all(chunks, axes, 0, 0, tiled=True, axis_index_groups=[order])  40.3 us
    all_to_all x3, blocking collectives, exchange(): lax.all_to_all(chunks, axes, 0, 0, tiled=True, axis_index_groups=[order])  39.8 us
    all_to_all x4, waiting for transfers between devices, exchange(): lax.all_to_all(chunks, axes, 0, 0, tiled=True, axis_index_groups=[order])  14 us
    pallas_call x10, Pallas kernels, local_call(): pl.pallas_call(body, out_shape=out_shape, in_specs=[pl.BlockSpec(memory_s...  10.7 us
    ppermute x3, starting transfers between devices, shards(): peer_expert = [lax.ppermute(weight, 'role', swap) for weight in own_expert]  6.25 us
    ppermute x2, starting transfers between devices, shards(): lax.ppermute(payload, 'x', [(i, (i + step) % X) for i in range(X)])  5.84 us
    ppermute x2, waiting for transfers between devices, shards(): lax.ppermute(payload, 'x', [(i, (i + step) % X) for i in range(X)])  5.4 us
    ppermute x1, starting transfers between devices, shards(): across = lax.ppermute(payload, 'x', [(i, (i + 2) % X) for i in range(X)])  4.93 us
  transfers between devices with their start and end apart: 10, of which 5 were waited for; matrix products, arithmetic and copies ran while one was open for 0% of the time, Pallas kernels for 1%

profile of v4, /device:TPU:8, one launch (start us, length us, event | category | flops | bytes accessed | tf_op | source)
XLA Modules:
  0.0 131.6 jit_solution(13532141251057731037)
XLA Ops:
  0.0 0.0 copy-start
  0.7 2.2 %shard_map.118 = (bf16[64,512]{1,0:T(8,128)(2,1)}, bf16[56,1280]{1,0:T(8,128)(2,1)}) custom-call(s32[1]{0:T(128)S(6)} %copy.13.length_ref, bf16[1,64,576]{2,1,0:T(8,128)(2,1)} %query_hbm.1, bf16[1,576,384]{2,1,0:T(8,128)(2,1)} %bitcast.23, bf16[56,1024]{1,0:T(8,128)(2,1)} %refs_0_.1, bf16[56,512]{1,0:T(8,128)(2,1)} %own_ref.1), custom_call_target="tpu_custom_call" | custom-call | tf_op jit(solution)/shard_map/pallas_call | solution.py:60
  2.9 4.9 %collective-permute-start = (bf16[56,1280]{1,0:T(8,128)(2,1)}, bf16[56,1280]{1,0:T(8,128)(2,1)S(1)}, u32[]{:S(2)}, u32[]{:S(2)}) collective-permute-start(bf16[56,1280]{1,0:T(8,128)(2,1)} %get-tuple-element.17), channel_id=1, source_target_pairs={{0,128},{64,192},{128,0},{192,64},{1,129},{65,193},{129,1},{193,65... | collective-permute-start | bytes 430088 | tf_op jit(solution)/shard_map/ppermute | solution.py:359
  7.8 9.5 %all_to_all.35 = bf16[8,8,512]{2,1,0:T(8,128)(2,1)S(1)} all-to-all(bf16[8,8,512]{2,1,0:T(8,128)(2,1)} %bitcast.24), channel_id=1, replica_groups={{258,259,256,257,2,3,0,1},{262,263,260,261,6,7,4,5},{266,267,264,265,10..., dimensions={0} | all-to-all | bytes 131072 | tf_op jit(solution)/shard_map/all_to_all | solution.py:71
  17.3 0.0 collective-permute-done.refs_1_.refs_0_
  17.3 0.0 copy-start.1
  17.3 1.2 copy-done.1
  18.5 0.0 copy-start.4
  18.5 1.0 shard_map.119
  19.6 0.0 copy-start.11
  19.6 0.0 copy-start.6
  19.6 17.7 %all-to-all-start.1 = ((bf16[16,8,1024]{2,1,0:T(8,128)(2,1)}), bf16[16,8,1024]{2,1,0:T(8,128)(2,1)S(1)}, u32[]{:S(2)}, u32[]{:S(2)}) async-start(bf16[16,8,1024]{2,1,0:T(8,128)(2,1)} %shard_map.119), calls=%async_computation.1 | async-start | bytes 524288 | tf_op jit(solution)/shard_map/all_to_all | solution.py:71
  37.3 0.0 copy-done.11
  37.3 3.0 %collective-permute-start.2 = (bf16[56,1280]{1,0:T(8,128)(2,1)S(1)}, bf16[56,1280]{1,0:T(8,128)(2,1)S(1)}, u32[]{:S(2)}, u32[]{:S(2)}) collective-permute-start(bf16[56,1280]{1,0:T(8,128)(2,1)S(1)} %copy-done.11), channel_id=1, source_target_pairs={{0,192},{64,0},{128,64},{192,128},{1,193},{65,1},{129,65},{193,129... | collective-permute-start | bytes 430088 | tf_op jit(solution)/shard_map/ppermute | solution.py:369
  40.3 2.8 %collective-permute-start.1 = (bf16[56,1280]{1,0:T(8,128)(2,1)S(1)}, bf16[56,1280]{1,0:T(8,128)(2,1)S(1)}, u32[]{:S(2)}, u32[]{:S(2)}) collective-permute-start(bf16[56,1280]{1,0:T(8,128)(2,1)S(1)} %copy-done.11), channel_id=1, source_target_pairs={{0,64},{64,128},{128,192},{192,0},{1,65},{65,129},{129,193},{193,1... | collective-permute-start | bytes 430088 | tf_op jit(solution)/shard_map/ppermute | solution.py:369
  43.1 1.1 collective-permute-done.2.refs_3_.refs_2_
  44.3 4.3 %collective-permute-done.1.refs_2_.refs_1_ = bf16[56,1280]{1,0:T(8,128)(2,1)S(1)} collective-permute-done((bf16[56,1280]{1,0:T(8,128)(2,1)S(1)}, bf16[56,1280]{1,0:T(8,128)(2,1)S(1)}, u32[]{:S(2)}, u32[]{:S(2)}) %collective-permute-start.1) | collective-permute-done | bytes 143392 | tf_op jit(solution)/shard_map/ppermute | solution.py:369
  48.5 0.8 all-to-all-done.1
  49.3 0.0 copy-start.5
  49.3 0.9 copy-done.5
  50.2 0.0 copy-start.2
  50.2 0.0 copy-start.3
  50.2 1.1 shard_map.120
  51.3 4.3 %all-to-all-start.2 = ((bf16[8,32,128]{2,1,0:T(8,128)(2,1)}), bf16[8,32,128]{2,1,0:T(8,128)(2,1)S(1)}, u32[]{:S(2)}, u32[]{:S(2)}) async-start(bf16[8,32,128]{2,1,0:T(8,128)(2,1)} %shard_map.120), calls=%async_computation.2 | async-start | bytes 131072 | tf_op jit(solution)/shard_map/all_to_all | solution.py:71
  55.7 0.0 copy-done.6
  55.7 0.2 shard_map.121.residual_ref
  55.9 3.9 %all-to-all-done.2.parts_ref = bf16[8,32,128]{2,1,0:T(8,128)(2,1)S(1)} async-done(((bf16[8,32,128]{2,1,0:T(8,128)(2,1)}), bf16[8,32,128]{2,1,0:T(8,128)(2,1)S(1)}, u32[]{:S(2)}, u32[]{:S(2)}) %all-to-all-start.2) | async-done | bytes 65568 | tf_op jit(solution)/shard_map/all_to_all | solution.py:71
  59.8 0.7 shard_map.122
  60.5 12.0 %all-to-all-start.3 = ((bf16[16,32,128]{2,1,0:T(8,128)(2,1)}), bf16[16,32,128]{2,1,0:T(8,128)(2,1)S(1)}, u32[]{:S(2)}, u32[]{:S(2)}) async-start(bf16[16,32,128]{2,1,0:T(8,128)(2,1)} %get-tuple-element.20), calls=%async_computation.3 | async-start | bytes 262144 | tf_op jit(solution)/shard_map/all_to_all | solution.py:71
  72.5 0.0 copy-done.2
  72.5 1.9 %collective-permute-start.3 = (bf16[3584,128]{1,0:T(8,128)(2,1)S(1)}, bf16[3584,128]{1,0:T(8,128)(2,1)}, u32[]{:S(2)}, u32[]{:S(2)}) collective-permute-start(bf16[3584,128]{1,0:T(8,128)(2,1)S(1)} %bitcast.15), channel_id=1, source_target_pairs={{0,256},{256,0},{1,257},{257,1},{2,258},{258,2},{3,259},{259,3},{4... | collective-permute-start | bytes 2752520 | tf_op jit(solution)/shard_map/ppermute | solution.py:389
  74.5 0.0 copy-done.3
  74.5 2.4 %collective-permute-start.4 = (bf16[3584,128]{1,0:T(8,128)(2,1)S(1)}, bf16[3584,128]{1,0:T(8,128)(2,1)}, u32[]{:S(2)}, u32[]{:S(2)}) collective-permute-start(bf16[3584,128]{1,0:T(8,128)(2,1)S(1)} %bitcast.17), channel_id=1, source_target_pairs={{0,256},{256,0},{1,257},{257,1},{2,258},{258,2},{3,259},{259,3},{4... | collective-permute-start | bytes 2752520 | tf_op jit(solution)/shard_map/ppermute | solution.py:389
  76.9 0.0 copy-done.4
  76.9 1.9 %collective-permute-start.5 = (bf16[128,3584]{1,0:T(8,128)(2,1)S(1)}, bf16[128,3584]{1,0:T(8,128)(2,1)}, u32[]{:S(2)}, u32[]{:S(2)}) collective-permute-start(bf16[128,3584]{1,0:T(8,128)(2,1)S(1)} %bitcast.19), channel_id=1, source_target_pairs={{0,256},{256,0},{1,257},{257,1},{2,258},{258,2},{3,259},{259,3},{4... | collective-permute-start | bytes 2752520 | tf_op jit(solution)/shard_map/ppermute | solution.py:389
  78.8 0.0 copy-start.10
  78.8 0.0 copy-done
  78.8 0.1 dynamic-slice_bitcast_fusion.weight_ref
  78.9 0.6 copy-done.10
  79.5 0.1 dynamic-slice_bitcast_fusion.1
  79.6 0.4 shard_map.123
  80.0 0.0 copy-start.7
  80.0 0.6 copy-done.7
  80.7 0.0 all-to-all-done.3.parts_ref
  80.7 1.1 shard_map.124
  81.8 0.0 copy-start.9
  81.8 6.2 %all-to-all-start.4 = ((bf16[16,16,1152]{2,1,0:T(8,128)(2,1)}), bf16[16,16,1152]{2,1,0:T(8,128)(2,1)S(1)}, u32[]{:S(2)}, u32[]{:S(2)}) async-start(bf16[16,16,1152]{2,1,0:T(8,128)(2,1)} %shard_map.124), calls=%async_computation.4 | async-start | bytes 1179648 | tf_op jit(solution)/shard_map/all_to_all | solution.py:71
  88.0 0.0 copy-done.9
  88.0 0.0 collective-permute-done.3.refs_3_
  88.0 0.0 collective-permute-done.4.refs_4_
  88.0 0.0 collective-permute-done.5.refs_5_
  88.0 9.3 %all-to-all-done.4.arrived_ref = bf16[16,16,1152]{2,1,0:T(8,128)(2,1)S(1)} async-done(((bf16[16,16,1152]{2,1,0:T(8,128)(2,1)}), bf16[16,16,1152]{2,1,0:T(8,128)(2,1)S(1)}, u32[]{:S(2)}, u32[]{:S(2)}) %all-to-all-start.4) | async-done | bytes 589856 | tf_op jit(solution)/shard_map/all_to_all | solution.py:71
  97.4 2.8 %shard_map.125 = (bf16[16,16,896]{2,1,0:T(8,128)(2,1)S(1)}, bf16[32,128]{1,0:T(8,128)(2,1)S(1)}) custom-call(bf16[16,16,1152]{2,1,0:T(8,128)(2,1)S(1)} %all-to-all-done.4.arrived_ref, f32[4,1,896]{2,1,0:T(1,128)S(1)} %reshape.18.gain_ref, bf16[3584,128]{1,0:T(8,128)(2,1)S(1)} %bitcast.16, bf16[3584,128]{1,0:T(8,128)(2,1)S(1)} %bitcast.18, ...), custom_call_target="tpu_custom_call" | custom-call | tf_op jit(solution)/shard_map/pallas_call | solution.py:60
  100.2 13.2 %all_to_all.36.parts_ref = bf16[16,16,896]{2,1,0:T(8,128)(2,1)S(1)} all-to-all(bf16[16,16,896]{2,1,0:T(8,128)(2,1)S(1)} %get-tuple-element.23), channel_id=1, replica_groups={{130,131,128,129,194,195,192,193,2,3,0,1,66,67,64,65},{134,135,132,133,..., dimensions={0} | all-to-all | bytes 917504 | tf_op jit(solution)/shard_map/all_to_all | solution.py:71
  113.4 0.2 shard_map.126
  113.6 0.0 copy-start.8
  113.6 17.1 %all_to_all.37 = bf16[16,32,128]{2,1,0:T(8,128)(2,1)S(1)} all-to-all(bf16[16,32,128]{2,1,0:T(8,128)(2,1)S(1)} %shard_map.126), channel_id=1, replica_groups={{32,36,40,44,48,52,56,60,0,4,8,12,16,20,24,28},{33,37,41,45,49,53,57,61..., dimensions={0} | all-to-all | bytes 262144 | tf_op jit(solution)/shard_map/all_to_all | solution.py:71
  130.7 0.0 copy-done.8
  130.7 0.9 shard_map.127
  (1 shorter events, 0.0 us)
Async XLA Ops:
  0.0 78.8 %copy-start = (f32[512,8]{0,1:T(8,128)S(1)}, f32[512,8]{0,1:T(8,128)}, u32[]{:S(2)}) copy-start(f32[512,8]{0,1:T(8,128)} %param.20) | copy-start | bytes 49156
  2.9 14.4 %collective-permute-start = (bf16[56,1280]{1,0:T(8,128)(2,1)}, bf16[56,1280]{1,0:T(8,128)(2,1)S(1)}, u32[]{:S(2)}, u32[]{:S(2)}) collective-permute-start(bf16[56,1280]{1,0:T(8,128)(2,1)} %get-tuple-element.17), channel_id=1, source_target_pairs={{0,128},{64,192},{128,0},{192,64},{1,129},{65,193},{129,1},{193,65... | collective-permute-start | bytes 430088 | tf_op jit(solution)/shard_map/ppermute | solution.py:359
  17.3 1.2 copy-start.1
  18.5 58.4 %copy-start.4 = (bf16[1,128,3584]{2,1,0:T(8,128)(2,1)S(1)}, bf16[1,128,3584]{2,1,0:T(8,128)(2,1)}, u32[]{:S(2)}) copy-start(bf16[1,128,3584]{2,1,0:T(8,128)(2,1)} %param.23) | copy-start | bytes 2752516
  19.6 17.7 %copy-start.11 = (bf16[56,1280]{1,0:T(8,128)(2,1)S(1)}, bf16[56,1280]{1,0:T(8,128)(2,1)}, u32[]{:S(2)}) copy-start(bf16[56,1280]{1,0:T(8,128)(2,1)} %get-tuple-element.17) | copy-start | bytes 430084
  19.6 36.1 %copy-start.6 = (bf16[56,512]{1,0:T(8,128)(2,1)S(1)}, bf16[56,512]{1,0:T(8,128)(2,1)}, u32[]{:S(2)}) copy-start(bf16[56,512]{1,0:T(8,128)(2,1)} %own_ref.1) | copy-start | bytes 172036
  19.6 29.7 %all-to-all-start.1 = ((bf16[16,8,1024]{2,1,0:T(8,128)(2,1)}), bf16[16,8,1024]{2,1,0:T(8,128)(2,1)S(1)}, u32[]{:S(2)}, u32[]{:S(2)}) async-start(bf16[16,8,1024]{2,1,0:T(8,128)(2,1)} %shard_map.119), calls=%async_computation.1 | async-start | bytes 524288 | tf_op jit(solution)/shard_map/all_to_all | solution.py:71
  37.3 7.0 %collective-permute-start.2 = (bf16[56,1280]{1,0:T(8,128)(2,1)S(1)}, bf16[56,1280]{1,0:T(8,128)(2,1)S(1)}, u32[]{:S(2)}, u32[]{:S(2)}) collective-permute-start(bf16[56,1280]{1,0:T(8,128)(2,1)S(1)} %copy-done.11), channel_id=1, source_target_pairs={{0,192},{64,0},{128,64},{192,128},{1,193},{65,1},{129,65},{193,129... | collective-permute-start | bytes 430088 | tf_op jit(solution)/shard_map/ppermute | solution.py:369
  40.3 8.2 %collective-permute-start.1 = (bf16[56,1280]{1,0:T(8,128)(2,1)S(1)}, bf16[56,1280]{1,0:T(8,128)(2,1)S(1)}, u32[]{:S(2)}, u32[]{:S(2)}) collective-permute-start(bf16[56,1280]{1,0:T(8,128)(2,1)S(1)} %copy-done.11), channel_id=1, source_target_pairs={{0,64},{64,128},{128,192},{192,0},{1,65},{65,129},{129,193},{193,1... | collective-permute-start | bytes 430088 | tf_op jit(solution)/shard_map/ppermute | solution.py:369
  49.3 0.9 copy-start.5
  50.2 22.3 %copy-start.2 = (bf16[1,3584,128]{2,1,0:T(8,128)(2,1)S(1)}, bf16[1,3584,128]{2,1,0:T(8,128)(2,1)}, u32[]{:S(2)}) copy-start(bf16[1,3584,128]{2,1,0:T(8,128)(2,1)} %param.21) | copy-start | bytes 2752516
  50.2 24.3 %copy-start.3 = (bf16[1,3584,128]{2,1,0:T(8,128)(2,1)S(1)}, bf16[1,3584,128]{2,1,0:T(8,128)(2,1)}, u32[]{:S(2)}) copy-start(bf16[1,3584,128]{2,1,0:T(8,128)(2,1)} %param.22) | copy-start | bytes 2752516
  51.3 8.5 %all-to-all-start.2 = ((bf16[8,32,128]{2,1,0:T(8,128)(2,1)}), bf16[8,32,128]{2,1,0:T(8,128)(2,1)S(1)}, u32[]{:S(2)}, u32[]{:S(2)}) async-start(bf16[8,32,128]{2,1,0:T(8,128)(2,1)} %shard_map.120), calls=%async_computation.2 | async-start | bytes 131072 | tf_op jit(solution)/shard_map/all_to_all | solution.py:71
  60.5 20.2 %all-to-all-start.3 = ((bf16[16,32,128]{2,1,0:T(8,128)(2,1)}), bf16[16,32,128]{2,1,0:T(8,128)(2,1)S(1)}, u32[]{:S(2)}, u32[]{:S(2)}) async-start(bf16[16,32,128]{2,1,0:T(8,128)(2,1)} %get-tuple-element.20), calls=%async_computation.3 | async-start | bytes 262144 | tf_op jit(solution)/shard_map/all_to_all | solution.py:71
  72.5 15.5 %collective-permute-start.3 = (bf16[3584,128]{1,0:T(8,128)(2,1)S(1)}, bf16[3584,128]{1,0:T(8,128)(2,1)}, u32[]{:S(2)}, u32[]{:S(2)}) collective-permute-start(bf16[3584,128]{1,0:T(8,128)(2,1)S(1)} %bitcast.15), channel_id=1, source_target_pairs={{0,256},{256,0},{1,257},{257,1},{2,258},{258,2},{3,259},{259,3},{4... | collective-permute-start | bytes 2752520 | tf_op jit(solution)/shard_map/ppermute | solution.py:389
  74.5 13.6 %collective-permute-start.4 = (bf16[3584,128]{1,0:T(8,128)(2,1)S(1)}, bf16[3584,128]{1,0:T(8,128)(2,1)}, u32[]{:S(2)}, u32[]{:S(2)}) collective-permute-start(bf16[3584,128]{1,0:T(8,128)(2,1)S(1)} %bitcast.17), channel_id=1, source_target_pairs={{0,256},{256,0},{1,257},{257,1},{2,258},{258,2},{3,259},{259,3},{4... | collective-permute-start | bytes 2752520 | tf_op jit(solution)/shard_map/ppermute | solution.py:389
  76.9 11.1 %collective-permute-start.5 = (bf16[128,3584]{1,0:T(8,128)(2,1)S(1)}, bf16[128,3584]{1,0:T(8,128)(2,1)}, u32[]{:S(2)}, u32[]{:S(2)}) collective-permute-start(bf16[128,3584]{1,0:T(8,128)(2,1)S(1)} %bitcast.19), channel_id=1, source_target_pairs={{0,256},{256,0},{1,257},{257,1},{2,258},{258,2},{3,259},{259,3},{4... | collective-permute-start | bytes 2752520 | tf_op jit(solution)/shard_map/ppermute | solution.py:389
  78.8 0.7 copy-start.10
  80.0 0.7 copy-start.7
  81.8 6.2 %copy-start.9 = (f32[3584]{0:T(1024)S(1)}, f32[3584]{0:T(1024)}, u32[]{:S(2)}) copy-start(f32[3584]{0:T(1024)} %param.18) | copy-start | bytes 43012
  81.8 15.6 %all-to-all-start.4 = ((bf16[16,16,1152]{2,1,0:T(8,128)(2,1)}), bf16[16,16,1152]{2,1,0:T(8,128)(2,1)S(1)}, u32[]{:S(2)}, u32[]{:S(2)}) async-start(bf16[16,16,1152]{2,1,0:T(8,128)(2,1)} %shard_map.124), calls=%async_computation.4 | async-start | bytes 1179648 | tf_op jit(solution)/shard_map/all_to_all | solution.py:71
  113.6 17.1 %copy-start.8 = (bf16[512,128]{1,0:T(8,128)(2,1)S(1)}, bf16[512,128]{1,0:T(8,128)(2,1)}, u32[]{:S(2)}) copy-start(bf16[512,128]{1,0:T(8,128)(2,1)} %copy-done.7) | copy-start | bytes 393220

commit v5 on v4

--- a/solution.py
+++ b/solution.py
@@ -20,21 +20,30 @@
 PLANE = Z * COLS
 HALF = 64
 
-Z_FIRST, X_FIRST, TP_FIRST = 8, 2, 2
-Z_ORDER = [(i + Z_FIRST) % Z for i in range(Z)]
+VALUE_FIRST, HIDDEN_FIRST, RETURN_FIRST = 8, 4, 8
+X_FIRST, TP_FIRST = 2, 2
+
+
+def z_order(first):
+    return [(i + first) % Z for i in range(Z)]
+
+
+def z_places(first):
+    return [(z - first) % Z for z in range(Z)]
+
+
 HEAD_ORDER = [
     (1 - role) * TP + (lane + TP_FIRST) % TP for role in range(ROLE) for lane in range(TP)
 ]
 PLANE_ORDER = [
     (x + X_FIRST) % X * TP + (lane + TP_FIRST) % TP for x in range(X) for lane in range(TP)
 ]
-Z_AT = [Z_ORDER.index(z) for z in range(Z)]
 HEAD_AT = [HEAD_ORDER.index(i) for i in range(MEMBERS)]
 PLANE_AT = [[PLANE_ORDER.index(x * TP + lane) for lane in range(TP)] for x in range(X)]
 
 F32 = jnp.float32
 BF16 = jnp.bfloat16
-VMEM_LIMIT = 48 * 1024 * 1024
+VMEM_LIMIT = 16 * 1024 * 1024
 ALL_VMEM = 60 * 1024 * 1024
 
 
@@ -152,7 +161,7 @@
         lane = lax.rem(x + TP - TP_FIRST, TP)
         for role in range(ROLE):
             tile = jnp.concatenate(
-                [product[Z_AT[z], role * TP : (role + 1) * TP] for z in range(Z)], axis=0
+                [product[at, role * TP : (role + 1) * TP] for at in z_places(VALUE_FIRST)], axis=0
             )
             out_ref[(1 - role) * TP + lane] = packed(tile).astype(BF16)
 
@@ -214,14 +223,14 @@
                 table = jnp.where(hit, weights_ref[expert : expert + 1, :], 0.0)
                 high = table.astype(BF16)
                 low = (table - high.astype(F32)).astype(BF16)
-                rows = pl.ds(Z_AT[z] * 32 + pair * MOST, MOST)
+                rows = pl.ds(z_places(RETURN_FIRST)[z] * 32 + pair * MOST, MOST)
                 lanes = pl.ds(half * HALF, ROWBLK)
                 high_ref[rows, lanes] = high
                 low_ref[rows, lanes] = low
 
 
-def dispatch_kernel(parts_ref, pick_ref, own_ref, out_ref):
-    parts = [parts_ref[Z_AT[z]].astype(F32) for z in range(Z)]
+def dispatch_kernel(parts_ref, pick_ref, out_ref):
+    parts = [parts_ref[at].astype(F32) for at in z_places(HIDDEN_FIRST)]
     hidden = jnp.concatenate(
         [
             jnp.concatenate([part[:, start : start + COLS] for part in parts], axis=1)
@@ -230,35 +239,33 @@
         axis=0,
     ).astype(BF16)
     rows = nn_dot(pick_ref[...], hidden).astype(BF16)
-    own = own_ref[...]
     for x in range(X):
-        piece = jnp.concatenate([rows[x * MOST : (x + 1) * MOST], own[:MOST], own[MOST:]], axis=1)
+        piece = rows[x * MOST : (x + 1) * MOST]
         for lane in range(TP):
             out_ref[PLANE_AT[x][lane]] = piece
 
 
 def expert_kernel(arrived_ref, gain_ref, *refs):
-    own_refs, peer_refs, (out_ref, tile_ref) = refs[:3], refs[3:6], refs[6:]
-    x = lax.rem(lax.axis_index("tp") + X - X_FIRST, X)
-    lane = lax.rem(lax.axis_index("x") + TP - TP_FIRST, TP)
-    tile = arrived_ref[x * TP + lane]
-    tile_ref[:MOST] = tile[:, PLANE : PLANE + 128]
-    tile_ref[MOST:] = tile[:, PLANE + 128 :]
+    own_refs, peer_refs, out_ref = refs[:3], refs[3:6], refs[6]
     rows = X * MOST
     total = jnp.zeros((rows, 1), F32)
-    own = jnp.zeros((rows, 256), F32)
-    peer = jnp.zeros((rows, 256), F32)
+    scaled = []
     for lane in range(TP):
         value = jnp.concatenate(
-            [arrived_ref[PLANE_AT[x][lane], :, :PLANE] for x in range(X)], axis=0
+            [arrived_ref[PLANE_AT[x][lane]] for x in range(X)], axis=0
         ).astype(F32)
-        depth = pl.ds(lane * PLANE, PLANE)
         total = total + jnp.sum(value * value, axis=1, keepdims=True)
-        scaled = (value * gain_ref[lane]).astype(BF16)
-        own, peer = [
-            so_far + nn_dot(scaled, jnp.concatenate([refs[0][depth], refs[1][depth]], axis=1))
-            for so_far, refs in ((own, own_refs), (peer, peer_refs))
-        ]
+        scaled.append((value * gain_ref[lane]).astype(BF16))
+
+    def hidden_sums(refs):
+        sums = jnp.zeros((rows, 256), F32)
+        for lane in range(TP):
+            depth = pl.ds(lane * PLANE, PLANE)
+            both = jnp.concatenate([refs[0][depth], refs[1][depth]], axis=1)
+            sums = sums + nn_dot(scaled[lane], both)
+        return sums
+
+    own, peer = hidden_sums(own_refs), hidden_sums(peer_refs)
     inverse = lax.rsqrt(total / WIDTH + NORM_EPS)
 
     def activate(both):
@@ -287,7 +294,7 @@
     gap = jnp.zeros((32, HALF - COLS), F32)
     for z in range(Z):
         cut = slice(z * COLS, (z + 1) * COLS)
-        out_ref[Z_AT[z]] = jnp.concatenate([low[:, cut], gap, high[:, cut], gap], axis=1).astype(BF16)
+        out_ref[z_places(RETURN_FIRST)[z]] = jnp.concatenate([low[:, cut], gap, high[:, cut], gap], axis=1).astype(BF16)
 
 
 def combine_kernel(returned_ref, high_ref, low_ref, own_ref, out_ref):
@@ -303,6 +310,28 @@
         nt_dot((place == column + start).astype(F32).astype(BF16), own) for start in (0, HALF)
     ]
     out_ref[...] = (jnp.concatenate(hidden, axis=1) + mixture).astype(BF16)
+
+
+def preload_kernel(*refs):
+    count = (len(refs) - 1) // 2
+    sems = refs[-1]
+    copies = [
+        pltpu.make_async_copy(refs[i], refs[count + i], sems.at[i]) for i in range(count)
+    ]
+    for copy in copies:
+        copy.start()
+    for copy in copies:
+        copy.wait()
+
+
+def preload(*arrays):
+    return local_call(
+        preload_kernel,
+        tuple(shape(array.shape, array.dtype) for array in arrays),
+        *arrays,
+        scratch=(pltpu.SemaphoreType.DMA((len(arrays),)),),
+        hbm=range(len(arrays)),
+    )
 
 
 def shards(
@@ -355,25 +384,27 @@
         hbm=(1, 2, 3, 4),
         vmem=ALL_VMEM,
     )
+    attended, late_value, late_weight = lax.optimization_barrier(
+        (attended, value_up, output_weight)
+    )
+    value_blocks, weight_rows = preload(late_value, late_weight)
     attended = attended.reshape(MEMBERS, own_heads, LAT)
-    across = lax.ppermute(payload, "x", [(i, (i + 2) % X) for i in range(X)])
     regrouped = exchange(attended, ("role", "tp"), HEAD_ORDER)
-    regrouped, across = lax.optimization_barrier((regrouped, across))
     values = local_call(
         value_kernel,
         shape((Z, MEMBERS, own_heads * 128)),
         regrouped.reshape(MEMBERS * own_heads, LAT),
-        value_up,
-    )
-    payloads = [across] + [
-        lax.ppermute(payload, "x", [(i, (i + step) % X) for i in range(X)]) for step in (1, 3)
-    ]
-    gathered = exchange(values, "z", Z_ORDER)
+        value_blocks,
+    )
+    right, left = ([(i, (i + step) % X) for i in range(X)] for step in (1, X - 1))
+    near = lax.ppermute(payload, "x", right)
+    payloads = [lax.ppermute(near, "x", right), near, lax.ppermute(payload, "x", left)]
+    gathered = exchange(values, "z", z_order(VALUE_FIRST))
     projected = local_call(
         project_kernel,
         shape((MEMBERS, 32, 128)),
         gathered.reshape(Z * MEMBERS, own_heads * 128),
-        output_weight,
+        weight_rows,
         *payloads,
     )
     residual_tile = local_call(
@@ -387,14 +418,18 @@
     gain_rows = norm_gain.reshape(TP, 1, PLANE)
     own_expert = (gate_weight[0], up_weight[0], down_weight[0])
     peer_expert = [lax.ppermute(weight, "role", swap) for weight in own_expert]
-    hidden = exchange(hidden, "z", Z_ORDER)
+    hidden = exchange(hidden, "z", z_order(HIDDEN_FIRST))
     outbound = local_call(
-        dispatch_kernel, shape((X * TP, MOST, PLANE + 256)), hidden, pick, own
+        dispatch_kernel, shape((X * TP, MOST, PLANE)), hidden, pick
+    )
+    own = lax.ppermute(
+        own, ("x", "tp"), [(a * TP + b, b * TP + a) for a in range(X) for b in range(TP)]
     )
     arrived = exchange(outbound, ("x", "tp"), PLANE_ORDER)
-    partial, own = local_call(
+    arrived, own = lax.optimization_barrier((arrived, own))
+    partial = local_call(
         expert_kernel,
-        (shape((X * TP, MOST, PLANE)), shape((32, 128))),
+        shape((X * TP, MOST, PLANE)),
         arrived,
         gain_rows,
         *own_expert,
@@ -402,7 +437,7 @@
     )
     hidden_parts = exchange(partial, ("x", "tp"), PLANE_ORDER)
     columns = local_call(columns_kernel, shape((Z, 32, 128)), hidden_parts)
-    returned = exchange(columns, "z", Z_ORDER)
+    returned = exchange(columns, "z", z_order(RETURN_FIRST))
     return local_call(
         combine_kernel,
         shape((COLS, ROWBLK)),

time: 133 us -> 128 us (0.962)
  the two profiles are of different devices: /device:TPU:8 before, /device:TPU:4 now
where the time goes in v5:
time: 128 us; the launch traced here: 127 us
  starting transfers between devices  65.8 us (51%)
  blocking collectives  29.6 us (23%)
  waiting for transfers between devices  15.8 us (12%)
  Pallas kernels  10.8 us (8%)
  local copies, waits for them, and re-layouts  3.59 us (3%)
    all_to_all x5, starting transfers between devices, exchange(): lax.all_to_all(chunks, axes, 0, 0, tiled=True, axis_index_groups=[order])  45.7 us
    all_to_all x2, blocking collectives, exchange(): lax.all_to_all(chunks, axes, 0, 0, tiled=True, axis_index_groups=[order])  29.6 us
    pallas_call x11, Pallas kernels, local_call(): pl.pallas_call(body, out_shape=out_shape, in_specs=[pl.BlockSpec(memory_s...  10.8 us
    all_to_all x5, waiting for transfers between devices, exchange(): lax.all_to_all(chunks, axes, 0, 0, tiled=True, axis_index_groups=[order])  6.29 us
    ppermute x3, starting transfers between devices, shards(): peer_expert = [lax.ppermute(weight, 'role', swap) for weight in own_expert]  6.25 us
    ppermute x1, starting transfers between devices, shards(): lax.ppermute(own, ('x', 'tp'), [(a * TP + b, b * TP + a) for a in range(X...  4.9 us
    ppermute x1, waiting for transfers between devices, shards(): lax.ppermute(own, ('x', 'tp'), [(a * TP + b, b * TP + a) for a in range(X...  4.5 us
    ppermute x1, waiting for transfers between devices, shards(): lax.ppermute(near, 'x', right)  3.87 us
  transfers between devices with their start and end apart: 12, of which 6 were waited for; matrix products, arithmetic and copies ran while one was open for 0% of the time, Pallas kernels for 2%

profile of v5, /device:TPU:4, one launch (start us, length us, event | category | flops | bytes accessed | tf_op | source)
XLA Modules:
  0.0 126.5 jit_solution(714075864929703734)
XLA Ops:
  0.0 0.0 copy-start
  0.7 2.2 %shard_map.118 = (bf16[64,512]{1,0:T(8,128)(2,1)}, bf16[56,1280]{1,0:T(8,128)(2,1)}) custom-call(s32[1]{0:T(128)S(6)} %copy.13.length_ref, bf16[1,64,576]{2,1,0:T(8,128)(2,1)} %query_hbm.1, bf16[1,576,384]{2,1,0:T(8,128)(2,1)} %bitcast.23, bf16[56,1024]{1,0:T(8,128)(2,1)} %refs_1_, bf16[56,512]{1,0:T(8,128)(2,1)} %own_ref.1), custom_call_target="tpu_custom_call" | custom-call | tf_op jit(solution)/shard_map/pallas_call | solution.py:69
  2.9 0.0 copy-start.5
  2.9 6.1 %all-to-all-start = ((bf16[8,8,512]{2,1,0:T(8,128)(2,1)}), bf16[8,8,512]{2,1,0:T(8,128)(2,1)S(1)}, u32[]{:S(2)}, u32[]{:S(2)}) async-start(bf16[8,8,512]{2,1,0:T(8,128)(2,1)} %bitcast.24), calls=%async_computation | async-start | bytes 131072 | tf_op jit(solution)/shard_map/all_to_all | solution.py:80
  9.0 0.0 copy-done.5
  9.0 0.0 copy-start.1
  9.0 1.2 copy-done.1
  10.2 0.2 shard_map.119
  10.4 0.0 copy-start.7
  10.4 0.6 copy-done.7
  11.1 0.5 all-to-all-done
  11.6 0.0 copy-start.4
  11.6 1.0 shard_map.120
  12.6 0.0 copy-start.11
  12.6 0.0 copy-start.6
  12.6 19.0 %all-to-all-start.1 = ((bf16[16,8,1024]{2,1,0:T(8,128)(2,1)}), bf16[16,8,1024]{2,1,0:T(8,128)(2,1)S(1)}, u32[]{:S(2)}, u32[]{:S(2)}) async-start(bf16[16,8,1024]{2,1,0:T(8,128)(2,1)} %shard_map.120), calls=%async_computation.1 | async-start | bytes 524288 | tf_op jit(solution)/shard_map/all_to_all | solution.py:80
  31.6 0.0 copy-done.11
  31.6 3.1 %collective-permute-start = (bf16[56,1280]{1,0:T(8,128)(2,1)S(1)}, bf16[56,1280]{1,0:T(8,128)(2,1)S(1)}, u32[]{:S(2)}, u32[]{:S(2)}) collective-permute-start(bf16[56,1280]{1,0:T(8,128)(2,1)S(1)} %copy-done.11), channel_id=1, source_target_pairs={{0,64},{64,128},{128,192},{192,0},{1,65},{65,129},{129,193},{193,1... | collective-permute-start | bytes 430088 | tf_op jit(solution)/shard_map/ppermute | solution.py:400
  34.7 2.7 %collective-permute-start.2 = (bf16[56,1280]{1,0:T(8,128)(2,1)S(1)}, bf16[56,1280]{1,0:T(8,128)(2,1)S(1)}, u32[]{:S(2)}, u32[]{:S(2)}) collective-permute-start(bf16[56,1280]{1,0:T(8,128)(2,1)S(1)} %copy-done.11), channel_id=1, source_target_pairs={{0,192},{64,0},{128,64},{192,128},{1,193},{65,1},{129,65},{193,129... | collective-permute-start | bytes 430088 | tf_op jit(solution)/shard_map/ppermute | solution.py:401
  37.5 1.1 collective-permute-done.refs_2_.refs_1_
  38.6 3.1 %collective-permute-start.1 = (bf16[56,1280]{1,0:T(8,128)(2,1)S(1)}, bf16[56,1280]{1,0:T(8,128)(2,1)S(1)}, u32[]{:S(2)}, u32[]{:S(2)}) collective-permute-start(bf16[56,1280]{1,0:T(8,128)(2,1)S(1)} %collective-permute-done.refs_2_.refs_1_), channel_id=1, source_target_pairs={{0,64},{64,128},{128,192},{192,0},{1,65},{65,129},{129,193},{193,1... | collective-permute-start | bytes 430088 | tf_op jit(solution)/shard_map/ppermute | solution.py:401
  41.7 0.0 collective-permute-done.2.refs_3_.refs_2_
  41.7 3.9 %collective-permute-done.1.refs_1_.refs_0_ = bf16[56,1280]{1,0:T(8,128)(2,1)S(1)} collective-permute-done((bf16[56,1280]{1,0:T(8,128)(2,1)S(1)}, bf16[56,1280]{1,0:T(8,128)(2,1)S(1)}, u32[]{:S(2)}, u32[]{:S(2)}) %collective-permute-start.1) | collective-permute-done | bytes 143392 | tf_op jit(solution)/shard_map/ppermute | solution.py:401
  45.6 0.0 all-to-all-done.1
  45.6 0.0 copy-start.8
  45.6 0.9 copy-done.8
  46.5 0.0 copy-start.2
  46.5 0.0 copy-start.3
  46.5 1.1 shard_map.121
  47.6 5.0 %all-to-all-start.2 = ((bf16[8,32,128]{2,1,0:T(8,128)(2,1)}), bf16[8,32,128]{2,1,0:T(8,128)(2,1)S(1)}, u32[]{:S(2)}, u32[]{:S(2)}) async-start(bf16[8,32,128]{2,1,0:T(8,128)(2,1)} %shard_map.121), calls=%async_computation.2 | async-start | bytes 131072 | tf_op jit(solution)/shard_map/all_to_all | solution.py:80
  52.7 0.0 copy-done.6
  52.7 0.2 shard_map.122.residual_ref
  52.9 2.7 %all-to-all-done.2.parts_ref = bf16[8,32,128]{2,1,0:T(8,128)(2,1)S(1)} async-done(((bf16[8,32,128]{2,1,0:T(8,128)(2,1)}), bf16[8,32,128]{2,1,0:T(8,128)(2,1)S(1)}, u32[]{:S(2)}, u32[]{:S(2)}) %all-to-all-start.2) | async-done | bytes 65568 | tf_op jit(solution)/shard_map/all_to_all | solution.py:80
  55.6 0.7 shard_map.123
  56.3 9.3 %all-to-all-start.3 = ((bf16[16,32,128]{2,1,0:T(8,128)(2,1)}), bf16[16,32,128]{2,1,0:T(8,128)(2,1)S(1)}, u32[]{:S(2)}, u32[]{:S(2)}) async-start(bf16[16,32,128]{2,1,0:T(8,128)(2,1)} %get-tuple-element.26), calls=%async_computation.3 | async-start | bytes 262144 | tf_op jit(solution)/shard_map/all_to_all | solution.py:80
  65.6 0.0 copy-done.2
  65.6 1.9 %collective-permute-start.4 = (bf16[3584,128]{1,0:T(8,128)(2,1)S(1)}, bf16[3584,128]{1,0:T(8,128)(2,1)}, u32[]{:S(2)}, u32[]{:S(2)}) collective-permute-start(bf16[3584,128]{1,0:T(8,128)(2,1)S(1)} %bitcast.15), channel_id=1, source_target_pairs={{0,256},{256,0},{1,257},{257,1},{2,258},{258,2},{3,259},{259,3},{4... | collective-permute-start | bytes 2752520 | tf_op jit(solution)/shard_map/ppermute | solution.py:420
  67.6 0.0 copy-done.3
  67.6 2.4 %collective-permute-start.5 = (bf16[3584,128]{1,0:T(8,128)(2,1)S(1)}, bf16[3584,128]{1,0:T(8,128)(2,1)}, u32[]{:S(2)}, u32[]{:S(2)}) collective-permute-start(bf16[3584,128]{1,0:T(8,128)(2,1)S(1)} %bitcast.17), channel_id=1, source_target_pairs={{0,256},{256,0},{1,257},{257,1},{2,258},{258,2},{3,259},{259,3},{4... | collective-permute-start | bytes 2752520 | tf_op jit(solution)/shard_map/ppermute | solution.py:420
  70.0 0.0 copy-done.4
  70.0 1.9 %collective-permute-start.6 = (bf16[128,3584]{1,0:T(8,128)(2,1)S(1)}, bf16[128,3584]{1,0:T(8,128)(2,1)}, u32[]{:S(2)}, u32[]{:S(2)}) collective-permute-start(bf16[128,3584]{1,0:T(8,128)(2,1)S(1)} %bitcast.19), channel_id=1, source_target_pairs={{0,256},{256,0},{1,257},{257,1},{2,258},{258,2},{3,259},{259,3},{4... | collective-permute-start | bytes 2752520 | tf_op jit(solution)/shard_map/ppermute | solution.py:420
  71.9 0.0 copy-start.10
  72.0 0.0 copy-done
  72.0 0.1 dynamic-slice_bitcast_fusion.weight_ref
  72.1 0.6 copy-done.10
  72.7 0.1 dynamic-slice_bitcast_fusion.1
  72.7 0.4 shard_map.124
  73.1 3.0 %all-to-all-done.3.parts_ref = bf16[16,32,128]{2,1,0:T(8,128)(2,1)S(1)} async-done(((bf16[16,32,128]{2,1,0:T(8,128)(2,1)}), bf16[16,32,128]{2,1,0:T(8,128)(2,1)S(1)}, u32[]{:S(2)}, u32[]{:S(2)}) %all-to-all-start.3) | async-done | bytes 131104 | tf_op jit(solution)/shard_map/all_to_all | solution.py:80
  76.2 1.0 shard_map.125
  77.2 0.0 copy-start.9
  77.2 6.3 %all-to-all-start.4 = ((bf16[16,16,896]{2,1,0:T(8,128)(2,1)}), bf16[16,16,896]{2,1,0:T(8,128)(2,1)S(1)}, u32[]{:S(2)}, u32[]{:S(2)}) async-start(bf16[16,16,896]{2,1,0:T(8,128)(2,1)} %shard_map.125), calls=%async_computation.4 | async-start | bytes 917504 | tf_op jit(solution)/shard_map/all_to_all | solution.py:80
  83.5 4.9 %collective-permute-start.3 = (bf16[32,128]{1,0:T(8,128)(2,1)S(1)}, bf16[32,128]{1,0:T(8,128)(2,1)S(1)}, u32[]{:S(2)}, u32[]{:S(2)}) collective-permute-start(bf16[32,128]{1,0:T(8,128)(2,1)S(1)} %get-tuple-element.28), channel_id=1, source_target_pairs={{0,0},{1,64},{2,128},{3,192},{64,1},{65,65},{66,129},{67,193},{128... | collective-permute-start | bytes 24584 | tf_op jit(solution)/shard_map/ppermute | solution.py:425
  88.4 0.0 copy-done.9
  88.4 4.5 %collective-permute-done.3.own_ref = bf16[32,128]{1,0:T(8,128)(2,1)S(1)} collective-permute-done((bf16[32,128]{1,0:T(8,128)(2,1)S(1)}, bf16[32,128]{1,0:T(8,128)(2,1)S(1)}, u32[]{:S(2)}, u32[]{:S(2)}) %collective-permute-start.3) | collective-permute-done | bytes 8224 | tf_op jit(solution)/shard_map/ppermute | solution.py:425
  92.9 0.0 all-to-all-done.4.arrived_ref
  92.9 0.0 collective-permute-done.4.refs_3_
  92.9 0.0 collective-permute-done.5.refs_4_
  92.9 0.0 collective-permute-done.6.refs_5_
  92.9 2.8 %shard_map.126 = bf16[16,16,896]{2,1,0:T(8,128)(2,1)S(1)} custom-call(bf16[16,16,896]{2,1,0:T(8,128)(2,1)S(1)} %all-to-all-done.4.arrived_ref, f32[4,1,896]{2,1,0:T(1,128)S(1)} %reshape.18.gain_ref, bf16[3584,128]{1,0:T(8,128)(2,1)S(1)} %bitcast.16, bf16[3584,128]{1,0:T(8,128)(2,1)S(1)} %bitcast.18, bf16[128,3584]{1,0:T(8,128)(2,1)S(1)} %bitcast.20, ...), custom_call_target="tpu_custom_call" | custom-call | tf_op jit(solution)/shard_map/pallas_call | solution.py:69
  95.8 12.1 %all_to_all.35.parts_ref = bf16[16,16,896]{2,1,0:T(8,128)(2,1)S(1)} all-to-all(bf16[16,16,896]{2,1,0:T(8,128)(2,1)S(1)} %shard_map.126), channel_id=1, replica_groups={{130,131,128,129,194,195,192,193,2,3,0,1,66,67,64,65},{134,135,132,133,..., dimensions={0} | all-to-all | bytes 917504 | tf_op jit(solution)/shard_map/all_to_all | solution.py:80
  107.9 0.2 shard_map.127
  108.1 17.5 %all_to_all.36 = bf16[16,32,128]{2,1,0:T(8,128)(2,1)S(1)} all-to-all(bf16[16,32,128]{2,1,0:T(8,128)(2,1)S(1)} %shard_map.127), channel_id=1, replica_groups={{32,36,40,44,48,52,56,60,0,4,8,12,16,20,24,28},{33,37,41,45,49,53,57,61..., dimensions={0} | all-to-all | bytes 262144 | tf_op jit(solution)/shard_map/all_to_all | solution.py:80
  125.6 0.9 shard_map.128
  (1 shorter events, 0.0 us)
Async XLA Ops:
  0.0 72.0 %copy-start = (f32[512,8]{0,1:T(8,128)S(1)}, f32[512,8]{0,1:T(8,128)}, u32[]{:S(2)}) copy-start(f32[512,8]{0,1:T(8,128)} %param.20) | copy-start | bytes 49156
  2.9 6.1 %copy-start.5 = (bf16[56,1024]{1,0:T(8,128)(2,1)S(1)}, bf16[56,1024]{1,0:T(8,128)(2,1)}, u32[]{:S(2)}) copy-start(bf16[56,1024]{1,0:T(8,128)(2,1)} %refs_1_) | copy-start | bytes 344068
  2.9 8.7 %all-to-all-start = ((bf16[8,8,512]{2,1,0:T(8,128)(2,1)}), bf16[8,8,512]{2,1,0:T(8,128)(2,1)S(1)}, u32[]{:S(2)}, u32[]{:S(2)}) async-start(bf16[8,8,512]{2,1,0:T(8,128)(2,1)} %bitcast.24), calls=%async_computation | async-start | bytes 131072 | tf_op jit(solution)/shard_map/all_to_all | solution.py:80
  9.0 1.2 copy-start.1
  10.4 0.7 copy-start.7
  11.6 58.4 %copy-start.4 = (bf16[1,128,3584]{2,1,0:T(8,128)(2,1)S(1)}, bf16[1,128,3584]{2,1,0:T(8,128)(2,1)}, u32[]{:S(2)}) copy-start(bf16[1,128,3584]{2,1,0:T(8,128)(2,1)} %param.23) | copy-start | bytes 2752516
  12.6 19.0 %copy-start.11 = (bf16[56,1280]{1,0:T(8,128)(2,1)S(1)}, bf16[56,1280]{1,0:T(8,128)(2,1)}, u32[]{:S(2)}) copy-start(bf16[56,1280]{1,0:T(8,128)(2,1)} %get-tuple-element.25) | copy-start | bytes 430084
  12.6 40.0 %copy-start.6 = (bf16[56,512]{1,0:T(8,128)(2,1)S(1)}, bf16[56,512]{1,0:T(8,128)(2,1)}, u32[]{:S(2)}) copy-start(bf16[56,512]{1,0:T(8,128)(2,1)} %own_ref.1) | copy-start | bytes 172036
  12.6 33.0 %all-to-all-start.1 = ((bf16[16,8,1024]{2,1,0:T(8,128)(2,1)}), bf16[16,8,1024]{2,1,0:T(8,128)(2,1)S(1)}, u32[]{:S(2)}, u32[]{:S(2)}) async-start(bf16[16,8,1024]{2,1,0:T(8,128)(2,1)} %shard_map.120), calls=%async_computation.1 | async-start | bytes 524288 | tf_op jit(solution)/shard_map/all_to_all | solution.py:80
  31.6 7.0 %collective-permute-start = (bf16[56,1280]{1,0:T(8,128)(2,1)S(1)}, bf16[56,1280]{1,0:T(8,128)(2,1)S(1)}, u32[]{:S(2)}, u32[]{:S(2)}) collective-permute-start(bf16[56,1280]{1,0:T(8,128)(2,1)S(1)} %copy-done.11), channel_id=1, source_target_pairs={{0,64},{64,128},{128,192},{192,0},{1,65},{65,129},{129,193},{193,1... | collective-permute-start | bytes 430088 | tf_op jit(solution)/shard_map/ppermute | solution.py:400
  34.7 7.0 %collective-permute-start.2 = (bf16[56,1280]{1,0:T(8,128)(2,1)S(1)}, bf16[56,1280]{1,0:T(8,128)(2,1)S(1)}, u32[]{:S(2)}, u32[]{:S(2)}) collective-permute-start(bf16[56,1280]{1,0:T(8,128)(2,1)S(1)} %copy-done.11), channel_id=1, source_target_pairs={{0,192},{64,0},{128,64},{192,128},{1,193},{65,1},{129,65},{193,129... | collective-permute-start | bytes 430088 | tf_op jit(solution)/shard_map/ppermute | solution.py:401
  38.6 7.0 %collective-permute-start.1 = (bf16[56,1280]{1,0:T(8,128)(2,1)S(1)}, bf16[56,1280]{1,0:T(8,128)(2,1)S(1)}, u32[]{:S(2)}, u32[]{:S(2)}) collective-permute-start(bf16[56,1280]{1,0:T(8,128)(2,1)S(1)} %collective-permute-done.refs_2_.refs_1_), channel_id=1, source_target_pairs={{0,64},{64,128},{128,192},{192,0},{1,65},{65,129},{129,193},{193,1... | collective-permute-start | bytes 430088 | tf_op jit(solution)/shard_map/ppermute | solution.py:401
  45.6 0.9 copy-start.8
  46.5 19.2 %copy-start.2 = (bf16[1,3584,128]{2,1,0:T(8,128)(2,1)S(1)}, bf16[1,3584,128]{2,1,0:T(8,128)(2,1)}, u32[]{:S(2)}) copy-start(bf16[1,3584,128]{2,1,0:T(8,128)(2,1)} %param.21) | copy-start | bytes 2752516
  46.5 21.1 %copy-start.3 = (bf16[1,3584,128]{2,1,0:T(8,128)(2,1)S(1)}, bf16[1,3584,128]{2,1,0:T(8,128)(2,1)}, u32[]{:S(2)}) copy-start(bf16[1,3584,128]{2,1,0:T(8,128)(2,1)} %param.22) | copy-start | bytes 2752516
  47.6 8.0 %all-to-all-start.2 = ((bf16[8,32,128]{2,1,0:T(8,128)(2,1)}), bf16[8,32,128]{2,1,0:T(8,128)(2,1)S(1)}, u32[]{:S(2)}, u32[]{:S(2)}) async-start(bf16[8,32,128]{2,1,0:T(8,128)(2,1)} %shard_map.121), calls=%async_computation.2 | async-start | bytes 131072 | tf_op jit(solution)/shard_map/all_to_all | solution.py:80
  56.3 19.9 %all-to-all-start.3 = ((bf16[16,32,128]{2,1,0:T(8,128)(2,1)}), bf16[16,32,128]{2,1,0:T(8,128)(2,1)S(1)}, u32[]{:S(2)}, u32[]{:S(2)}) async-start(bf16[16,32,128]{2,1,0:T(8,128)(2,1)} %get-tuple-element.26), calls=%async_computation.3 | async-start | bytes 262144 | tf_op jit(solution)/shard_map/all_to_all | solution.py:80
  65.6 27.3 %collective-permute-start.4 = (bf16[3584,128]{1,0:T(8,128)(2,1)S(1)}, bf16[3584,128]{1,0:T(8,128)(2,1)}, u32[]{:S(2)}, u32[]{:S(2)}) collective-permute-start(bf16[3584,128]{1,0:T(8,128)(2,1)S(1)} %bitcast.15), channel_id=1, source_target_pairs={{0,256},{256,0},{1,257},{257,1},{2,258},{258,2},{3,259},{259,3},{4... | collective-permute-start | bytes 2752520 | tf_op jit(solution)/shard_map/ppermute | solution.py:420
  67.6 25.3 %collective-permute-start.5 = (bf16[3584,128]{1,0:T(8,128)(2,1)S(1)}, bf16[3584,128]{1,0:T(8,128)(2,1)}, u32[]{:S(2)}, u32[]{:S(2)}) collective-permute-start(bf16[3584,128]{1,0:T(8,128)(2,1)S(1)} %bitcast.17), channel_id=1, source_target_pairs={{0,256},{256,0},{1,257},{257,1},{2,258},{258,2},{3,259},{259,3},{4... | collective-permute-start | bytes 2752520 | tf_op jit(solution)/shard_map/ppermute | solution.py:420
  70.0 22.9 %collective-permute-start.6 = (bf16[128,3584]{1,0:T(8,128)(2,1)S(1)}, bf16[128,3584]{1,0:T(8,128)(2,1)}, u32[]{:S(2)}, u32[]{:S(2)}) collective-permute-start(bf16[128,3584]{1,0:T(8,128)(2,1)S(1)} %bitcast.19), channel_id=1, source_target_pairs={{0,256},{256,0},{1,257},{257,1},{2,258},{258,2},{3,259},{259,3},{4... | collective-permute-start | bytes 2752520 | tf_op jit(solution)/shard_map/ppermute | solution.py:420
  71.9 0.7 copy-start.10
  77.2 11.2 %copy-start.9 = (f32[3584]{0:T(1024)S(1)}, f32[3584]{0:T(1024)}, u32[]{:S(2)}) copy-start(f32[3584]{0:T(1024)} %param.18) | copy-start | bytes 43012
  77.2 15.7 %all-to-all-start.4 = ((bf16[16,16,896]{2,1,0:T(8,128)(2,1)}), bf16[16,16,896]{2,1,0:T(8,128)(2,1)S(1)}, u32[]{:S(2)}, u32[]{:S(2)}) async-start(bf16[16,16,896]{2,1,0:T(8,128)(2,1)} %shard_map.125), calls=%async_computation.4 | async-start | bytes 917504 | tf_op jit(solution)/shard_map/all_to_all | solution.py:80
  83.5 9.4 %collective-permute-start.3 = (bf16[32,128]{1,0:T(8,128)(2,1)S(1)}, bf16[32,128]{1,0:T(8,128)(2,1)S(1)}, u32[]{:S(2)}, u32[]{:S(2)}) collective-permute-start(bf16[32,128]{1,0:T(8,128)(2,1)S(1)} %get-tuple-element.28), channel_id=1, source_target_pairs={{0,0},{1,64},{2,128},{3,192},{64,1},{65,65},{66,129},{67,193},{128... | collective-permute-start | bytes 24584 | tf_op jit(solution)/shard_map/ppermute | solution.py:425

commit v6 on v5

--- a/solution.py
+++ b/solution.py
@@ -21,7 +21,8 @@
 HALF = 64
 
 VALUE_FIRST, HIDDEN_FIRST, RETURN_FIRST = 8, 4, 8
-X_FIRST, TP_FIRST = 2, 2
+HEAD_ROLE_FIRST, HEAD_TP_FIRST = 1, 2
+PLANE_X_FIRST, PLANE_TP_FIRST = 2, 2
 
 
 def z_order(first):
@@ -33,10 +34,14 @@
 
 
 HEAD_ORDER = [
-    (1 - role) * TP + (lane + TP_FIRST) % TP for role in range(ROLE) for lane in range(TP)
+    (role + HEAD_ROLE_FIRST) % ROLE * TP + (lane + HEAD_TP_FIRST) % TP
+    for role in range(ROLE)
+    for lane in range(TP)
 ]
 PLANE_ORDER = [
-    (x + X_FIRST) % X * TP + (lane + TP_FIRST) % TP for x in range(X) for lane in range(TP)
+    (x + PLANE_X_FIRST) % X * TP + (lane + PLANE_TP_FIRST) % TP
+    for x in range(X)
+    for lane in range(TP)
 ]
 HEAD_AT = [HEAD_ORDER.index(i) for i in range(MEMBERS)]
 PLANE_AT = [[PLANE_ORDER.index(x * TP + lane) for lane in range(TP)] for x in range(X)]
@@ -158,12 +163,12 @@
     values = values_ref[...]
     for x, weight in by_source(weights):
         product = nt_dot(values, weight[:, :depth]).reshape(Z, MEMBERS, COLS)
-        lane = lax.rem(x + TP - TP_FIRST, TP)
+        lane = lax.rem(x + TP - HEAD_TP_FIRST, TP)
         for role in range(ROLE):
             tile = jnp.concatenate(
                 [product[at, role * TP : (role + 1) * TP] for at in z_places(VALUE_FIRST)], axis=0
             )
-            out_ref[(1 - role) * TP + lane] = packed(tile).astype(BF16)
+            out_ref[(role + HEAD_ROLE_FIRST) % ROLE * TP + lane] = packed(tile).astype(BF16)
 
 
 def residual_kernel(own_ref, *refs):
@@ -182,16 +187,20 @@
     out_ref[...] = packed(total)
 
 
-def hidden_kernel(parts_ref, residual_ref, out_ref, own_ref):
+def hidden_kernel(parts_ref, residual_ref, out_ref):
     total = jnp.sum(parts_ref[...].astype(F32), axis=0)
     total = (residual_ref[...] + total).astype(BF16)
-    own_ref[...] = total
     out_ref[...] = jnp.broadcast_to(total[None], out_ref.shape)
 
 
-def route_kernel(
-    sent_ref, routed_ref, weight_ref, pick_ref, high_ref, low_ref, weights_ref, rank_ref
-):
+def block_of(ref, block):
+    pair = ref[:, pl.ds(pl.multiple_of(block // 2 * (2 * ROWBLK), 2 * ROWBLK), 2 * ROWBLK)]
+    return jnp.where(lax.rem(block, 2) == 0, pair[:, :ROWBLK], pair[:, ROWBLK:])
+
+
+def route_kernel(routed_ref, weight_ref, pick_ref, slots_ref, place_ref, rank_ref):
+    role, x, lane = (lax.axis_index(name) for name in ("role", "x", "tp"))
+    z = lax.axis_index("z")
     dims = (EXPERTS, ROWBLK)
     expert_ids = lax.broadcasted_iota(jnp.int32, dims, 0)
     earlier = lax.broadcasted_iota(jnp.int32, (ROWBLK, ROWBLK), 0) < lax.broadcasted_iota(
@@ -200,33 +209,47 @@
     before = jnp.where(earlier, 1.0, 0.0).astype(BF16)
     slots = lax.broadcasted_iota(jnp.int32, (MOST, ROWBLK), 0).astype(F32)
 
-    def ranks(ids_ref):
+    def ranks(ids):
         named = jnp.zeros(dims, F32)
-        weights = jnp.zeros(dims, F32)
-        for k in range(ids_ref.shape[0]):
-            chosen = expert_ids == ids_ref[k : k + 1, :]
-            named = named + jnp.where(chosen, 1.0, 0.0)
-            weights = weights + jnp.where(chosen, weight_ref[k : k + 1, :], 0.0)
+        for k in range(ids.shape[0]):
+            named = named + jnp.where(expert_ids == ids[k : k + 1, :], 1.0, 0.0)
         rank = nn_dot(named.astype(BF16), before)
-        return jnp.where(named > 0.5, rank, -1.0), weights
-
-    rank_ref[...], _ = ranks(sent_ref)
-    for x in range(X):
-        row = rank_ref[pl.ds(x * Z + lax.axis_index("z"), 1), :]
-        pick_ref[x * MOST : (x + 1) * MOST, :] = jnp.where(row == slots, 1.0, 0.0).astype(BF16)
-    rank_ref[...], weights_ref[...] = ranks(routed_ref)
+        return jnp.where(named > 0.5, rank, -1.0)
+
+    rank_ref[...] = ranks(block_of(routed_ref, role * X + x))
+    for i in range(X):
+        row = rank_ref[pl.ds(i * Z + z, 1), :]
+        pick_ref[i * MOST : (i + 1) * MOST, :] = jnp.where(row == slots, 1.0, 0.0).astype(BF16)
+
+    rank_ref[...] = ranks(block_of(routed_ref, role * TP + lane))
     for half in range(2):
-        for z in range(Z):
+        for i in range(Z):
             for pair in range(2):
-                expert = (half * 2 + pair) * Z + z
+                expert = (half * 2 + pair) * Z + i
                 hit = rank_ref[expert : expert + 1, :] == slots
-                table = jnp.where(hit, weights_ref[expert : expert + 1, :], 0.0)
-                high = table.astype(BF16)
-                low = (table - high.astype(F32)).astype(BF16)
-                rows = pl.ds(z_places(RETURN_FIRST)[z] * 32 + pair * MOST, MOST)
+                rows = pl.ds(z_places(RETURN_FIRST)[i] * 32 + pair * MOST, MOST)
                 lanes = pl.ds(half * HALF, ROWBLK)
-                high_ref[rows, lanes] = high
-                low_ref[rows, lanes] = low
+                place_ref[rows, lanes] = jnp.where(hit, 1.0, 0.0).astype(BF16)
+
+    span = ROWBLK * X
+    start = pl.multiple_of(role * span, span)
+    mine = routed_ref[:, pl.ds(start, span)] == x * Z + z
+    named = jnp.where(mine, 1.0, 0.0)
+    weights = jnp.sum(jnp.where(mine, weight_ref[:, pl.ds(start, span)], 0.0), axis=0, keepdims=True)
+    source = lax.broadcasted_iota(jnp.int32, (span, span), 0)
+    request = lax.broadcasted_iota(jnp.int32, (span, span), 1)
+    inside = (source < request) & (source // ROWBLK == request // ROWBLK)
+    rank = nn_dot(named.astype(BF16), jnp.where(inside, 1.0, 0.0).astype(BF16))
+    rank = jnp.sum(rank, axis=0, keepdims=True)
+    chosen = jnp.sum(named, axis=0, keepdims=True)
+    rank = jnp.where(chosen > 0.5, rank, -1.0)
+    slot = lax.broadcasted_iota(jnp.int32, (X * MOST, span), 0)
+    token = lax.broadcasted_iota(jnp.int32, (X * MOST, span), 1)
+    hit = (rank == lax.rem(slot, MOST).astype(F32)) & (token // ROWBLK == slot // MOST)
+    weight = jnp.sum(jnp.where(hit, weights, 0.0), axis=1, keepdims=True)
+    first = jnp.sum(jnp.where(hit, named[:1], 0.0), axis=1, keepdims=True)
+    column = lax.broadcasted_iota(jnp.int32, slots_ref.shape, 1)
+    slots_ref[...] = jnp.where(column == 0, weight, first)
 
 
 def dispatch_kernel(parts_ref, pick_ref, out_ref):
@@ -245,16 +268,17 @@
             out_ref[PLANE_AT[x][lane]] = piece
 
 
-def expert_kernel(arrived_ref, gain_ref, *refs):
+def expert_kernel(arrived_ref, gain_ref, slots_ref, *refs):
     own_refs, peer_refs, out_ref = refs[:3], refs[3:6], refs[6]
     rows = X * MOST
     total = jnp.zeros((rows, 1), F32)
-    scaled = []
+    values, scaled = [], []
     for lane in range(TP):
         value = jnp.concatenate(
             [arrived_ref[PLANE_AT[x][lane]] for x in range(X)], axis=0
         ).astype(F32)
         total = total + jnp.sum(value * value, axis=1, keepdims=True)
+        values.append(value)
         scaled.append((value * gain_ref[lane]).astype(BF16))
 
     def hidden_sums(refs):
@@ -274,10 +298,12 @@
         return (gate / (1.0 + jnp.exp(-gate)) * up).astype(BF16)
 
     activated = jnp.concatenate([activate(own), activate(peer)], axis=1)
+    weight = slots_ref[:, 0:1]
+    first = slots_ref[:, 1:2] * jnp.where(lax.axis_index("tp") == 0, 1.0, 0.0)
     for x in range(X):
         lanes = slice(x * PLANE, (x + 1) * PLANE)
         down = jnp.concatenate([own_refs[2][:, lanes], peer_refs[2][:, lanes]], axis=0)
-        product = nn_dot(activated, down).astype(BF16)
+        product = (nn_dot(activated, down) * weight + values[x] * first).astype(BF16)
         for lane in range(TP):
             out_ref[PLANE_AT[x][lane]] = product[lane * MOST : (lane + 1) * MOST]
 
@@ -297,19 +323,13 @@
         out_ref[z_places(RETURN_FIRST)[z]] = jnp.concatenate([low[:, cut], gap, high[:, cut], gap], axis=1).astype(BF16)
 
 
-def combine_kernel(returned_ref, high_ref, low_ref, own_ref, out_ref):
-    returned = returned_ref[...]
+def combine_kernel(returned_ref, place_ref, out_ref):
     dims = (((0,), (0,)), ((), ()))
-    mixed = lax.dot_general(returned, high_ref[...], dims, preferred_element_type=F32)
-    mixed = mixed + lax.dot_general(returned, low_ref[...], dims, preferred_element_type=F32)
-    mixture = mixed[:COLS, :ROWBLK] + mixed[HALF : HALF + COLS, HALF : HALF + ROWBLK]
-    column = lax.broadcasted_iota(jnp.int32, (COLS, 2 * HALF), 0)
-    place = lax.broadcasted_iota(jnp.int32, (COLS, 2 * HALF), 1)
-    own = own_ref[...]
-    hidden = [
-        nt_dot((place == column + start).astype(F32).astype(BF16), own) for start in (0, HALF)
-    ]
-    out_ref[...] = (jnp.concatenate(hidden, axis=1) + mixture).astype(BF16)
+    mixed = lax.dot_general(
+        returned_ref[...], place_ref[...], dims, preferred_element_type=F32
+    )
+    mixed = mixed[:COLS, :ROWBLK] + mixed[HALF : HALF + COLS, HALF : HALF + ROWBLK]
+    out_ref[...] = mixed.astype(BF16)
 
 
 def preload_kernel(*refs):
@@ -349,19 +369,12 @@
     down_weight,
 ):
     swap = [(0, 1), (1, 0)]
-    role, x, lane = (lax.axis_index(name) for name in ("role", "x", "tp"))
-
-    sent = lax.dynamic_slice_in_dim(routed_experts, (role * X + x) * ROWBLK, ROWBLK, 0).T
-    block = (role * TP + lane) * ROWBLK
-    routed = lax.dynamic_slice_in_dim(routed_experts, block, ROWBLK, 0).T
-    weights = lax.dynamic_slice_in_dim(route_weights, block, ROWBLK, 0).T
-    pick, high, low = local_call(
+    pick, slots, places = local_call(
         route_kernel,
-        (shape((X * MOST, ROWBLK)), shape((Z * 32, 128)), shape((Z * 32, 128))),
-        sent,
-        routed,
-        weights,
-        scratch=(pltpu.VMEM((EXPERTS, ROWBLK), F32), pltpu.VMEM((EXPERTS, ROWBLK), F32)),
+        (shape((X * MOST, ROWBLK)), shape((X * MOST, 128), F32), shape((Z * 32, 128))),
+        routed_experts.T,
+        route_weights.T,
+        scratch=(pltpu.VMEM((EXPERTS, ROWBLK), F32),),
     )
 
     heads = queries.shape[1]
@@ -411,9 +424,7 @@
         residual_kernel, shape((32, 128), F32), residual, *payloads
     )
     head_parts = exchange(projected, ("role", "tp"), HEAD_ORDER)
-    hidden, own = local_call(
-        hidden_kernel, (shape((Z, 32, 128)), shape((32, 128))), head_parts, residual_tile
-    )
+    hidden = local_call(hidden_kernel, shape((Z, 32, 128)), head_parts, residual_tile)
 
     gain_rows = norm_gain.reshape(TP, 1, PLANE)
     own_expert = (gate_weight[0], up_weight[0], down_weight[0])
@@ -422,16 +433,13 @@
     outbound = local_call(
         dispatch_kernel, shape((X * TP, MOST, PLANE)), hidden, pick
     )
-    own = lax.ppermute(
-        own, ("x", "tp"), [(a * TP + b, b * TP + a) for a in range(X) for b in range(TP)]
-    )
     arrived = exchange(outbound, ("x", "tp"), PLANE_ORDER)
-    arrived, own = lax.optimization_barrier((arrived, own))
     partial = local_call(
         expert_kernel,
         shape((X * TP, MOST, PLANE)),
         arrived,
         gain_rows,
+        slots,
         *own_expert,
         *peer_expert,
     )
@@ -442,9 +450,7 @@
         combine_kernel,
         shape((COLS, ROWBLK)),
         returned.reshape(Z * 32, 128),
-        high,
-        low,
-        own,
+        places,
     )
 
 

time: 128 us -> 125 us (0.977)
  starting transfers between devices: 65.8 us -> 61.1 us
  waiting for transfers between devices: 15.8 us -> 19.5 us
    all_to_all x5, waiting for transfers between devices: 6.29 us -> 14.5 us  [exchange(): lax.all_to_all(chunks, axes, 0, 0, tiled=True, axis_index_groups=[order])]
    ppermute x1 -> x0, starting transfers between devices: 4.9 us -> none  [shards(): lax.ppermute(own, ('x', 'tp'), [(a * TP + b, b * TP + a) for a in range(X...]
    ppermute x1 -> x0, waiting for transfers between devices: 4.5 us -> none  [shards(): lax.ppermute(own, ('x', 'tp'), [(a * TP + b, b * TP + a) for a in range(X...]
  transfers between devices with their start and end apart: 12 -> 11, of which waited for: 6 -> 6; matrix products, arithmetic and copies ran while one was open for 0% -> 0% of each run, Pallas kernels for 2% -> 2%
where the time goes in v6:
time: 125 us; the launch traced here: 124 us
  starting transfers between devices  61.1 us (49%)
  blocking collectives  29.3 us (23%)
  waiting for transfers between devices  19.5 us (16%)
  Pallas kernels  10.8 us (9%)
  local copies, waits for them, and re-layouts  2.82 us (2%)
    all_to_all x5, starting transfers between devices, exchange(): lax.all_to_all(chunks, axes, 0, 0, tiled=True, axis_index_groups=[order])  45.9 us
    all_to_all x2, blocking collectives, exchange(): lax.all_to_all(chunks, axes, 0, 0, tiled=True, axis_index_groups=[order])  29.3 us
    all_to_all x5, waiting for transfers between devices, exchange(): lax.all_to_all(chunks, axes, 0, 0, tiled=True, axis_index_groups=[order])  14.5 us
    pallas_call x11, Pallas kernels, local_call(): pl.pallas_call(body, out_shape=out_shape, in_specs=[pl.BlockSpec(memory_s...  10.8 us
    ppermute x3, starting transfers between devices, shards(): peer_expert = [lax.ppermute(weight, 'role', swap) for weight in own_expert]  6.25 us
    ppermute x1, waiting for transfers between devices, shards(): lax.ppermute(near, 'x', right)  3.87 us
    ppermute x1, starting transfers between devices, shards(): near = lax.ppermute(payload, 'x', right)  3.11 us
    ppermute x1, starting transfers between devices, shards(): lax.ppermute(near, 'x', right)  3.09 us
  transfers between devices with their start and end apart: 11, of which 6 were waited for; matrix products, arithmetic and copies ran while one was open for 0% of the time, Pallas kernels for 2%

profile of v6, /device:TPU:4, one launch (start us, length us, event | category | flops | bytes accessed | tf_op | source)
XLA Modules:
  0.0 124.4 jit_solution(12217009080056891323)
XLA Ops:
  0.7 2.2 %shard_map.118 = (bf16[64,512]{1,0:T(8,128)(2,1)}, bf16[56,1280]{1,0:T(8,128)(2,1)}) custom-call(s32[1]{0:T(128)S(6)} %copy.13.length_ref, bf16[1,64,576]{2,1,0:T(8,128)(2,1)} %query_hbm.1, bf16[1,576,384]{2,1,0:T(8,128)(2,1)} %bitcast.21, bf16[56,1024]{1,0:T(8,128)(2,1)} %refs_1_, bf16[56,512]{1,0:T(8,128)(2,1)} %own_ref.1), custom_call_target="tpu_custom_call" | custom-call | tf_op jit(solution)/shard_map/pallas_call | solution.py:74
  2.9 0.0 copy-start.4
  2.9 6.1 %all-to-all-start = ((bf16[8,8,512]{2,1,0:T(8,128)(2,1)}), bf16[8,8,512]{2,1,0:T(8,128)(2,1)S(1)}, u32[]{:S(2)}, u32[]{:S(2)}) async-start(bf16[8,8,512]{2,1,0:T(8,128)(2,1)} %bitcast.22), calls=%async_computation | async-start | bytes 131072 | tf_op jit(solution)/shard_map/all_to_all | solution.py:85
  9.0 0.0 copy-done.4
  9.0 0.0 copy-start
  9.0 1.2 copy-done
  10.2 0.2 shard_map.119
  10.4 0.0 copy-start.6
  10.4 0.6 copy-done.6
  11.1 0.5 all-to-all-done
  11.6 0.0 copy-start.3
  11.6 1.0 shard_map.120
  12.6 0.0 copy-start.11
  12.6 0.0 copy-start.5
  12.6 19.0 %all-to-all-start.1 = ((bf16[16,8,1024]{2,1,0:T(8,128)(2,1)}), bf16[16,8,1024]{2,1,0:T(8,128)(2,1)S(1)}, u32[]{:S(2)}, u32[]{:S(2)}) async-start(bf16[16,8,1024]{2,1,0:T(8,128)(2,1)} %shard_map.120), calls=%async_computation.1 | async-start | bytes 524288 | tf_op jit(solution)/shard_map/all_to_all | solution.py:85
  31.6 0.0 copy-done.11
  31.6 3.1 %collective-permute-start = (bf16[56,1280]{1,0:T(8,128)(2,1)S(1)}, bf16[56,1280]{1,0:T(8,128)(2,1)S(1)}, u32[]{:S(2)}, u32[]{:S(2)}) collective-permute-start(bf16[56,1280]{1,0:T(8,128)(2,1)S(1)} %copy-done.11), channel_id=1, source_target_pairs={{0,64},{64,128},{128,192},{192,0},{1,65},{65,129},{129,193},{193,1... | collective-permute-start | bytes 430088 | tf_op jit(solution)/shard_map/ppermute | solution.py:413
  34.7 2.7 %collective-permute-start.2 = (bf16[56,1280]{1,0:T(8,128)(2,1)S(1)}, bf16[56,1280]{1,0:T(8,128)(2,1)S(1)}, u32[]{:S(2)}, u32[]{:S(2)}) collective-permute-start(bf16[56,1280]{1,0:T(8,128)(2,1)S(1)} %copy-done.11), channel_id=1, source_target_pairs={{0,192},{64,0},{128,64},{192,128},{1,193},{65,1},{129,65},{193,129... | collective-permute-start | bytes 430088 | tf_op jit(solution)/shard_map/ppermute | solution.py:414
  37.5 1.1 collective-permute-done.refs_2_.refs_1_
  38.6 3.1 %collective-permute-start.1 = (bf16[56,1280]{1,0:T(8,128)(2,1)S(1)}, bf16[56,1280]{1,0:T(8,128)(2,1)S(1)}, u32[]{:S(2)}, u32[]{:S(2)}) collective-permute-start(bf16[56,1280]{1,0:T(8,128)(2,1)S(1)} %collective-permute-done.refs_2_.refs_1_), channel_id=1, source_target_pairs={{0,64},{64,128},{128,192},{192,0},{1,65},{65,129},{129,193},{193,1... | collective-permute-start | bytes 430088 | tf_op jit(solution)/shard_map/ppermute | solution.py:414
  41.7 0.0 collective-permute-done.2.refs_3_.refs_2_
  41.7 3.9 %collective-permute-done.1.refs_1_.refs_0_ = bf16[56,1280]{1,0:T(8,128)(2,1)S(1)} collective-permute-done((bf16[56,1280]{1,0:T(8,128)(2,1)S(1)}, bf16[56,1280]{1,0:T(8,128)(2,1)S(1)}, u32[]{:S(2)}, u32[]{:S(2)}) %collective-permute-start.1) | collective-permute-done | bytes 143392 | tf_op jit(solution)/shard_map/ppermute | solution.py:414
  45.6 0.0 all-to-all-done.1
  45.6 0.0 copy-start.7
  45.6 0.9 copy-done.7
  46.5 0.0 copy-start.1
  46.5 0.0 copy-start.2
  46.5 1.1 shard_map.121
  47.6 5.0 %all-to-all-start.2 = ((bf16[8,32,128]{2,1,0:T(8,128)(2,1)}), bf16[8,32,128]{2,1,0:T(8,128)(2,1)S(1)}, u32[]{:S(2)}, u32[]{:S(2)}) async-start(bf16[8,32,128]{2,1,0:T(8,128)(2,1)} %shard_map.121), calls=%async_computation.2 | async-start | bytes 131072 | tf_op jit(solution)/shard_map/all_to_all | solution.py:85
  52.7 0.0 copy-done.5
  52.7 0.2 shard_map.122.residual_ref
  52.9 2.8 %all-to-all-done.2.parts_ref = bf16[8,32,128]{2,1,0:T(8,128)(2,1)S(1)} async-done(((bf16[8,32,128]{2,1,0:T(8,128)(2,1)}), bf16[8,32,128]{2,1,0:T(8,128)(2,1)S(1)}, u32[]{:S(2)}, u32[]{:S(2)}) %all-to-all-start.2) | async-done | bytes 65568 | tf_op jit(solution)/shard_map/all_to_all | solution.py:85
  55.7 0.7 shard_map.123
  56.3 0.0 copy-start.8
  56.3 0.0 copy-start.9
  56.3 9.4 %all-to-all-start.3 = ((bf16[16,32,128]{2,1,0:T(8,128)(2,1)}), bf16[16,32,128]{2,1,0:T(8,128)(2,1)S(1)}, u32[]{:S(2)}, u32[]{:S(2)}) async-start(bf16[16,32,128]{2,1,0:T(8,128)(2,1)} %shard_map.123), calls=%async_computation.3 | async-start | bytes 262144 | tf_op jit(solution)/shard_map/all_to_all | solution.py:85
  65.8 0.0 copy-done.1
  65.8 1.9 %collective-permute-start.3 = (bf16[3584,128]{1,0:T(8,128)(2,1)S(1)}, bf16[3584,128]{1,0:T(8,128)(2,1)}, u32[]{:S(2)}, u32[]{:S(2)}) collective-permute-start(bf16[3584,128]{1,0:T(8,128)(2,1)S(1)} %bitcast.11), channel_id=1, source_target_pairs={{0,256},{256,0},{1,257},{257,1},{2,258},{258,2},{3,259},{259,3},{4... | collective-permute-start | bytes 2752520 | tf_op jit(solution)/shard_map/ppermute | solution.py:431
  67.7 0.0 copy-done.2
  67.7 2.4 %collective-permute-start.4 = (bf16[3584,128]{1,0:T(8,128)(2,1)S(1)}, bf16[3584,128]{1,0:T(8,128)(2,1)}, u32[]{:S(2)}, u32[]{:S(2)}) collective-permute-start(bf16[3584,128]{1,0:T(8,128)(2,1)S(1)} %bitcast.13), channel_id=1, source_target_pairs={{0,256},{256,0},{1,257},{257,1},{2,258},{258,2},{3,259},{259,3},{4... | collective-permute-start | bytes 2752520 | tf_op jit(solution)/shard_map/ppermute | solution.py:431
  70.1 0.0 copy-done.3
  70.2 1.9 %collective-permute-start.5 = (bf16[128,3584]{1,0:T(8,128)(2,1)S(1)}, bf16[128,3584]{1,0:T(8,128)(2,1)}, u32[]{:S(2)}, u32[]{:S(2)}) collective-permute-start(bf16[128,3584]{1,0:T(8,128)(2,1)S(1)} %bitcast.15), channel_id=1, source_target_pairs={{0,256},{256,0},{1,257},{257,1},{2,258},{258,2},{3,259},{259,3},{4... | collective-permute-start | bytes 2752520 | tf_op jit(solution)/shard_map/ppermute | solution.py:431
  72.1 0.0 copy-done.8
  72.1 0.0 copy-done.9
  72.1 0.4 shard_map.124
  72.5 3.8 %all-to-all-done.3.parts_ref = bf16[16,32,128]{2,1,0:T(8,128)(2,1)S(1)} async-done(((bf16[16,32,128]{2,1,0:T(8,128)(2,1)}), bf16[16,32,128]{2,1,0:T(8,128)(2,1)S(1)}, u32[]{:S(2)}, u32[]{:S(2)}) %all-to-all-start.3) | async-done | bytes 131104 | tf_op jit(solution)/shard_map/all_to_all | solution.py:85
  76.3 1.0 shard_map.125
  77.3 0.0 copy-start.10
  77.3 6.3 %all-to-all-start.4 = ((bf16[16,16,896]{2,1,0:T(8,128)(2,1)}), bf16[16,16,896]{2,1,0:T(8,128)(2,1)S(1)}, u32[]{:S(2)}, u32[]{:S(2)}) async-start(bf16[16,16,896]{2,1,0:T(8,128)(2,1)} %shard_map.125), calls=%async_computation.4 | async-start | bytes 917504 | tf_op jit(solution)/shard_map/all_to_all | solution.py:85
  83.6 0.0 copy-done.10
  83.7 0.0 collective-permute-done.3.refs_3_
  83.7 0.0 collective-permute-done.4.refs_4_
  83.7 0.0 collective-permute-done.5.refs_5_
  83.7 7.5 %all-to-all-done.4.arrived_ref = bf16[16,16,896]{2,1,0:T(8,128)(2,1)S(1)} async-done(((bf16[16,16,896]{2,1,0:T(8,128)(2,1)}), bf16[16,16,896]{2,1,0:T(8,128)(2,1)S(1)}, u32[]{:S(2)}, u32[]{:S(2)}) %all-to-all-start.4) | async-done | bytes 458784 | tf_op jit(solution)/shard_map/all_to_all | solution.py:85
  91.1 2.9 %shard_map.126 = bf16[16,16,896]{2,1,0:T(8,128)(2,1)S(1)} custom-call(bf16[16,16,896]{2,1,0:T(8,128)(2,1)S(1)} %all-to-all-done.4.arrived_ref, f32[4,1,896]{2,1,0:T(1,128)S(1)} %reshape.18.gain_ref, f32[64,128]{1,0:T(8,128)S(1)} %get-tuple-element.23.slots_ref, bf16[3584,128]{1,0:T(8,128)(2,1)S(1)} %bitcast.12, bf16[3584,128]{1,0:T(8,128)(2,1)S(1)} %bitcast.14, ...), custom_call_target="tpu_custom_call" | custom-call | tf_op jit(solution)/shard_map/pallas_call | solution.py:74
  94.0 12.1 %all_to_all.35.parts_ref = bf16[16,16,896]{2,1,0:T(8,128)(2,1)S(1)} all-to-all(bf16[16,16,896]{2,1,0:T(8,128)(2,1)S(1)} %shard_map.126), channel_id=1, replica_groups={{130,131,128,129,194,195,192,193,2,3,0,1,66,67,64,65},{134,135,132,133,..., dimensions={0} | all-to-all | bytes 917504 | tf_op jit(solution)/shard_map/all_to_all | solution.py:85
  106.1 0.2 shard_map.127
  106.3 17.2 %all_to_all.36 = bf16[16,32,128]{2,1,0:T(8,128)(2,1)S(1)} all-to-all(bf16[16,32,128]{2,1,0:T(8,128)(2,1)S(1)} %shard_map.127), channel_id=1, replica_groups={{32,36,40,44,48,52,56,60,0,4,8,12,16,20,24,28},{33,37,41,45,49,53,57,61..., dimensions={0} | all-to-all | bytes 262144 | tf_op jit(solution)/shard_map/all_to_all | solution.py:85
  123.5 0.9 shard_map.128
  (1 shorter events, 0.0 us)
Async XLA Ops:
  2.9 6.1 %copy-start.4 = (bf16[56,1024]{1,0:T(8,128)(2,1)S(1)}, bf16[56,1024]{1,0:T(8,128)(2,1)}, u32[]{:S(2)}) copy-start(bf16[56,1024]{1,0:T(8,128)(2,1)} %refs_1_) | copy-start | bytes 344068
  2.9 8.7 %all-to-all-start = ((bf16[8,8,512]{2,1,0:T(8,128)(2,1)}), bf16[8,8,512]{2,1,0:T(8,128)(2,1)S(1)}, u32[]{:S(2)}, u32[]{:S(2)}) async-start(bf16[8,8,512]{2,1,0:T(8,128)(2,1)} %bitcast.22), calls=%async_computation | async-start | bytes 131072 | tf_op jit(solution)/shard_map/all_to_all | solution.py:85
  9.0 1.2 copy-start
  10.4 0.7 copy-start.6
  11.6 58.6 %copy-start.3 = (bf16[1,128,3584]{2,1,0:T(8,128)(2,1)S(1)}, bf16[1,128,3584]{2,1,0:T(8,128)(2,1)}, u32[]{:S(2)}) copy-start(bf16[1,128,3584]{2,1,0:T(8,128)(2,1)} %param.23) | copy-start | bytes 2752516
  12.6 19.0 %copy-start.11 = (bf16[56,1280]{1,0:T(8,128)(2,1)S(1)}, bf16[56,1280]{1,0:T(8,128)(2,1)}, u32[]{:S(2)}) copy-start(bf16[56,1280]{1,0:T(8,128)(2,1)} %get-tuple-element.21) | copy-start | bytes 430084
  12.6 40.0 %copy-start.5 = (bf16[56,512]{1,0:T(8,128)(2,1)S(1)}, bf16[56,512]{1,0:T(8,128)(2,1)}, u32[]{:S(2)}) copy-start(bf16[56,512]{1,0:T(8,128)(2,1)} %own_ref.1) | copy-start | bytes 172036
  12.6 33.0 %all-to-all-start.1 = ((bf16[16,8,1024]{2,1,0:T(8,128)(2,1)}), bf16[16,8,1024]{2,1,0:T(8,128)(2,1)S(1)}, u32[]{:S(2)}, u32[]{:S(2)}) async-start(bf16[16,8,1024]{2,1,0:T(8,128)(2,1)} %shard_map.120), calls=%async_computation.1 | async-start | bytes 524288 | tf_op jit(solution)/shard_map/all_to_all | solution.py:85
  31.6 7.0 %collective-permute-start = (bf16[56,1280]{1,0:T(8,128)(2,1)S(1)}, bf16[56,1280]{1,0:T(8,128)(2,1)S(1)}, u32[]{:S(2)}, u32[]{:S(2)}) collective-permute-start(bf16[56,1280]{1,0:T(8,128)(2,1)S(1)} %copy-done.11), channel_id=1, source_target_pairs={{0,64},{64,128},{128,192},{192,0},{1,65},{65,129},{129,193},{193,1... | collective-permute-start | bytes 430088 | tf_op jit(solution)/shard_map/ppermute | solution.py:413
  34.7 7.0 %collective-permute-start.2 = (bf16[56,1280]{1,0:T(8,128)(2,1)S(1)}, bf16[56,1280]{1,0:T(8,128)(2,1)S(1)}, u32[]{:S(2)}, u32[]{:S(2)}) collective-permute-start(bf16[56,1280]{1,0:T(8,128)(2,1)S(1)} %copy-done.11), channel_id=1, source_target_pairs={{0,192},{64,0},{128,64},{192,128},{1,193},{65,1},{129,65},{193,129... | collective-permute-start | bytes 430088 | tf_op jit(solution)/shard_map/ppermute | solution.py:414
  38.6 7.0 %collective-permute-start.1 = (bf16[56,1280]{1,0:T(8,128)(2,1)S(1)}, bf16[56,1280]{1,0:T(8,128)(2,1)S(1)}, u32[]{:S(2)}, u32[]{:S(2)}) collective-permute-start(bf16[56,1280]{1,0:T(8,128)(2,1)S(1)} %collective-permute-done.refs_2_.refs_1_), channel_id=1, source_target_pairs={{0,64},{64,128},{128,192},{192,0},{1,65},{65,129},{129,193},{193,1... | collective-permute-start | bytes 430088 | tf_op jit(solution)/shard_map/ppermute | solution.py:414
  45.6 0.9 copy-start.7
  46.5 19.3 %copy-start.1 = (bf16[1,3584,128]{2,1,0:T(8,128)(2,1)S(1)}, bf16[1,3584,128]{2,1,0:T(8,128)(2,1)}, u32[]{:S(2)}) copy-start(bf16[1,3584,128]{2,1,0:T(8,128)(2,1)} %param.21) | copy-start | bytes 2752516
  46.5 21.2 %copy-start.2 = (bf16[1,3584,128]{2,1,0:T(8,128)(2,1)S(1)}, bf16[1,3584,128]{2,1,0:T(8,128)(2,1)}, u32[]{:S(2)}) copy-start(bf16[1,3584,128]{2,1,0:T(8,128)(2,1)} %param.22) | copy-start | bytes 2752516
  47.6 8.0 %all-to-all-start.2 = ((bf16[8,32,128]{2,1,0:T(8,128)(2,1)}), bf16[8,32,128]{2,1,0:T(8,128)(2,1)S(1)}, u32[]{:S(2)}, u32[]{:S(2)}) async-start(bf16[8,32,128]{2,1,0:T(8,128)(2,1)} %shard_map.121), calls=%async_computation.2 | async-start | bytes 131072 | tf_op jit(solution)/shard_map/all_to_all | solution.py:85
  56.3 15.8 %copy-start.8 = (s32[512,8]{0,1:T(8,128)S(1)}, s32[512,8]{0,1:T(8,128)}, u32[]{:S(2)}) copy-start(s32[512,8]{0,1:T(8,128)} %param.19) | copy-start | bytes 49156
  56.3 15.8 %copy-start.9 = (f32[512,8]{0,1:T(8,128)S(1)}, f32[512,8]{0,1:T(8,128)}, u32[]{:S(2)}) copy-start(f32[512,8]{0,1:T(8,128)} %param.20) | copy-start | bytes 49156
  56.3 19.9 %all-to-all-start.3 = ((bf16[16,32,128]{2,1,0:T(8,128)(2,1)}), bf16[16,32,128]{2,1,0:T(8,128)(2,1)S(1)}, u32[]{:S(2)}, u32[]{:S(2)}) async-start(bf16[16,32,128]{2,1,0:T(8,128)(2,1)} %shard_map.123), calls=%async_computation.3 | async-start | bytes 262144 | tf_op jit(solution)/shard_map/all_to_all | solution.py:85
  65.8 17.9 %collective-permute-start.3 = (bf16[3584,128]{1,0:T(8,128)(2,1)S(1)}, bf16[3584,128]{1,0:T(8,128)(2,1)}, u32[]{:S(2)}, u32[]{:S(2)}) collective-permute-start(bf16[3584,128]{1,0:T(8,128)(2,1)S(1)} %bitcast.11), channel_id=1, source_target_pairs={{0,256},{256,0},{1,257},{257,1},{2,258},{258,2},{3,259},{259,3},{4... | collective-permute-start | bytes 2752520 | tf_op jit(solution)/shard_map/ppermute | solution.py:431
  67.7 15.9 %collective-permute-start.4 = (bf16[3584,128]{1,0:T(8,128)(2,1)S(1)}, bf16[3584,128]{1,0:T(8,128)(2,1)}, u32[]{:S(2)}, u32[]{:S(2)}) collective-permute-start(bf16[3584,128]{1,0:T(8,128)(2,1)S(1)} %bitcast.13), channel_id=1, source_target_pairs={{0,256},{256,0},{1,257},{257,1},{2,258},{258,2},{3,259},{259,3},{4... | collective-permute-start | bytes 2752520 | tf_op jit(solution)/shard_map/ppermute | solution.py:431
  70.2 13.5 %collective-permute-start.5 = (bf16[128,3584]{1,0:T(8,128)(2,1)S(1)}, bf16[128,3584]{1,0:T(8,128)(2,1)}, u32[]{:S(2)}, u32[]{:S(2)}) collective-permute-start(bf16[128,3584]{1,0:T(8,128)(2,1)S(1)} %bitcast.15), channel_id=1, source_target_pairs={{0,256},{256,0},{1,257},{257,1},{2,258},{258,2},{3,259},{259,3},{4... | collective-permute-start | bytes 2752520 | tf_op jit(solution)/shard_map/ppermute | solution.py:431
  77.3 6.3 %copy-start.10 = (f32[3584]{0:T(1024)S(1)}, f32[3584]{0:T(1024)}, u32[]{:S(2)}) copy-start(f32[3584]{0:T(1024)} %param.18) | copy-start | bytes 43012
  77.3 13.8 %all-to-all-start.4 = ((bf16[16,16,896]{2,1,0:T(8,128)(2,1)}), bf16[16,16,896]{2,1,0:T(8,128)(2,1)S(1)}, u32[]{:S(2)}, u32[]{:S(2)}) async-start(bf16[16,16,896]{2,1,0:T(8,128)(2,1)} %shard_map.125), calls=%async_computation.4 | async-start | bytes 917504 | tf_op jit(solution)/shard_map/all_to_all | solution.py:85

commit v7 on v6

--- a/solution.py
+++ b/solution.py
@@ -85,50 +85,34 @@
     return lax.all_to_all(chunks, axes, 0, 0, tiled=True, axis_index_groups=[order])
 
 
+def whole(dims):
+    return pl.BlockSpec(dims, lambda i: (0,) * len(dims))
+
+
 def shape(dims, dtype=BF16):
     return jax.ShapeDtypeStruct(dims, dtype)
 
 
 def attend_kernel(
-    length_ref,
-    query_hbm,
-    cache_hbm,
-    weight_hbm,
-    residual_hbm,
-    out_ref,
-    payload_hbm,
-    query_ref,
-    cache_ref,
-    sems,
+    length_ref, query_ref, cache_ref, weight_ref, residual_ref, out_ref, payload_ref
 ):
-    depth = weight_hbm.shape[1]
-    span = residual_hbm.shape[1] // ROLE
+    depth = weight_ref.shape[1]
+    span = residual_ref.shape[1] // ROLE
     start = pl.multiple_of(lax.axis_index("role") * span, span)
-    copies = [
-        pltpu.make_async_copy(cache_hbm.at[0], cache_ref, sems.at[0]),
-        pltpu.make_async_copy(query_hbm.at[0], query_ref, sems.at[1]),
-        pltpu.make_async_copy(weight_hbm, payload_hbm.at[:, pl.ds(0, depth)], sems.at[2]),
-        pltpu.make_async_copy(
-            residual_hbm.at[:, pl.ds(start, span)], payload_hbm.at[:, pl.ds(depth, span)], sems.at[3]
-        ),
-    ]
-    for copy in copies:
-        copy.start()
-    copies[0].wait()
-    copies[1].wait()
-    scores = nn_dot(query_ref[...], cache_ref[...]) * SOFTMAX_SCALE
+    payload_ref[:, :depth] = weight_ref[...]
+    payload_ref[:, depth:] = residual_ref[:, pl.ds(start, span)]
+    cache = cache_ref[0]
+    scores = nn_dot(query_ref[0], cache) * SOFTMAX_SCALE
     visible = lax.broadcasted_iota(jnp.int32, scores.shape, 1) < length_ref[0]
     scores = jnp.where(visible, scores, -1e30)
     row_max = jnp.max(scores, axis=1, keepdims=True)
     weights = jnp.where(visible, jnp.exp(scores - row_max), 0.0)
     row_total = jnp.sum(weights, axis=1, keepdims=True)
-    summed = nt_dot(weights.astype(BF16), cache_ref[:LAT])
+    summed = nt_dot(weights.astype(BF16), cache[:LAT])
     attended = summed / row_total
     heads = attended.shape[0] // MEMBERS
     attended = [attended[i * heads : (i + 1) * heads] for i in HEAD_ORDER]
     out_ref[...] = jnp.concatenate(attended, axis=0).astype(BF16)
-    for copy in copies[2:]:
-        copy.wait()
 
 
 def value_kernel(att_ref, value_ref, out_ref):
@@ -380,27 +364,18 @@
     heads = queries.shape[1]
     own_heads = heads // MEMBERS
     width = output_weight.shape[1] + residual.shape[1] // ROLE
-    attended, payload = local_call(
+    cache = latent_cache.swapaxes(1, 2)
+    attended, payload = pl.pallas_call(
         attend_kernel,
-        (shape((heads, LAT)), shape((COLS, width))),
-        lengths,
-        queries,
-        latent_cache.swapaxes(1, 2),
-        output_weight,
-        residual,
-        scratch=(
-            pltpu.VMEM(queries.shape[1:], BF16),
-            pltpu.VMEM(latent_cache.shape[:0:-1], BF16),
-            pltpu.SemaphoreType.DMA((4,)),
-        ),
-        smem=(0,),
-        hbm=(1, 2, 3, 4),
-        vmem=ALL_VMEM,
-    )
-    attended, late_value, late_weight = lax.optimization_barrier(
-        (attended, value_up, output_weight)
-    )
-    value_blocks, weight_rows = preload(late_value, late_weight)
+        grid=(1,),
+        out_shape=(shape((heads, LAT)), shape((COLS, width))),
+        in_specs=[pl.BlockSpec(memory_space=pltpu.SMEM)]
+        + [whole(array.shape) for array in (queries, cache, output_weight, residual)],
+        out_specs=(whole((heads, LAT)), whole((COLS, width))),
+        compiler_params=pltpu.CompilerParams(vmem_limit_bytes=ALL_VMEM),
+    )(lengths, queries, cache, output_weight, residual)
+    attended, late_value = lax.optimization_barrier((attended, value_up))
+    (value_blocks,) = preload(late_value)
     attended = attended.reshape(MEMBERS, own_heads, LAT)
     regrouped = exchange(attended, ("role", "tp"), HEAD_ORDER)
     values = local_call(
@@ -417,7 +392,7 @@
         project_kernel,
         shape((MEMBERS, 32, 128)),
         gathered.reshape(Z * MEMBERS, own_heads * 128),
-        weight_rows,
+        output_weight,
         *payloads,
     )
     residual_tile = local_call(

time: 125 us -> 125 us (level)
    pallas_call x11 -> x10, Pallas kernels: 10.8 us -> 8.44 us  [local_call(): pl.pallas_call(body, out_shape=out_shape, in_specs=[pl.BlockSpec(memory_s...]
    pallas_call x0 -> x1, Pallas kernels: none -> 2.15 us  [shards(): pl.pallas_call(attend_kernel, grid=(1,), out_shape=(shape((heads, LAT)),...]
    unnamed x24 -> x20, local copies, waits for them, and re-layouts: 2.8 us -> 2.15 us
  transfers between devices with their start and end apart: 11 -> 11, of which waited for: 6 -> 6; matrix products, arithmetic and copies ran while one was open for 0% -> 0% of each run, Pallas kernels for 2% -> 1%
where the time goes in v7:
time: 125 us; the launch traced here: 124 us
  starting transfers between devices  60.9 us (49%)
  blocking collectives  29.3 us (23%)
  waiting for transfers between devices  20.4 us (16%)
  Pallas kernels  10.6 us (8%)
  local copies, waits for them, and re-layouts  2.17 us (2%)
    all_to_all x5, starting transfers between devices, exchange(): lax.all_to_all(chunks, axes, 0, 0, tiled=True, axis_index_groups=[order])  45.7 us
    all_to_all x2, blocking collectives, exchange(): lax.all_to_all(chunks, axes, 0, 0, tiled=True, axis_index_groups=[order])  29.3 us
    all_to_all x5, waiting for transfers between devices, exchange(): lax.all_to_all(chunks, axes, 0, 0, tiled=True, axis_index_groups=[order])  15.4 us
    pallas_call x10, Pallas kernels, local_call(): pl.pallas_call(body, out_shape=out_shape, in_specs=[pl.BlockSpec(memory_s...  8.44 us
    ppermute x3, starting transfers between devices, shards(): peer_expert = [lax.ppermute(weight, 'role', swap) for weight in own_expert]  6.25 us
    ppermute x1, waiting for transfers between devices, shards(): lax.ppermute(near, 'x', right)  3.87 us
    ppermute x1, starting transfers between devices, shards(): near = lax.ppermute(payload, 'x', right)  3.11 us
    ppermute x1, starting transfers between devices, shards(): lax.ppermute(near, 'x', right)  3.09 us
  transfers between devices with their start and end apart: 11, of which 6 were waited for; matrix products, arithmetic and copies ran while one was open for 0% of the time, Pallas kernels for 1%

profile of v7, /device:TPU:4, one launch (start us, length us, event | category | flops | bytes accessed | tf_op | source)
XLA Modules:
  0.0 124.1 jit_solution(15008295287733889725)
XLA Ops:
  0.7 2.2 %shard_map.118 = (bf16[64,512]{1,0:T(8,128)(2,1)}, bf16[56,1280]{1,0:T(8,128)(2,1)}) custom-call(s32[1]{0:T(128)S(6)} %copy.13.length_ref, bf16[1,64,576]{2,1,0:T(8,128)(2,1)} %query_ref.1, bf16[1,576,384]{2,1,0:T(8,128)(2,1)} %bitcast.21, bf16[56,1024]{1,0:T(8,128)(2,1)} %refs_0_.2, bf16[56,512]{1,0:T(8,128)(2,1)} %own_ref.1), custom_call_target="tpu_custom_call" | custom-call | tf_op jit(solution)/shard_map/pallas_call | solution.py:368
  2.8 5.9 %all-to-all-start = ((bf16[8,8,512]{2,1,0:T(8,128)(2,1)}), bf16[8,8,512]{2,1,0:T(8,128)(2,1)S(1)}, u32[]{:S(2)}, u32[]{:S(2)}) async-start(bf16[8,8,512]{2,1,0:T(8,128)(2,1)} %bitcast.22), calls=%async_computation | async-start | bytes 131072 | tf_op jit(solution)/shard_map/all_to_all | solution.py:85
  8.7 0.0 copy-start
  8.7 1.2 copy-done
  10.0 0.1 shard_map.119.value_ref
  10.1 1.3 %all-to-all-done = bf16[8,8,512]{2,1,0:T(8,128)(2,1)S(1)} async-done(((bf16[8,8,512]{2,1,0:T(8,128)(2,1)}), bf16[8,8,512]{2,1,0:T(8,128)(2,1)S(1)}, u32[]{:S(2)}, u32[]{:S(2)}) %all-to-all-start) | async-done | bytes 65568 | tf_op jit(solution)/shard_map/all_to_all | solution.py:85
  11.4 0.0 copy-start.3
  11.4 1.0 shard_map.120
  12.4 0.0 copy-start.9
  12.4 0.0 copy-start.5
  12.4 19.0 %all-to-all-start.1 = ((bf16[16,8,1024]{2,1,0:T(8,128)(2,1)}), bf16[16,8,1024]{2,1,0:T(8,128)(2,1)S(1)}, u32[]{:S(2)}, u32[]{:S(2)}) async-start(bf16[16,8,1024]{2,1,0:T(8,128)(2,1)} %shard_map.120), calls=%async_computation.1 | async-start | bytes 524288 | tf_op jit(solution)/shard_map/all_to_all | solution.py:85
  31.4 0.0 copy-done.9
  31.4 3.1 %collective-permute-start = (bf16[56,1280]{1,0:T(8,128)(2,1)S(1)}, bf16[56,1280]{1,0:T(8,128)(2,1)S(1)}, u32[]{:S(2)}, u32[]{:S(2)}) collective-permute-start(bf16[56,1280]{1,0:T(8,128)(2,1)S(1)} %copy-done.9), channel_id=1, source_target_pairs={{0,64},{64,128},{128,192},{192,0},{1,65},{65,129},{129,193},{193,1... | collective-permute-start | bytes 430088 | tf_op jit(solution)/shard_map/ppermute | solution.py:388
  34.5 2.7 %collective-permute-start.2 = (bf16[56,1280]{1,0:T(8,128)(2,1)S(1)}, bf16[56,1280]{1,0:T(8,128)(2,1)S(1)}, u32[]{:S(2)}, u32[]{:S(2)}) collective-permute-start(bf16[56,1280]{1,0:T(8,128)(2,1)S(1)} %copy-done.9), channel_id=1, source_target_pairs={{0,192},{64,0},{128,64},{192,128},{1,193},{65,1},{129,65},{193,129... | collective-permute-start | bytes 430088 | tf_op jit(solution)/shard_map/ppermute | solution.py:389
  37.2 1.1 collective-permute-done.refs_2_.refs_1_
  38.4 3.1 %collective-permute-start.1 = (bf16[56,1280]{1,0:T(8,128)(2,1)S(1)}, bf16[56,1280]{1,0:T(8,128)(2,1)S(1)}, u32[]{:S(2)}, u32[]{:S(2)}) collective-permute-start(bf16[56,1280]{1,0:T(8,128)(2,1)S(1)} %collective-permute-done.refs_2_.refs_1_), channel_id=1, source_target_pairs={{0,64},{64,128},{128,192},{192,0},{1,65},{65,129},{129,193},{193,1... | collective-permute-start | bytes 430088 | tf_op jit(solution)/shard_map/ppermute | solution.py:389
  41.5 0.0 collective-permute-done.2.refs_3_.refs_2_
  41.5 3.9 %collective-permute-done.1.refs_1_.refs_0_ = bf16[56,1280]{1,0:T(8,128)(2,1)S(1)} collective-permute-done((bf16[56,1280]{1,0:T(8,128)(2,1)S(1)}, bf16[56,1280]{1,0:T(8,128)(2,1)S(1)}, u32[]{:S(2)}, u32[]{:S(2)}) %collective-permute-start.1) | collective-permute-done | bytes 143392 | tf_op jit(solution)/shard_map/ppermute | solution.py:389
  45.4 0.0 all-to-all-done.1
  45.4 0.0 copy-start.4
  45.4 0.9 copy-done.4
  46.3 0.0 copy-start.1
  46.3 0.0 copy-start.2
  46.3 1.1 shard_map.121
  47.4 5.1 %all-to-all-start.2 = ((bf16[8,32,128]{2,1,0:T(8,128)(2,1)}), bf16[8,32,128]{2,1,0:T(8,128)(2,1)S(1)}, u32[]{:S(2)}, u32[]{:S(2)}) async-start(bf16[8,32,128]{2,1,0:T(8,128)(2,1)} %shard_map.121), calls=%async_computation.2 | async-start | bytes 131072 | tf_op jit(solution)/shard_map/all_to_all | solution.py:85
  52.4 0.0 copy-done.5
  52.4 0.2 shard_map.122.residual_ref
  52.7 2.8 %all-to-all-done.2.parts_ref = bf16[8,32,128]{2,1,0:T(8,128)(2,1)S(1)} async-done(((bf16[8,32,128]{2,1,0:T(8,128)(2,1)}), bf16[8,32,128]{2,1,0:T(8,128)(2,1)S(1)}, u32[]{:S(2)}, u32[]{:S(2)}) %all-to-all-start.2) | async-done | bytes 65568 | tf_op jit(solution)/shard_map/all_to_all | solution.py:85
  55.4 0.7 shard_map.123
  56.1 0.0 copy-start.6
  56.1 0.0 copy-start.7
  56.1 9.4 %all-to-all-start.3 = ((bf16[16,32,128]{2,1,0:T(8,128)(2,1)}), bf16[16,32,128]{2,1,0:T(8,128)(2,1)S(1)}, u32[]{:S(2)}, u32[]{:S(2)}) async-start(bf16[16,32,128]{2,1,0:T(8,128)(2,1)} %shard_map.123), calls=%async_computation.3 | async-start | bytes 262144 | tf_op jit(solution)/shard_map/all_to_all | solution.py:85
  65.5 0.0 copy-done.1
  65.5 1.9 %collective-permute-start.3 = (bf16[3584,128]{1,0:T(8,128)(2,1)S(1)}, bf16[3584,128]{1,0:T(8,128)(2,1)}, u32[]{:S(2)}, u32[]{:S(2)}) collective-permute-start(bf16[3584,128]{1,0:T(8,128)(2,1)S(1)} %bitcast.11), channel_id=1, source_target_pairs={{0,256},{256,0},{1,257},{257,1},{2,258},{258,2},{3,259},{259,3},{4... | collective-permute-start | bytes 2752520 | tf_op jit(solution)/shard_map/ppermute | solution.py:406
  67.5 0.0 copy-done.2
  67.5 2.4 %collective-permute-start.4 = (bf16[3584,128]{1,0:T(8,128)(2,1)S(1)}, bf16[3584,128]{1,0:T(8,128)(2,1)}, u32[]{:S(2)}, u32[]{:S(2)}) collective-permute-start(bf16[3584,128]{1,0:T(8,128)(2,1)S(1)} %bitcast.13), channel_id=1, source_target_pairs={{0,256},{256,0},{1,257},{257,1},{2,258},{258,2},{3,259},{259,3},{4... | collective-permute-start | bytes 2752520 | tf_op jit(solution)/shard_map/ppermute | solution.py:406
  69.9 0.0 copy-done.3
  69.9 1.9 %collective-permute-start.5 = (bf16[128,3584]{1,0:T(8,128)(2,1)S(1)}, bf16[128,3584]{1,0:T(8,128)(2,1)}, u32[]{:S(2)}, u32[]{:S(2)}) collective-permute-start(bf16[128,3584]{1,0:T(8,128)(2,1)S(1)} %bitcast.15), channel_id=1, source_target_pairs={{0,256},{256,0},{1,257},{257,1},{2,258},{258,2},{3,259},{259,3},{4... | collective-permute-start | bytes 2752520 | tf_op jit(solution)/shard_map/ppermute | solution.py:406
  71.8 0.0 copy-done.6
  71.8 0.0 copy-done.7
  71.9 0.4 shard_map.124
  72.3 3.8 %all-to-all-done.3.parts_ref = bf16[16,32,128]{2,1,0:T(8,128)(2,1)S(1)} async-done(((bf16[16,32,128]{2,1,0:T(8,128)(2,1)}), bf16[16,32,128]{2,1,0:T(8,128)(2,1)S(1)}, u32[]{:S(2)}, u32[]{:S(2)}) %all-to-all-start.3) | async-done | bytes 131104 | tf_op jit(solution)/shard_map/all_to_all | solution.py:85
  76.1 1.0 shard_map.125
  77.1 0.0 copy-start.8
  77.1 6.3 %all-to-all-start.4 = ((bf16[16,16,896]{2,1,0:T(8,128)(2,1)}), bf16[16,16,896]{2,1,0:T(8,128)(2,1)S(1)}, u32[]{:S(2)}, u32[]{:S(2)}) async-start(bf16[16,16,896]{2,1,0:T(8,128)(2,1)} %shard_map.125), calls=%async_computation.4 | async-start | bytes 917504 | tf_op jit(solution)/shard_map/all_to_all | solution.py:85
  83.4 0.0 copy-done.8
  83.4 0.0 collective-permute-done.3.refs_3_
  83.4 0.0 collective-permute-done.4.refs_4_
  83.4 0.0 collective-permute-done.5.refs_5_
  83.4 7.5 %all-to-all-done.4.arrived_ref = bf16[16,16,896]{2,1,0:T(8,128)(2,1)S(1)} async-done(((bf16[16,16,896]{2,1,0:T(8,128)(2,1)}), bf16[16,16,896]{2,1,0:T(8,128)(2,1)S(1)}, u32[]{:S(2)}, u32[]{:S(2)}) %all-to-all-start.4) | async-done | bytes 458784 | tf_op jit(solution)/shard_map/all_to_all | solution.py:85
  90.9 2.8 %shard_map.126 = bf16[16,16,896]{2,1,0:T(8,128)(2,1)S(1)} custom-call(bf16[16,16,896]{2,1,0:T(8,128)(2,1)S(1)} %all-to-all-done.4.arrived_ref, f32[4,1,896]{2,1,0:T(1,128)S(1)} %reshape.18.gain_ref, f32[64,128]{1,0:T(8,128)S(1)} %get-tuple-element.17.slots_ref, bf16[3584,128]{1,0:T(8,128)(2,1)S(1)} %bitcast.12, bf16[3584,128]{1,0:T(8,128)(2,1)S(1)} %bitcast.14, ...), custom_call_target="tpu_custom_call" | custom-call | tf_op jit(solution)/shard_map/pallas_call | solution.py:74
  93.7 12.1 %all_to_all.35.parts_ref = bf16[16,16,896]{2,1,0:T(8,128)(2,1)S(1)} all-to-all(bf16[16,16,896]{2,1,0:T(8,128)(2,1)S(1)} %shard_map.126), channel_id=1, replica_groups={{130,131,128,129,194,195,192,193,2,3,0,1,66,67,64,65},{134,135,132,133,..., dimensions={0} | all-to-all | bytes 917504 | tf_op jit(solution)/shard_map/all_to_all | solution.py:85
  105.9 0.2 shard_map.127
  106.0 17.2 %all_to_all.36 = bf16[16,32,128]{2,1,0:T(8,128)(2,1)S(1)} all-to-all(bf16[16,32,128]{2,1,0:T(8,128)(2,1)S(1)} %shard_map.127), channel_id=1, replica_groups={{32,36,40,44,48,52,56,60,0,4,8,12,16,20,24,28},{33,37,41,45,49,53,57,61..., dimensions={0} | all-to-all | bytes 262144 | tf_op jit(solution)/shard_map/all_to_all | solution.py:85
  123.2 0.9 shard_map.128
  (1 shorter events, 0.0 us)
Async XLA Ops:
  2.8 8.6 %all-to-all-start = ((bf16[8,8,512]{2,1,0:T(8,128)(2,1)}), bf16[8,8,512]{2,1,0:T(8,128)(2,1)S(1)}, u32[]{:S(2)}, u32[]{:S(2)}) async-start(bf16[8,8,512]{2,1,0:T(8,128)(2,1)} %bitcast.22), calls=%async_computation | async-start | bytes 131072 | tf_op jit(solution)/shard_map/all_to_all | solution.py:85
  8.7 1.2 copy-start
  11.4 58.5 %copy-start.3 = (bf16[1,128,3584]{2,1,0:T(8,128)(2,1)S(1)}, bf16[1,128,3584]{2,1,0:T(8,128)(2,1)}, u32[]{:S(2)}) copy-start(bf16[1,128,3584]{2,1,0:T(8,128)(2,1)} %param.23) | copy-start | bytes 2752516
  12.4 19.0 %copy-start.9 = (bf16[56,1280]{1,0:T(8,128)(2,1)S(1)}, bf16[56,1280]{1,0:T(8,128)(2,1)}, u32[]{:S(2)}) copy-start(bf16[56,1280]{1,0:T(8,128)(2,1)} %get-tuple-element.15) | copy-start | bytes 430084
  12.4 40.0 %copy-start.5 = (bf16[56,512]{1,0:T(8,128)(2,1)S(1)}, bf16[56,512]{1,0:T(8,128)(2,1)}, u32[]{:S(2)}) copy-start(bf16[56,512]{1,0:T(8,128)(2,1)} %own_ref.1) | copy-start | bytes 172036
  12.4 33.0 %all-to-all-start.1 = ((bf16[16,8,1024]{2,1,0:T(8,128)(2,1)}), bf16[16,8,1024]{2,1,0:T(8,128)(2,1)S(1)}, u32[]{:S(2)}, u32[]{:S(2)}) async-start(bf16[16,8,1024]{2,1,0:T(8,128)(2,1)} %shard_map.120), calls=%async_computation.1 | async-start | bytes 524288 | tf_op jit(solution)/shard_map/all_to_all | solution.py:85
  31.4 7.0 %collective-permute-start = (bf16[56,1280]{1,0:T(8,128)(2,1)S(1)}, bf16[56,1280]{1,0:T(8,128)(2,1)S(1)}, u32[]{:S(2)}, u32[]{:S(2)}) collective-permute-start(bf16[56,1280]{1,0:T(8,128)(2,1)S(1)} %copy-done.9), channel_id=1, source_target_pairs={{0,64},{64,128},{128,192},{192,0},{1,65},{65,129},{129,193},{193,1... | collective-permute-start | bytes 430088 | tf_op jit(solution)/shard_map/ppermute | solution.py:388
  34.5 7.0 %collective-permute-start.2 = (bf16[56,1280]{1,0:T(8,128)(2,1)S(1)}, bf16[56,1280]{1,0:T(8,128)(2,1)S(1)}, u32[]{:S(2)}, u32[]{:S(2)}) collective-permute-start(bf16[56,1280]{1,0:T(8,128)(2,1)S(1)} %copy-done.9), channel_id=1, source_target_pairs={{0,192},{64,0},{128,64},{192,128},{1,193},{65,1},{129,65},{193,129... | collective-permute-start | bytes 430088 | tf_op jit(solution)/shard_map/ppermute | solution.py:389
  38.4 7.0 %collective-permute-start.1 = (bf16[56,1280]{1,0:T(8,128)(2,1)S(1)}, bf16[56,1280]{1,0:T(8,128)(2,1)S(1)}, u32[]{:S(2)}, u32[]{:S(2)}) collective-permute-start(bf16[56,1280]{1,0:T(8,128)(2,1)S(1)} %collective-permute-done.refs_2_.refs_1_), channel_id=1, source_target_pairs={{0,64},{64,128},{128,192},{192,0},{1,65},{65,129},{129,193},{193,1... | collective-permute-start | bytes 430088 | tf_op jit(solution)/shard_map/ppermute | solution.py:389
  45.4 0.9 copy-start.4
  46.3 19.3 %copy-start.1 = (bf16[1,3584,128]{2,1,0:T(8,128)(2,1)S(1)}, bf16[1,3584,128]{2,1,0:T(8,128)(2,1)}, u32[]{:S(2)}) copy-start(bf16[1,3584,128]{2,1,0:T(8,128)(2,1)} %param.21) | copy-start | bytes 2752516
  46.3 21.2 %copy-start.2 = (bf16[1,3584,128]{2,1,0:T(8,128)(2,1)S(1)}, bf16[1,3584,128]{2,1,0:T(8,128)(2,1)}, u32[]{:S(2)}) copy-start(bf16[1,3584,128]{2,1,0:T(8,128)(2,1)} %param.22) | copy-start | bytes 2752516
  47.4 8.1 %all-to-all-start.2 = ((bf16[8,32,128]{2,1,0:T(8,128)(2,1)}), bf16[8,32,128]{2,1,0:T(8,128)(2,1)S(1)}, u32[]{:S(2)}, u32[]{:S(2)}) async-start(bf16[8,32,128]{2,1,0:T(8,128)(2,1)} %shard_map.121), calls=%async_computation.2 | async-start | bytes 131072 | tf_op jit(solution)/shard_map/all_to_all | solution.py:85
  56.1 15.8 %copy-start.6 = (s32[512,8]{0,1:T(8,128)S(1)}, s32[512,8]{0,1:T(8,128)}, u32[]{:S(2)}) copy-start(s32[512,8]{0,1:T(8,128)} %param.19) | copy-start | bytes 49156
  56.1 15.8 %copy-start.7 = (f32[512,8]{0,1:T(8,128)S(1)}, f32[512,8]{0,1:T(8,128)}, u32[]{:S(2)}) copy-start(f32[512,8]{0,1:T(8,128)} %param.20) | copy-start | bytes 49156
  56.1 20.0 %all-to-all-start.3 = ((bf16[16,32,128]{2,1,0:T(8,128)(2,1)}), bf16[16,32,128]{2,1,0:T(8,128)(2,1)S(1)}, u32[]{:S(2)}, u32[]{:S(2)}) async-start(bf16[16,32,128]{2,1,0:T(8,128)(2,1)} %shard_map.123), calls=%async_computation.3 | async-start | bytes 262144 | tf_op jit(solution)/shard_map/all_to_all | solution.py:85
  65.5 17.9 %collective-permute-start.3 = (bf16[3584,128]{1,0:T(8,128)(2,1)S(1)}, bf16[3584,128]{1,0:T(8,128)(2,1)}, u32[]{:S(2)}, u32[]{:S(2)}) collective-permute-start(bf16[3584,128]{1,0:T(8,128)(2,1)S(1)} %bitcast.11), channel_id=1, source_target_pairs={{0,256},{256,0},{1,257},{257,1},{2,258},{258,2},{3,259},{259,3},{4... | collective-permute-start | bytes 2752520 | tf_op jit(solution)/shard_map/ppermute | solution.py:406
  67.5 15.9 %collective-permute-start.4 = (bf16[3584,128]{1,0:T(8,128)(2,1)S(1)}, bf16[3584,128]{1,0:T(8,128)(2,1)}, u32[]{:S(2)}, u32[]{:S(2)}) collective-permute-start(bf16[3584,128]{1,0:T(8,128)(2,1)S(1)} %bitcast.13), channel_id=1, source_target_pairs={{0,256},{256,0},{1,257},{257,1},{2,258},{258,2},{3,259},{259,3},{4... | collective-permute-start | bytes 2752520 | tf_op jit(solution)/shard_map/ppermute | solution.py:406
  69.9 13.5 %collective-permute-start.5 = (bf16[128,3584]{1,0:T(8,128)(2,1)S(1)}, bf16[128,3584]{1,0:T(8,128)(2,1)}, u32[]{:S(2)}, u32[]{:S(2)}) collective-permute-start(bf16[128,3584]{1,0:T(8,128)(2,1)S(1)} %bitcast.15), channel_id=1, source_target_pairs={{0,256},{256,0},{1,257},{257,1},{2,258},{258,2},{3,259},{259,3},{4... | collective-permute-start | bytes 2752520 | tf_op jit(solution)/shard_map/ppermute | solution.py:406
  77.1 6.3 %copy-start.8 = (f32[3584]{0:T(1024)S(1)}, f32[3584]{0:T(1024)}, u32[]{:S(2)}) copy-start(f32[3584]{0:T(1024)} %param.18) | copy-start | bytes 43012
  77.1 13.8 %all-to-all-start.4 = ((bf16[16,16,896]{2,1,0:T(8,128)(2,1)}), bf16[16,16,896]{2,1,0:T(8,128)(2,1)S(1)}, u32[]{:S(2)}, u32[]{:S(2)}) async-start(bf16[16,16,896]{2,1,0:T(8,128)(2,1)} %shard_map.125), calls=%async_computation.4 | async-start | bytes 917504 | tf_op jit(solution)/shard_map/all_to_all | solution.py:85

commit v8 on v7

--- a/solution.py
+++ b/solution.py
@@ -386,7 +386,8 @@
     )
     right, left = ([(i, (i + step) % X) for i in range(X)] for step in (1, X - 1))
     near = lax.ppermute(payload, "x", right)
-    payloads = [lax.ppermute(near, "x", right), near, lax.ppermute(payload, "x", left)]
+    across = lax.ppermute(payload, "x", [(i, (i + 2) % X) for i in range(X)])
+    payloads = [across, near, lax.ppermute(payload, "x", left)]
     gathered = exchange(values, "z", z_order(VALUE_FIRST))
     projected = local_call(
         project_kernel,

time: 125 us -> 125 us (level)
    ppermute x2, starting transfers between devices: 5.83 us -> 4.39 us  [the longest x1 2.42 us: shards(): across = lax.ppermute(payload, 'x', [(i, (i + 2) % X) for i in range(X)])]
  transfers between devices with their start and end apart: 11 -> 11, of which waited for: 6 -> 7; matrix products, arithmetic and copies ran while one was open for 0% -> 0% of each run, Pallas kernels for 1% -> 1%
where the time goes in v8:
time: 125 us; the launch traced here: 124 us
  starting transfers between devices  60.8 us (49%)
  blocking collectives  29.3 us (23%)
  waiting for transfers between devices  20.4 us (16%)
  Pallas kernels  10.6 us (8%)
  local copies, waits for them, and re-layouts  2.17 us (2%)
    all_to_all x5, starting transfers between devices, exchange(): lax.all_to_all(chunks, axes, 0, 0, tiled=True, axis_index_groups=[order])  46.1 us
    all_to_all x2, blocking collectives, exchange(): lax.all_to_all(chunks, axes, 0, 0, tiled=True, axis_index_groups=[order])  29.3 us
    all_to_all x5, waiting for transfers between devices, exchange(): lax.all_to_all(chunks, axes, 0, 0, tiled=True, axis_index_groups=[order])  15.4 us
    pallas_call x10, Pallas kernels, local_call(): pl.pallas_call(body, out_shape=out_shape, in_specs=[pl.BlockSpec(memory_s...  8.45 us
    ppermute x3, starting transfers between devices, shards(): peer_expert = [lax.ppermute(weight, 'role', swap) for weight in own_expert]  6.25 us
    ppermute x1, starting transfers between devices, shards(): near = lax.ppermute(payload, 'x', right)  4 us
  transfers between devices with their start and end apart: 11, of which 7 were waited for; matrix products, arithmetic and copies ran while one was open for 0% of the time, Pallas kernels for 1%

profile of v8, /device:TPU:4, one launch (start us, length us, event | category | flops | bytes accessed | tf_op | source)
XLA Modules:
  0.0 124.1 jit_solution(1213287398189378709)
XLA Ops:
  0.7 2.2 %shard_map.118 = (bf16[64,512]{1,0:T(8,128)(2,1)}, bf16[56,1280]{1,0:T(8,128)(2,1)}) custom-call(s32[1]{0:T(128)S(6)} %copy.13.length_ref, bf16[1,64,576]{2,1,0:T(8,128)(2,1)} %query_ref.1, bf16[1,576,384]{2,1,0:T(8,128)(2,1)} %bitcast.21, bf16[56,1024]{1,0:T(8,128)(2,1)} %refs_0_.2, bf16[56,512]{1,0:T(8,128)(2,1)} %own_ref.1), custom_call_target="tpu_custom_call" | custom-call | tf_op jit(solution)/shard_map/pallas_call | solution.py:368
  2.8 5.9 %all-to-all-start = ((bf16[8,8,512]{2,1,0:T(8,128)(2,1)}), bf16[8,8,512]{2,1,0:T(8,128)(2,1)S(1)}, u32[]{:S(2)}, u32[]{:S(2)}) async-start(bf16[8,8,512]{2,1,0:T(8,128)(2,1)} %bitcast.22), calls=%async_computation | async-start | bytes 131072 | tf_op jit(solution)/shard_map/all_to_all | solution.py:85
  8.7 0.0 copy-start
  8.7 1.2 copy-done
  10.0 0.1 shard_map.119.value_ref
  10.1 1.3 %all-to-all-done = bf16[8,8,512]{2,1,0:T(8,128)(2,1)S(1)} async-done(((bf16[8,8,512]{2,1,0:T(8,128)(2,1)}), bf16[8,8,512]{2,1,0:T(8,128)(2,1)S(1)}, u32[]{:S(2)}, u32[]{:S(2)}) %all-to-all-start) | async-done | bytes 65568 | tf_op jit(solution)/shard_map/all_to_all | solution.py:85
  11.4 0.0 copy-start.3
  11.4 1.0 shard_map.120
  12.4 0.0 copy-start.9
  12.4 0.0 copy-start.5
  12.4 19.0 %all-to-all-start.1 = ((bf16[16,8,1024]{2,1,0:T(8,128)(2,1)}), bf16[16,8,1024]{2,1,0:T(8,128)(2,1)S(1)}, u32[]{:S(2)}, u32[]{:S(2)}) async-start(bf16[16,8,1024]{2,1,0:T(8,128)(2,1)} %shard_map.120), calls=%async_computation.1 | async-start | bytes 524288 | tf_op jit(solution)/shard_map/all_to_all | solution.py:85
  31.4 0.0 copy-done.9
  31.4 2.4 %collective-permute-start = (bf16[56,1280]{1,0:T(8,128)(2,1)S(1)}, bf16[56,1280]{1,0:T(8,128)(2,1)S(1)}, u32[]{:S(2)}, u32[]{:S(2)}) collective-permute-start(bf16[56,1280]{1,0:T(8,128)(2,1)S(1)} %copy-done.9), channel_id=1, source_target_pairs={{0,128},{64,192},{128,0},{192,64},{1,129},{65,193},{129,1},{193,65... | collective-permute-start | bytes 430088 | tf_op jit(solution)/shard_map/ppermute | solution.py:389
  33.8 4.0 %collective-permute-start.1 = (bf16[56,1280]{1,0:T(8,128)(2,1)S(1)}, bf16[56,1280]{1,0:T(8,128)(2,1)S(1)}, u32[]{:S(2)}, u32[]{:S(2)}) collective-permute-start(bf16[56,1280]{1,0:T(8,128)(2,1)S(1)} %copy-done.9), channel_id=1, source_target_pairs={{0,64},{64,128},{128,192},{192,0},{1,65},{65,129},{129,193},{193,1... | collective-permute-start | bytes 430088 | tf_op jit(solution)/shard_map/ppermute | solution.py:388
  37.8 2.0 %collective-permute-start.2 = (bf16[56,1280]{1,0:T(8,128)(2,1)S(1)}, bf16[56,1280]{1,0:T(8,128)(2,1)S(1)}, u32[]{:S(2)}, u32[]{:S(2)}) collective-permute-start(bf16[56,1280]{1,0:T(8,128)(2,1)S(1)} %copy-done.9), channel_id=1, source_target_pairs={{0,192},{64,0},{128,64},{192,128},{1,193},{65,1},{129,65},{193,129... | collective-permute-start | bytes 430088 | tf_op jit(solution)/shard_map/ppermute | solution.py:390
  39.8 1.0 collective-permute-done.refs_1_.refs_0_
  40.8 2.1 %collective-permute-done.1.refs_2_.refs_1_ = bf16[56,1280]{1,0:T(8,128)(2,1)S(1)} collective-permute-done((bf16[56,1280]{1,0:T(8,128)(2,1)S(1)}, bf16[56,1280]{1,0:T(8,128)(2,1)S(1)}, u32[]{:S(2)}, u32[]{:S(2)}) %collective-permute-start.1) | collective-permute-done | bytes 143392 | tf_op jit(solution)/shard_map/ppermute | solution.py:388
  42.9 2.0 %collective-permute-done.2.refs_3_.refs_2_ = bf16[56,1280]{1,0:T(8,128)(2,1)S(1)} collective-permute-done((bf16[56,1280]{1,0:T(8,128)(2,1)S(1)}, bf16[56,1280]{1,0:T(8,128)(2,1)S(1)}, u32[]{:S(2)}, u32[]{:S(2)}) %collective-permute-start.2) | collective-permute-done | bytes 143392 | tf_op jit(solution)/shard_map/ppermute | solution.py:390
  44.9 0.0 all-to-all-done.1
  44.9 0.0 copy-start.4
  44.9 0.9 copy-done.4
  45.8 0.0 copy-start.1
  45.8 0.0 copy-start.2
  45.8 1.1 shard_map.121
  46.9 4.9 %all-to-all-start.2 = ((bf16[8,32,128]{2,1,0:T(8,128)(2,1)}), bf16[8,32,128]{2,1,0:T(8,128)(2,1)S(1)}, u32[]{:S(2)}, u32[]{:S(2)}) async-start(bf16[8,32,128]{2,1,0:T(8,128)(2,1)} %shard_map.121), calls=%async_computation.2 | async-start | bytes 131072 | tf_op jit(solution)/shard_map/all_to_all | solution.py:85
  51.8 0.0 copy-done.5
  51.8 0.2 shard_map.122.residual_ref
  52.1 2.8 %all-to-all-done.2.parts_ref = bf16[8,32,128]{2,1,0:T(8,128)(2,1)S(1)} async-done(((bf16[8,32,128]{2,1,0:T(8,128)(2,1)}), bf16[8,32,128]{2,1,0:T(8,128)(2,1)S(1)}, u32[]{:S(2)}, u32[]{:S(2)}) %all-to-all-start.2) | async-done | bytes 65568 | tf_op jit(solution)/shard_map/all_to_all | solution.py:85
  54.8 0.7 shard_map.123
  55.5 0.0 copy-start.6
  55.5 0.0 copy-start.7
  55.5 10.0 %all-to-all-start.3 = ((bf16[16,32,128]{2,1,0:T(8,128)(2,1)}), bf16[16,32,128]{2,1,0:T(8,128)(2,1)S(1)}, u32[]{:S(2)}, u32[]{:S(2)}) async-start(bf16[16,32,128]{2,1,0:T(8,128)(2,1)} %shard_map.123), calls=%async_computation.3 | async-start | bytes 262144 | tf_op jit(solution)/shard_map/all_to_all | solution.py:85
  65.5 0.0 copy-done.1
  65.5 1.9 %collective-permute-start.3 = (bf16[3584,128]{1,0:T(8,128)(2,1)S(1)}, bf16[3584,128]{1,0:T(8,128)(2,1)}, u32[]{:S(2)}, u32[]{:S(2)}) collective-permute-start(bf16[3584,128]{1,0:T(8,128)(2,1)S(1)} %bitcast.11), channel_id=1, source_target_pairs={{0,256},{256,0},{1,257},{257,1},{2,258},{258,2},{3,259},{259,3},{4... | collective-permute-start | bytes 2752520 | tf_op jit(solution)/shard_map/ppermute | solution.py:407
  67.5 0.0 copy-done.2
  67.5 2.4 %collective-permute-start.4 = (bf16[3584,128]{1,0:T(8,128)(2,1)S(1)}, bf16[3584,128]{1,0:T(8,128)(2,1)}, u32[]{:S(2)}, u32[]{:S(2)}) collective-permute-start(bf16[3584,128]{1,0:T(8,128)(2,1)S(1)} %bitcast.13), channel_id=1, source_target_pairs={{0,256},{256,0},{1,257},{257,1},{2,258},{258,2},{3,259},{259,3},{4... | collective-permute-start | bytes 2752520 | tf_op jit(solution)/shard_map/ppermute | solution.py:407
  69.9 0.0 copy-done.3
  69.9 1.9 %collective-permute-start.5 = (bf16[128,3584]{1,0:T(8,128)(2,1)S(1)}, bf16[128,3584]{1,0:T(8,128)(2,1)}, u32[]{:S(2)}, u32[]{:S(2)}) collective-permute-start(bf16[128,3584]{1,0:T(8,128)(2,1)S(1)} %bitcast.15), channel_id=1, source_target_pairs={{0,256},{256,0},{1,257},{257,1},{2,258},{258,2},{3,259},{259,3},{4... | collective-permute-start | bytes 2752520 | tf_op jit(solution)/shard_map/ppermute | solution.py:407
  71.8 0.0 copy-done.6
  71.9 0.0 copy-done.7
  71.9 0.4 shard_map.124
  72.3 3.8 %all-to-all-done.3.parts_ref = bf16[16,32,128]{2,1,0:T(8,128)(2,1)S(1)} async-done(((bf16[16,32,128]{2,1,0:T(8,128)(2,1)}), bf16[16,32,128]{2,1,0:T(8,128)(2,1)S(1)}, u32[]{:S(2)}, u32[]{:S(2)}) %all-to-all-start.3) | async-done | bytes 131104 | tf_op jit(solution)/shard_map/all_to_all | solution.py:85
  76.1 1.0 shard_map.125
  77.1 0.0 copy-start.8
  77.1 6.3 %all-to-all-start.4 = ((bf16[16,16,896]{2,1,0:T(8,128)(2,1)}), bf16[16,16,896]{2,1,0:T(8,128)(2,1)S(1)}, u32[]{:S(2)}, u32[]{:S(2)}) async-start(bf16[16,16,896]{2,1,0:T(8,128)(2,1)} %shard_map.125), calls=%async_computation.4 | async-start | bytes 917504 | tf_op jit(solution)/shard_map/all_to_all | solution.py:85
  83.4 0.0 copy-done.8
  83.4 0.0 collective-permute-done.3.refs_3_
  83.4 0.0 collective-permute-done.4.refs_4_
  83.4 0.0 collective-permute-done.5.refs_5_
  83.4 7.5 %all-to-all-done.4.arrived_ref = bf16[16,16,896]{2,1,0:T(8,128)(2,1)S(1)} async-done(((bf16[16,16,896]{2,1,0:T(8,128)(2,1)}), bf16[16,16,896]{2,1,0:T(8,128)(2,1)S(1)}, u32[]{:S(2)}, u32[]{:S(2)}) %all-to-all-start.4) | async-done | bytes 458784 | tf_op jit(solution)/shard_map/all_to_all | solution.py:85
  90.9 2.9 %shard_map.126 = bf16[16,16,896]{2,1,0:T(8,128)(2,1)S(1)} custom-call(bf16[16,16,896]{2,1,0:T(8,128)(2,1)S(1)} %all-to-all-done.4.arrived_ref, f32[4,1,896]{2,1,0:T(1,128)S(1)} %reshape.18.gain_ref, f32[64,128]{1,0:T(8,128)S(1)} %get-tuple-element.17.slots_ref, bf16[3584,128]{1,0:T(8,128)(2,1)S(1)} %bitcast.12, bf16[3584,128]{1,0:T(8,128)(2,1)S(1)} %bitcast.14, ...), custom_call_target="tpu_custom_call" | custom-call | tf_op jit(solution)/shard_map/pallas_call | solution.py:74
  93.8 12.1 %all_to_all.35.parts_ref = bf16[16,16,896]{2,1,0:T(8,128)(2,1)S(1)} all-to-all(bf16[16,16,896]{2,1,0:T(8,128)(2,1)S(1)} %shard_map.126), channel_id=1, replica_groups={{130,131,128,129,194,195,192,193,2,3,0,1,66,67,64,65},{134,135,132,133,..., dimensions={0} | all-to-all | bytes 917504 | tf_op jit(solution)/shard_map/all_to_all | solution.py:85
  105.9 0.2 shard_map.127
  106.0 17.2 %all_to_all.36 = bf16[16,32,128]{2,1,0:T(8,128)(2,1)S(1)} all-to-all(bf16[16,32,128]{2,1,0:T(8,128)(2,1)S(1)} %shard_map.127), channel_id=1, replica_groups={{32,36,40,44,48,52,56,60,0,4,8,12,16,20,24,28},{33,37,41,45,49,53,57,61..., dimensions={0} | all-to-all | bytes 262144 | tf_op jit(solution)/shard_map/all_to_all | solution.py:85
  123.2 0.9 shard_map.128
  (1 shorter events, 0.0 us)
Async XLA Ops:
  2.8 8.6 %all-to-all-start = ((bf16[8,8,512]{2,1,0:T(8,128)(2,1)}), bf16[8,8,512]{2,1,0:T(8,128)(2,1)S(1)}, u32[]{:S(2)}, u32[]{:S(2)}) async-start(bf16[8,8,512]{2,1,0:T(8,128)(2,1)} %bitcast.22), calls=%async_computation | async-start | bytes 131072 | tf_op jit(solution)/shard_map/all_to_all | solution.py:85
  8.7 1.2 copy-start
  11.4 58.5 %copy-start.3 = (bf16[1,128,3584]{2,1,0:T(8,128)(2,1)S(1)}, bf16[1,128,3584]{2,1,0:T(8,128)(2,1)}, u32[]{:S(2)}) copy-start(bf16[1,128,3584]{2,1,0:T(8,128)(2,1)} %param.23) | copy-start | bytes 2752516
  12.4 19.0 %copy-start.9 = (bf16[56,1280]{1,0:T(8,128)(2,1)S(1)}, bf16[56,1280]{1,0:T(8,128)(2,1)}, u32[]{:S(2)}) copy-start(bf16[56,1280]{1,0:T(8,128)(2,1)} %get-tuple-element.15) | copy-start | bytes 430084
  12.4 39.4 %copy-start.5 = (bf16[56,512]{1,0:T(8,128)(2,1)S(1)}, bf16[56,512]{1,0:T(8,128)(2,1)}, u32[]{:S(2)}) copy-start(bf16[56,512]{1,0:T(8,128)(2,1)} %own_ref.1) | copy-start | bytes 172036
  12.4 32.5 %all-to-all-start.1 = ((bf16[16,8,1024]{2,1,0:T(8,128)(2,1)}), bf16[16,8,1024]{2,1,0:T(8,128)(2,1)S(1)}, u32[]{:S(2)}, u32[]{:S(2)}) async-start(bf16[16,8,1024]{2,1,0:T(8,128)(2,1)} %shard_map.120), calls=%async_computation.1 | async-start | bytes 524288 | tf_op jit(solution)/shard_map/all_to_all | solution.py:85
  31.4 9.4 %collective-permute-start = (bf16[56,1280]{1,0:T(8,128)(2,1)S(1)}, bf16[56,1280]{1,0:T(8,128)(2,1)S(1)}, u32[]{:S(2)}, u32[]{:S(2)}) collective-permute-start(bf16[56,1280]{1,0:T(8,128)(2,1)S(1)} %copy-done.9), channel_id=1, source_target_pairs={{0,128},{64,192},{128,0},{192,64},{1,129},{65,193},{129,1},{193,65... | collective-permute-start | bytes 430088 | tf_op jit(solution)/shard_map/ppermute | solution.py:389
  33.8 9.1 %collective-permute-start.1 = (bf16[56,1280]{1,0:T(8,128)(2,1)S(1)}, bf16[56,1280]{1,0:T(8,128)(2,1)S(1)}, u32[]{:S(2)}, u32[]{:S(2)}) collective-permute-start(bf16[56,1280]{1,0:T(8,128)(2,1)S(1)} %copy-done.9), channel_id=1, source_target_pairs={{0,64},{64,128},{128,192},{192,0},{1,65},{65,129},{129,193},{193,1... | collective-permute-start | bytes 430088 | tf_op jit(solution)/shard_map/ppermute | solution.py:388
  37.8 7.1 %collective-permute-start.2 = (bf16[56,1280]{1,0:T(8,128)(2,1)S(1)}, bf16[56,1280]{1,0:T(8,128)(2,1)S(1)}, u32[]{:S(2)}, u32[]{:S(2)}) collective-permute-start(bf16[56,1280]{1,0:T(8,128)(2,1)S(1)} %copy-done.9), channel_id=1, source_target_pairs={{0,192},{64,0},{128,64},{192,128},{1,193},{65,1},{129,65},{193,129... | collective-permute-start | bytes 430088 | tf_op jit(solution)/shard_map/ppermute | solution.py:390
  44.9 0.9 copy-start.4
  45.8 19.7 %copy-start.1 = (bf16[1,3584,128]{2,1,0:T(8,128)(2,1)S(1)}, bf16[1,3584,128]{2,1,0:T(8,128)(2,1)}, u32[]{:S(2)}) copy-start(bf16[1,3584,128]{2,1,0:T(8,128)(2,1)} %param.21) | copy-start | bytes 2752516
  45.8 21.7 %copy-start.2 = (bf16[1,3584,128]{2,1,0:T(8,128)(2,1)S(1)}, bf16[1,3584,128]{2,1,0:T(8,128)(2,1)}, u32[]{:S(2)}) copy-start(bf16[1,3584,128]{2,1,0:T(8,128)(2,1)} %param.22) | copy-start | bytes 2752516
  46.9 7.9 %all-to-all-start.2 = ((bf16[8,32,128]{2,1,0:T(8,128)(2,1)}), bf16[8,32,128]{2,1,0:T(8,128)(2,1)S(1)}, u32[]{:S(2)}, u32[]{:S(2)}) async-start(bf16[8,32,128]{2,1,0:T(8,128)(2,1)} %shard_map.121), calls=%async_computation.2 | async-start | bytes 131072 | tf_op jit(solution)/shard_map/all_to_all | solution.py:85
  55.5 16.3 %copy-start.6 = (s32[512,8]{0,1:T(8,128)S(1)}, s32[512,8]{0,1:T(8,128)}, u32[]{:S(2)}) copy-start(s32[512,8]{0,1:T(8,128)} %param.19) | copy-start | bytes 49156
  55.5 16.3 %copy-start.7 = (f32[512,8]{0,1:T(8,128)S(1)}, f32[512,8]{0,1:T(8,128)}, u32[]{:S(2)}) copy-start(f32[512,8]{0,1:T(8,128)} %param.20) | copy-start | bytes 49156
  55.5 20.6 %all-to-all-start.3 = ((bf16[16,32,128]{2,1,0:T(8,128)(2,1)}), bf16[16,32,128]{2,1,0:T(8,128)(2,1)S(1)}, u32[]{:S(2)}, u32[]{:S(2)}) async-start(bf16[16,32,128]{2,1,0:T(8,128)(2,1)} %shard_map.123), calls=%async_computation.3 | async-start | bytes 262144 | tf_op jit(solution)/shard_map/all_to_all | solution.py:85
  65.5 17.9 %collective-permute-start.3 = (bf16[3584,128]{1,0:T(8,128)(2,1)S(1)}, bf16[3584,128]{1,0:T(8,128)(2,1)}, u32[]{:S(2)}, u32[]{:S(2)}) collective-permute-start(bf16[3584,128]{1,0:T(8,128)(2,1)S(1)} %bitcast.11), channel_id=1, source_target_pairs={{0,256},{256,0},{1,257},{257,1},{2,258},{258,2},{3,259},{259,3},{4... | collective-permute-start | bytes 2752520 | tf_op jit(solution)/shard_map/ppermute | solution.py:407
  67.5 15.9 %collective-permute-start.4 = (bf16[3584,128]{1,0:T(8,128)(2,1)S(1)}, bf16[3584,128]{1,0:T(8,128)(2,1)}, u32[]{:S(2)}, u32[]{:S(2)}) collective-permute-start(bf16[3584,128]{1,0:T(8,128)(2,1)S(1)} %bitcast.13), channel_id=1, source_target_pairs={{0,256},{256,0},{1,257},{257,1},{2,258},{258,2},{3,259},{259,3},{4... | collective-permute-start | bytes 2752520 | tf_op jit(solution)/shard_map/ppermute | solution.py:407
  69.9 13.5 %collective-permute-start.5 = (bf16[128,3584]{1,0:T(8,128)(2,1)S(1)}, bf16[128,3584]{1,0:T(8,128)(2,1)}, u32[]{:S(2)}, u32[]{:S(2)}) collective-permute-start(bf16[128,3584]{1,0:T(8,128)(2,1)S(1)} %bitcast.15), channel_id=1, source_target_pairs={{0,256},{256,0},{1,257},{257,1},{2,258},{258,2},{3,259},{259,3},{4... | collective-permute-start | bytes 2752520 | tf_op jit(solution)/shard_map/ppermute | solution.py:407
  77.1 6.3 %copy-start.8 = (f32[3584]{0:T(1024)S(1)}, f32[3584]{0:T(1024)}, u32[]{:S(2)}) copy-start(f32[3584]{0:T(1024)} %param.18) | copy-start | bytes 43012
  77.1 13.8 %all-to-all-start.4 = ((bf16[16,16,896]{2,1,0:T(8,128)(2,1)}), bf16[16,16,896]{2,1,0:T(8,128)(2,1)S(1)}, u32[]{:S(2)}, u32[]{:S(2)}) async-start(bf16[16,16,896]{2,1,0:T(8,128)(2,1)} %shard_map.125), calls=%async_computation.4 | async-start | bytes 917504 | tf_op jit(solution)/shard_map/all_to_all | solution.py:85

commit v9 on v8

--- a/solution.py
+++ b/solution.py
@@ -119,14 +119,14 @@
     heads = value_ref.shape[0]
     att = att_ref[...]
     rows = att.shape[0]
-    row_head = lax.broadcasted_iota(jnp.int32, (rows, 256), 0) % heads
-    lane_head = lax.broadcasted_iota(jnp.int32, (rows, 256), 1) // 128
-    for head in range(0, heads, 2):
-        pair = jnp.concatenate([value_ref[head], value_ref[head + 1]], axis=1)
+    row_head = lax.broadcasted_iota(jnp.int32, (rows, 512), 0) % heads
+    lane_head = lax.broadcasted_iota(jnp.int32, (rows, 512), 1) // 128
+    for head in range(0, heads, 4):
+        pair = jnp.concatenate([value_ref[head + i] for i in range(4)], axis=1)
         kept = jnp.where(row_head == head + lane_head, nn_dot(att, pair), 0.0)
-        value = jnp.sum(kept.reshape(rows // heads, heads, 256), axis=1)
+        value = jnp.sum(kept.reshape(rows // heads, heads, 512), axis=1)
         value = jnp.concatenate([value[i : i + 1] for i in HEAD_AT], axis=0).astype(BF16)
-        out_ref[:, :, head * 128 : (head + 2) * 128] = jnp.broadcast_to(
+        out_ref[:, :, head * 128 : (head + 4) * 128] = jnp.broadcast_to(
             value[None], (out_ref.shape[0],) + value.shape
         )
 

time: 125 us -> 125 us (level)
  no operation moved by 1% of the time
where the time goes in v9:
time: 125 us; the launch traced here: 124 us
  starting transfers between devices  60.8 us (49%)
  blocking collectives  29.3 us (23%)
  waiting for transfers between devices  20.4 us (16%)
  Pallas kernels  10.6 us (8%)
  local copies, waits for them, and re-layouts  2.17 us (2%)
    all_to_all x5, starting transfers between devices, exchange(): lax.all_to_all(chunks, axes, 0, 0, tiled=True, axis_index_groups=[order])  46.1 us
    all_to_all x2, blocking collectives, exchange(): lax.all_to_all(chunks, axes, 0, 0, tiled=True, axis_index_groups=[order])  29.3 us
    all_to_all x5, waiting for transfers between devices, exchange(): lax.all_to_all(chunks, axes, 0, 0, tiled=True, axis_index_groups=[order])  15.4 us
    pallas_call x10, Pallas kernels, local_call(): pl.pallas_call(body, out_shape=out_shape, in_specs=[pl.BlockSpec(memory_s...  8.45 us
    ppermute x3, starting transfers between devices, shards(): peer_expert = [lax.ppermute(weight, 'role', swap) for weight in own_expert]  6.25 us
    ppermute x1, starting transfers between devices, shards(): near = lax.ppermute(payload, 'x', right)  4 us
  transfers between devices with their start and end apart: 11, of which 7 were waited for; matrix products, arithmetic and copies ran while one was open for 0% of the time, Pallas kernels for 1%

profile of v9, /device:TPU:4, one launch (start us, length us, event | category | flops | bytes accessed | tf_op | source)
XLA Modules:
  0.0 124.1 jit_solution(1698270023059814527)
XLA Ops:
  0.7 2.2 %shard_map.118 = (bf16[64,512]{1,0:T(8,128)(2,1)}, bf16[56,1280]{1,0:T(8,128)(2,1)}) custom-call(s32[1]{0:T(128)S(6)} %copy.13.length_ref, bf16[1,64,576]{2,1,0:T(8,128)(2,1)} %query_ref.1, bf16[1,576,384]{2,1,0:T(8,128)(2,1)} %bitcast.21, bf16[56,1024]{1,0:T(8,128)(2,1)} %refs_0_.2, bf16[56,512]{1,0:T(8,128)(2,1)} %own_ref.1), custom_call_target="tpu_custom_call" | custom-call | tf_op jit(solution)/shard_map/pallas_call | solution.py:368
  2.8 5.9 %all-to-all-start = ((bf16[8,8,512]{2,1,0:T(8,128)(2,1)}), bf16[8,8,512]{2,1,0:T(8,128)(2,1)S(1)}, u32[]{:S(2)}, u32[]{:S(2)}) async-start(bf16[8,8,512]{2,1,0:T(8,128)(2,1)} %bitcast.22), calls=%async_computation | async-start | bytes 131072 | tf_op jit(solution)/shard_map/all_to_all | solution.py:85
  8.7 0.0 copy-start
  8.7 1.2 copy-done
  10.0 0.1 shard_map.119.value_ref
  10.1 1.3 %all-to-all-done = bf16[8,8,512]{2,1,0:T(8,128)(2,1)S(1)} async-done(((bf16[8,8,512]{2,1,0:T(8,128)(2,1)}), bf16[8,8,512]{2,1,0:T(8,128)(2,1)S(1)}, u32[]{:S(2)}, u32[]{:S(2)}) %all-to-all-start) | async-done | bytes 65568 | tf_op jit(solution)/shard_map/all_to_all | solution.py:85
  11.4 0.0 copy-start.3
  11.4 1.0 shard_map.120
  12.4 0.0 copy-start.9
  12.4 0.0 copy-start.5
  12.4 19.0 %all-to-all-start.1 = ((bf16[16,8,1024]{2,1,0:T(8,128)(2,1)}), bf16[16,8,1024]{2,1,0:T(8,128)(2,1)S(1)}, u32[]{:S(2)}, u32[]{:S(2)}) async-start(bf16[16,8,1024]{2,1,0:T(8,128)(2,1)} %shard_map.120), calls=%async_computation.1 | async-start | bytes 524288 | tf_op jit(solution)/shard_map/all_to_all | solution.py:85
  31.4 0.0 copy-done.9
  31.4 2.4 %collective-permute-start = (bf16[56,1280]{1,0:T(8,128)(2,1)S(1)}, bf16[56,1280]{1,0:T(8,128)(2,1)S(1)}, u32[]{:S(2)}, u32[]{:S(2)}) collective-permute-start(bf16[56,1280]{1,0:T(8,128)(2,1)S(1)} %copy-done.9), channel_id=1, source_target_pairs={{0,128},{64,192},{128,0},{192,64},{1,129},{65,193},{129,1},{193,65... | collective-permute-start | bytes 430088 | tf_op jit(solution)/shard_map/ppermute | solution.py:389
  33.8 4.0 %collective-permute-start.1 = (bf16[56,1280]{1,0:T(8,128)(2,1)S(1)}, bf16[56,1280]{1,0:T(8,128)(2,1)S(1)}, u32[]{:S(2)}, u32[]{:S(2)}) collective-permute-start(bf16[56,1280]{1,0:T(8,128)(2,1)S(1)} %copy-done.9), channel_id=1, source_target_pairs={{0,64},{64,128},{128,192},{192,0},{1,65},{65,129},{129,193},{193,1... | collective-permute-start | bytes 430088 | tf_op jit(solution)/shard_map/ppermute | solution.py:388
  37.8 2.0 %collective-permute-start.2 = (bf16[56,1280]{1,0:T(8,128)(2,1)S(1)}, bf16[56,1280]{1,0:T(8,128)(2,1)S(1)}, u32[]{:S(2)}, u32[]{:S(2)}) collective-permute-start(bf16[56,1280]{1,0:T(8,128)(2,1)S(1)} %copy-done.9), channel_id=1, source_target_pairs={{0,192},{64,0},{128,64},{192,128},{1,193},{65,1},{129,65},{193,129... | collective-permute-start | bytes 430088 | tf_op jit(solution)/shard_map/ppermute | solution.py:390
  39.8 1.0 collective-permute-done.refs_1_.refs_0_
  40.8 2.1 %collective-permute-done.1.refs_2_.refs_1_ = bf16[56,1280]{1,0:T(8,128)(2,1)S(1)} collective-permute-done((bf16[56,1280]{1,0:T(8,128)(2,1)S(1)}, bf16[56,1280]{1,0:T(8,128)(2,1)S(1)}, u32[]{:S(2)}, u32[]{:S(2)}) %collective-permute-start.1) | collective-permute-done | bytes 143392 | tf_op jit(solution)/shard_map/ppermute | solution.py:388
  42.9 2.0 %collective-permute-done.2.refs_3_.refs_2_ = bf16[56,1280]{1,0:T(8,128)(2,1)S(1)} collective-permute-done((bf16[56,1280]{1,0:T(8,128)(2,1)S(1)}, bf16[56,1280]{1,0:T(8,128)(2,1)S(1)}, u32[]{:S(2)}, u32[]{:S(2)}) %collective-permute-start.2) | collective-permute-done | bytes 143392 | tf_op jit(solution)/shard_map/ppermute | solution.py:390
  44.9 0.0 all-to-all-done.1
  44.9 0.0 copy-start.4
  44.9 0.9 copy-done.4
  45.8 0.0 copy-start.1
  45.8 0.0 copy-start.2
  45.8 1.1 shard_map.121
  46.9 4.9 %all-to-all-start.2 = ((bf16[8,32,128]{2,1,0:T(8,128)(2,1)}), bf16[8,32,128]{2,1,0:T(8,128)(2,1)S(1)}, u32[]{:S(2)}, u32[]{:S(2)}) async-start(bf16[8,32,128]{2,1,0:T(8,128)(2,1)} %shard_map.121), calls=%async_computation.2 | async-start | bytes 131072 | tf_op jit(solution)/shard_map/all_to_all | solution.py:85
  51.8 0.0 copy-done.5
  51.8 0.2 shard_map.122.residual_ref
  52.1 2.8 %all-to-all-done.2.parts_ref = bf16[8,32,128]{2,1,0:T(8,128)(2,1)S(1)} async-done(((bf16[8,32,128]{2,1,0:T(8,128)(2,1)}), bf16[8,32,128]{2,1,0:T(8,128)(2,1)S(1)}, u32[]{:S(2)}, u32[]{:S(2)}) %all-to-all-start.2) | async-done | bytes 65568 | tf_op jit(solution)/shard_map/all_to_all | solution.py:85
  54.8 0.7 shard_map.123
  55.5 0.0 copy-start.6
  55.5 0.0 copy-start.7
  55.5 10.0 %all-to-all-start.3 = ((bf16[16,32,128]{2,1,0:T(8,128)(2,1)}), bf16[16,32,128]{2,1,0:T(8,128)(2,1)S(1)}, u32[]{:S(2)}, u32[]{:S(2)}) async-start(bf16[16,32,128]{2,1,0:T(8,128)(2,1)} %shard_map.123), calls=%async_computation.3 | async-start | bytes 262144 | tf_op jit(solution)/shard_map/all_to_all | solution.py:85
  65.5 0.0 copy-done.1
  65.5 1.9 %collective-permute-start.3 = (bf16[3584,128]{1,0:T(8,128)(2,1)S(1)}, bf16[3584,128]{1,0:T(8,128)(2,1)}, u32[]{:S(2)}, u32[]{:S(2)}) collective-permute-start(bf16[3584,128]{1,0:T(8,128)(2,1)S(1)} %bitcast.11), channel_id=1, source_target_pairs={{0,256},{256,0},{1,257},{257,1},{2,258},{258,2},{3,259},{259,3},{4... | collective-permute-start | bytes 2752520 | tf_op jit(solution)/shard_map/ppermute | solution.py:407
  67.5 0.0 copy-done.2
  67.5 2.4 %collective-permute-start.4 = (bf16[3584,128]{1,0:T(8,128)(2,1)S(1)}, bf16[3584,128]{1,0:T(8,128)(2,1)}, u32[]{:S(2)}, u32[]{:S(2)}) collective-permute-start(bf16[3584,128]{1,0:T(8,128)(2,1)S(1)} %bitcast.13), channel_id=1, source_target_pairs={{0,256},{256,0},{1,257},{257,1},{2,258},{258,2},{3,259},{259,3},{4... | collective-permute-start | bytes 2752520 | tf_op jit(solution)/shard_map/ppermute | solution.py:407
  69.9 0.0 copy-done.3
  69.9 1.9 %collective-permute-start.5 = (bf16[128,3584]{1,0:T(8,128)(2,1)S(1)}, bf16[128,3584]{1,0:T(8,128)(2,1)}, u32[]{:S(2)}, u32[]{:S(2)}) collective-permute-start(bf16[128,3584]{1,0:T(8,128)(2,1)S(1)} %bitcast.15), channel_id=1, source_target_pairs={{0,256},{256,0},{1,257},{257,1},{2,258},{258,2},{3,259},{259,3},{4... | collective-permute-start | bytes 2752520 | tf_op jit(solution)/shard_map/ppermute | solution.py:407
  71.8 0.0 copy-done.6
  71.9 0.0 copy-done.7
  71.9 0.4 shard_map.124
  72.3 3.8 %all-to-all-done.3.parts_ref = bf16[16,32,128]{2,1,0:T(8,128)(2,1)S(1)} async-done(((bf16[16,32,128]{2,1,0:T(8,128)(2,1)}), bf16[16,32,128]{2,1,0:T(8,128)(2,1)S(1)}, u32[]{:S(2)}, u32[]{:S(2)}) %all-to-all-start.3) | async-done | bytes 131104 | tf_op jit(solution)/shard_map/all_to_all | solution.py:85
  76.1 1.0 shard_map.125
  77.1 0.0 copy-start.8
  77.1 6.3 %all-to-all-start.4 = ((bf16[16,16,896]{2,1,0:T(8,128)(2,1)}), bf16[16,16,896]{2,1,0:T(8,128)(2,1)S(1)}, u32[]{:S(2)}, u32[]{:S(2)}) async-start(bf16[16,16,896]{2,1,0:T(8,128)(2,1)} %shard_map.125), calls=%async_computation.4 | async-start | bytes 917504 | tf_op jit(solution)/shard_map/all_to_all | solution.py:85
  83.4 0.0 copy-done.8
  83.4 0.0 collective-permute-done.3.refs_3_
  83.4 0.0 collective-permute-done.4.refs_4_
  83.4 0.0 collective-permute-done.5.refs_5_
  83.4 7.5 %all-to-all-done.4.arrived_ref = bf16[16,16,896]{2,1,0:T(8,128)(2,1)S(1)} async-done(((bf16[16,16,896]{2,1,0:T(8,128)(2,1)}), bf16[16,16,896]{2,1,0:T(8,128)(2,1)S(1)}, u32[]{:S(2)}, u32[]{:S(2)}) %all-to-all-start.4) | async-done | bytes 458784 | tf_op jit(solution)/shard_map/all_to_all | solution.py:85
  90.9 2.9 %shard_map.126 = bf16[16,16,896]{2,1,0:T(8,128)(2,1)S(1)} custom-call(bf16[16,16,896]{2,1,0:T(8,128)(2,1)S(1)} %all-to-all-done.4.arrived_ref, f32[4,1,896]{2,1,0:T(1,128)S(1)} %reshape.18.gain_ref, f32[64,128]{1,0:T(8,128)S(1)} %get-tuple-element.17.slots_ref, bf16[3584,128]{1,0:T(8,128)(2,1)S(1)} %bitcast.12, bf16[3584,128]{1,0:T(8,128)(2,1)S(1)} %bitcast.14, ...), custom_call_target="tpu_custom_call" | custom-call | tf_op jit(solution)/shard_map/pallas_call | solution.py:74
  93.8 12.1 %all_to_all.35.parts_ref = bf16[16,16,896]{2,1,0:T(8,128)(2,1)S(1)} all-to-all(bf16[16,16,896]{2,1,0:T(8,128)(2,1)S(1)} %shard_map.126), channel_id=1, replica_groups={{130,131,128,129,194,195,192,193,2,3,0,1,66,67,64,65},{134,135,132,133,..., dimensions={0} | all-to-all | bytes 917504 | tf_op jit(solution)/shard_map/all_to_all | solution.py:85
  105.9 0.2 shard_map.127
  106.0 17.2 %all_to_all.36 = bf16[16,32,128]{2,1,0:T(8,128)(2,1)S(1)} all-to-all(bf16[16,32,128]{2,1,0:T(8,128)(2,1)S(1)} %shard_map.127), channel_id=1, replica_groups={{32,36,40,44,48,52,56,60,0,4,8,12,16,20,24,28},{33,37,41,45,49,53,57,61..., dimensions={0} | all-to-all | bytes 262144 | tf_op jit(solution)/shard_map/all_to_all | solution.py:85
  123.2 0.9 shard_map.128
  (1 shorter events, 0.0 us)
Async XLA Ops:
  2.8 8.6 %all-to-all-start = ((bf16[8,8,512]{2,1,0:T(8,128)(2,1)}), bf16[8,8,512]{2,1,0:T(8,128)(2,1)S(1)}, u32[]{:S(2)}, u32[]{:S(2)}) async-start(bf16[8,8,512]{2,1,0:T(8,128)(2,1)} %bitcast.22), calls=%async_computation | async-start | bytes 131072 | tf_op jit(solution)/shard_map/all_to_all | solution.py:85
  8.7 1.2 copy-start
  11.4 58.5 %copy-start.3 = (bf16[1,128,3584]{2,1,0:T(8,128)(2,1)S(1)}, bf16[1,128,3584]{2,1,0:T(8,128)(2,1)}, u32[]{:S(2)}) copy-start(bf16[1,128,3584]{2,1,0:T(8,128)(2,1)} %param.23) | copy-start | bytes 2752516
  12.4 19.0 %copy-start.9 = (bf16[56,1280]{1,0:T(8,128)(2,1)S(1)}, bf16[56,1280]{1,0:T(8,128)(2,1)}, u32[]{:S(2)}) copy-start(bf16[56,1280]{1,0:T(8,128)(2,1)} %get-tuple-element.15) | copy-start | bytes 430084
  12.4 39.4 %copy-start.5 = (bf16[56,512]{1,0:T(8,128)(2,1)S(1)}, bf16[56,512]{1,0:T(8,128)(2,1)}, u32[]{:S(2)}) copy-start(bf16[56,512]{1,0:T(8,128)(2,1)} %own_ref.1) | copy-start | bytes 172036
  12.4 32.5 %all-to-all-start.1 = ((bf16[16,8,1024]{2,1,0:T(8,128)(2,1)}), bf16[16,8,1024]{2,1,0:T(8,128)(2,1)S(1)}, u32[]{:S(2)}, u32[]{:S(2)}) async-start(bf16[16,8,1024]{2,1,0:T(8,128)(2,1)} %shard_map.120), calls=%async_computation.1 | async-start | bytes 524288 | tf_op jit(solution)/shard_map/all_to_all | solution.py:85
  31.4 9.4 %collective-permute-start = (bf16[56,1280]{1,0:T(8,128)(2,1)S(1)}, bf16[56,1280]{1,0:T(8,128)(2,1)S(1)}, u32[]{:S(2)}, u32[]{:S(2)}) collective-permute-start(bf16[56,1280]{1,0:T(8,128)(2,1)S(1)} %copy-done.9), channel_id=1, source_target_pairs={{0,128},{64,192},{128,0},{192,64},{1,129},{65,193},{129,1},{193,65... | collective-permute-start | bytes 430088 | tf_op jit(solution)/shard_map/ppermute | solution.py:389
  33.8 9.1 %collective-permute-start.1 = (bf16[56,1280]{1,0:T(8,128)(2,1)S(1)}, bf16[56,1280]{1,0:T(8,128)(2,1)S(1)}, u32[]{:S(2)}, u32[]{:S(2)}) collective-permute-start(bf16[56,1280]{1,0:T(8,128)(2,1)S(1)} %copy-done.9), channel_id=1, source_target_pairs={{0,64},{64,128},{128,192},{192,0},{1,65},{65,129},{129,193},{193,1... | collective-permute-start | bytes 430088 | tf_op jit(solution)/shard_map/ppermute | solution.py:388
  37.8 7.1 %collective-permute-start.2 = (bf16[56,1280]{1,0:T(8,128)(2,1)S(1)}, bf16[56,1280]{1,0:T(8,128)(2,1)S(1)}, u32[]{:S(2)}, u32[]{:S(2)}) collective-permute-start(bf16[56,1280]{1,0:T(8,128)(2,1)S(1)} %copy-done.9), channel_id=1, source_target_pairs={{0,192},{64,0},{128,64},{192,128},{1,193},{65,1},{129,65},{193,129... | collective-permute-start | bytes 430088 | tf_op jit(solution)/shard_map/ppermute | solution.py:390
  44.9 0.9 copy-start.4
  45.8 19.7 %copy-start.1 = (bf16[1,3584,128]{2,1,0:T(8,128)(2,1)S(1)}, bf16[1,3584,128]{2,1,0:T(8,128)(2,1)}, u32[]{:S(2)}) copy-start(bf16[1,3584,128]{2,1,0:T(8,128)(2,1)} %param.21) | copy-start | bytes 2752516
  45.8 21.7 %copy-start.2 = (bf16[1,3584,128]{2,1,0:T(8,128)(2,1)S(1)}, bf16[1,3584,128]{2,1,0:T(8,128)(2,1)}, u32[]{:S(2)}) copy-start(bf16[1,3584,128]{2,1,0:T(8,128)(2,1)} %param.22) | copy-start | bytes 2752516
  46.9 7.9 %all-to-all-start.2 = ((bf16[8,32,128]{2,1,0:T(8,128)(2,1)}), bf16[8,32,128]{2,1,0:T(8,128)(2,1)S(1)}, u32[]{:S(2)}, u32[]{:S(2)}) async-start(bf16[8,32,128]{2,1,0:T(8,128)(2,1)} %shard_map.121), calls=%async_computation.2 | async-start | bytes 131072 | tf_op jit(solution)/shard_map/all_to_all | solution.py:85
  55.5 16.3 %copy-start.6 = (s32[512,8]{0,1:T(8,128)S(1)}, s32[512,8]{0,1:T(8,128)}, u32[]{:S(2)}) copy-start(s32[512,8]{0,1:T(8,128)} %param.19) | copy-start | bytes 49156
  55.5 16.3 %copy-start.7 = (f32[512,8]{0,1:T(8,128)S(1)}, f32[512,8]{0,1:T(8,128)}, u32[]{:S(2)}) copy-start(f32[512,8]{0,1:T(8,128)} %param.20) | copy-start | bytes 49156
  55.5 20.6 %all-to-all-start.3 = ((bf16[16,32,128]{2,1,0:T(8,128)(2,1)}), bf16[16,32,128]{2,1,0:T(8,128)(2,1)S(1)}, u32[]{:S(2)}, u32[]{:S(2)}) async-start(bf16[16,32,128]{2,1,0:T(8,128)(2,1)} %shard_map.123), calls=%async_computation.3 | async-start | bytes 262144 | tf_op jit(solution)/shard_map/all_to_all | solution.py:85
  65.5 17.9 %collective-permute-start.3 = (bf16[3584,128]{1,0:T(8,128)(2,1)S(1)}, bf16[3584,128]{1,0:T(8,128)(2,1)}, u32[]{:S(2)}, u32[]{:S(2)}) collective-permute-start(bf16[3584,128]{1,0:T(8,128)(2,1)S(1)} %bitcast.11), channel_id=1, source_target_pairs={{0,256},{256,0},{1,257},{257,1},{2,258},{258,2},{3,259},{259,3},{4... | collective-permute-start | bytes 2752520 | tf_op jit(solution)/shard_map/ppermute | solution.py:407
  67.5 15.9 %collective-permute-start.4 = (bf16[3584,128]{1,0:T(8,128)(2,1)S(1)}, bf16[3584,128]{1,0:T(8,128)(2,1)}, u32[]{:S(2)}, u32[]{:S(2)}) collective-permute-start(bf16[3584,128]{1,0:T(8,128)(2,1)S(1)} %bitcast.13), channel_id=1, source_target_pairs={{0,256},{256,0},{1,257},{257,1},{2,258},{258,2},{3,259},{259,3},{4... | collective-permute-start | bytes 2752520 | tf_op jit(solution)/shard_map/ppermute | solution.py:407
  69.9 13.5 %collective-permute-start.5 = (bf16[128,3584]{1,0:T(8,128)(2,1)S(1)}, bf16[128,3584]{1,0:T(8,128)(2,1)}, u32[]{:S(2)}, u32[]{:S(2)}) collective-permute-start(bf16[128,3584]{1,0:T(8,128)(2,1)S(1)} %bitcast.15), channel_id=1, source_target_pairs={{0,256},{256,0},{1,257},{257,1},{2,258},{258,2},{3,259},{259,3},{4... | collective-permute-start | bytes 2752520 | tf_op jit(solution)/shard_map/ppermute | solution.py:407
  77.1 6.3 %copy-start.8 = (f32[3584]{0:T(1024)S(1)}, f32[3584]{0:T(1024)}, u32[]{:S(2)}) copy-start(f32[3584]{0:T(1024)} %param.18) | copy-start | bytes 43012
  77.1 13.8 %all-to-all-start.4 = ((bf16[16,16,896]{2,1,0:T(8,128)(2,1)}), bf16[16,16,896]{2,1,0:T(8,128)(2,1)S(1)}, u32[]{:S(2)}, u32[]{:S(2)}) async-start(bf16[16,16,896]{2,1,0:T(8,128)(2,1)} %shard_map.125), calls=%async_computation.4 | async-start | bytes 917504 | tf_op jit(solution)/shard_map/all_to_all | solution.py:85
